TPU v7x, 32 devices: a whole 2x2x4 slice. The times are simulated.
32 devices in a mesh: grp: 1, ep: 16 (over z, y, x), tp: 2 (over core).
Axes of the slice: x: 2, y: 2, z: 4, core: 2. Of those that a mesh axis runs over, the one named last changes fastest.
Arguments:
- tokens: bfloat16 [1024, 3584], P(('grp', 'ep')), may hold values from -6 to 6
- scores: float32 [1024, 8], P(('grp', 'ep')), may hold values from -6 to 6
- expert_ids: int32 [1024, 8], P(('grp', 'ep')), may hold values from 0 to 15, all different within a row; in each aligned block of 64 rows (0 to 63, 64 to 127, ...) at most 64 rows name the same one
- copied: int32 [16], P('grp'), may hold values 0 or 1
- w_gate: bfloat16 [16, 3584, 1024], P('ep', None, 'tp'), may hold values from -0.09375 to 0.09375
- w_up: bfloat16 [16, 3584, 1024], P('ep', None, 'tp'), may hold values from -0.09375 to 0.09375
- w_down: bfloat16 [16, 1024, 3584], P('ep', 'tp'), may hold values from -0.1875 to 0.1875
Outputs:
- combined: bfloat16 [1024, 3584], P(('grp', 'ep'), 'tp')
Inputs may be any that keep to these rules, and one draw needn't show every extreme that they name: `expert_ids`: each row names 8 different experts. Within each aligned block of 64 rows no expert is named more than 2 * 32 times, and in some block an expert is named exactly 2 * 32 times.
All inputs are finite; a program needn't handle non-finite values.
Results may differ from a plain program's by a relative error of at most 0.0065.
Values may be sent and summed in bfloat16 or wider, within the bound.
No kernel may reach another device: no remote copies, remote signals or barrier semaphores. Data moves between devices by JAX's collectives and lax.ppermute only.
A program may use at most 128 MiB of HBM per device.

v0:
```python
import jax
import jax.numpy as jnp
from jax import lax
from jax.sharding import PartitionSpec as P


def feed_forward(row_block, gate_mat, up_mat, down_mat):
    flat_rows = row_block.reshape(-1, row_block.shape[-1])
    gate_act = jnp.dot(flat_rows, gate_mat, preferred_element_type=jnp.float32)
    up_act = jnp.dot(flat_rows, up_mat, preferred_element_type=jnp.float32)
    hidden = (jax.nn.silu(gate_act) * up_act).astype(jnp.bfloat16)
    result = jnp.dot(hidden, down_mat, preferred_element_type=jnp.float32)
    return result.reshape(row_block.shape[:-1] + (down_mat.shape[1],))


def body(tokens, scores, expert_ids, copied, w_gate, w_up, w_down):
    ep_size = lax.axis_size("ep")
    tok_rows, width = tokens.shape
    top_count = expert_ids.shape[1]
    capacity = min(tok_rows * top_count // ep_size, tok_rows // 2)
    pair_count = tok_rows * top_count
    total_slots = ep_size * 2 * capacity
    flat_ids = expert_ids.reshape(pair_count)
    onehot = (flat_ids[:, None] == jnp.arange(ep_size, dtype=jnp.int32)[None, :]).astype(jnp.int32)
    earlier = jnp.cumsum(onehot, axis=0) - onehot
    row_rank = jnp.sum(earlier * onehot, axis=1)
    flagged = jnp.sum(onehot * copied[None, :], axis=1)
    spilled = (row_rank >= capacity).astype(jnp.int32)
    is_kept = (spilled == 0) | (flagged == 1)
    spare_weights = (w_gate, w_up, w_down)
    position = jnp.where(
        is_kept, (flat_ids * 2 + spilled) * capacity + row_rank - spilled * capacity, total_slots
    )
    token_of = jnp.arange(pair_count, dtype=jnp.int32) // top_count
    row_table = (
        jnp.full((total_slots,), tok_rows, jnp.int32).at[position].set(token_of, mode="drop")
    )
    padded = jnp.concatenate([tokens, jnp.zeros((1, width), tokens.dtype)], axis=0)
    outgoing = padded[row_table].reshape(ep_size, 2, capacity, width)
    block = lax.all_to_all(outgoing, "ep", split_axis=0, concat_axis=0, tiled=True)
    home_out = feed_forward(block[:, 0], w_gate[0], w_up[0], w_down[0])
    spare_out = feed_forward(
        block[:, 1], spare_weights[0][0], spare_weights[1][0], spare_weights[2][0]
    )
    partial_out = jnp.stack([home_out, spare_out], axis=1)
    summed = lax.psum_scatter(
        partial_out.astype(jnp.bfloat16), "tp", scatter_dimension=3, tiled=True
    )
    returned = lax.all_to_all(summed, "ep", split_axis=0, concat_axis=0, tiled=True)
    share = returned.shape[-1]
    flat_return = jnp.concatenate(
        [returned.reshape(total_slots, share), jnp.zeros((1, share), jnp.bfloat16)], axis=0
    )
    picked = flat_return[jnp.minimum(position, total_slots)]
    affinity = jax.nn.sigmoid(scores)
    gate_weight = 2.5 * affinity / jnp.sum(affinity, axis=1, keepdims=True)
    weight = jnp.where(is_kept, gate_weight.reshape(pair_count), jnp.float32(0.0))
    terms = picked.astype(jnp.float32) * weight[:, None]
    combined = jnp.sum(terms.reshape(tok_rows, top_count, share), axis=1)
    return combined.astype(jnp.bfloat16)


def solution(mesh):
    in_specs = (
        P(("grp", "ep"), None),
        P(("grp", "ep"), None),
        P(("grp", "ep"), None),
        P("grp"),
        P("ep", None, "tp"),
        P("ep", None, "tp"),
        P("ep", "tp", None),
    )
    out_specs = P(("grp", "ep"), "tp")
    return jax.shard_map(body, mesh=mesh, in_specs=in_specs, out_specs=out_specs, check_vma=False)
```

profile of v0, /device:TPU:14, one launch (start us, length us, event | category | flops | bytes accessed | tf_op | source)
XLA Modules:
  0.0 338.4 jit_solution(3163593669919094230)
XLA Ops:
  6.5 0.0 reduce-scatter.2.cloned.1.call-start
  6.5 0.8 copy.15
  7.3 0.1 eq.73
  7.4 0.1 eq.69
  7.5 0.7 broadcast_multiply_fusion
  8.2 1.2 reduce-window.6
  9.3 0.2 slice_reduce_fusion
  9.6 0.1 copy.18
  9.7 0.1 mul.81
  9.8 0.8 fusion.27
  10.6 2.4 scatter_custom_fusion
  13.1 1.1 concatenate.6
  14.1 7.3 %gather_fusion = bf16[1024,3584]{1,0:T(8,128)(2,1)} fusion(bf16[65,3584]{1,0:T(8,128)(2,1)S(1)} %concatenate.6, s32[1024]{0:T(1024)S(1)} %fusion.30), kind=kCustom, calls=%fused_computation | custom fusion | bytes 14684160 | tf_op jit(solution)/shard_map/gather | solution.py:39
  21.4 166.2 %all_to_all.10 = bf16[16,2,32,3584]{3,2,1,0:T(8,128)(2,1)S(1)} all-to-all(bf16[16,2,32,3584]{3,2,1,0:T(8,128)(2,1)} %bitcast.65), channel_id=1, replica_groups=mesh['grp'=1,'ep'=16,'tp'=2] {'ep'}, dimensions={0} | all-to-all | bytes 14680064 | tf_op jit(solution)/shard_map/all_to_all | solution.py:40
  187.6 0.8 fusion.38
  188.4 0.0 copy-start.1
  188.4 4.2 %fusion.11 = f32[512,512]{1,0:T(8,128)S(1)} fusion(bf16[512,3584]{1,0:T(8,128)(2,1)S(1)} %bitcast.68, bf16[1,3584,512]{2,1,0:T(8,128)(2,1)} %param.11), kind=kOutput, calls=%fused_computation.18 | convolution fusion | flops 1879048192 | bytes 8388608 | tf_op jit(solution)/shard_map/dot_general | solution.py:9
  192.7 0.0 copy-done.1
  192.7 0.0 copy-start.2
  192.7 2.1 fusion.9
  194.7 0.0 copy-done.2
  194.7 2.1 fusion.22
  196.9 0.0 copy-start.3
  196.9 2.1 fusion.19
  199.0 0.0 copy-done.3
  199.1 2.1 fusion
  201.1 2.1 fusion.1
  203.2 3.6 %pad_maximum_fusion = bf16[16,2,32,3584]{3,2,0,1:T(8,128)(2,1)} fusion(bf16[16,1,32,3584]{3,2,0,1:T(8,128)(2,1)S(1)} %fusion.1, bf16[16,1,32,3584]{3,2,0,1:T(8,128)(2,1)S(1)} %fusion), kind=kLoop, calls=%fused_computation.3 | loop fusion | flops 3670016 | bytes 14680064 | tf_op jit(solution)/shard_map/stack | solution.py:45
  206.8 0.0 reduce-scatter.2.cloned.1.call-update
  206.8 16.2 %reduce-scatter.2.cloned.1.call-done = bf16[16,2,32,1792]{3,2,0,1:T(8,128)(2,1)} async-done(((bf16[16,2,32,3584]{3,2,0,1:T(8,128)(2,1)}), bf16[16,2,32,1792]{3,2,0,1:T(8,128)(2,1)}) %reduce-scatter.2.cloned.1.call-update) | async-done | bytes 3670032 | tf_op jit(solution)/shard_map/reduce_scatter | solution.py:46
  223.0 4.2 %copy.19 = bf16[16,2,32,1792]{3,2,1,0:T(8,128)(2,1)} copy(bf16[16,2,32,1792]{3,2,0,1:T(8,128)(2,1)} %reduce-scatter.2.cloned.1.call-done) | data formatting | bytes 7340032 | tf_op jit(solution)/shard_map/reduce_scatter | solution.py:46
  227.2 0.0 copy-start
  227.2 7.1 %all-to-all-start.1 = ((bf16[16,2,32,1792]{3,2,1,0:T(8,128)(2,1)}), bf16[16,2,32,1792]{3,2,1,0:T(8,128)(2,1)}, u32[]{:S(2)}, u32[]{:S(2)}) async-start(bf16[16,2,32,1792]{3,2,1,0:T(8,128)(2,1)} %copy.19), calls=%async_computation.2 | async-start | bytes 7340032 | tf_op jit(solution)/shard_map/all_to_all | solution.py:49
  234.3 0.1 or.24
  234.4 0.0 copy-done
  234.4 0.1 copy.20
  234.5 0.1 fusion.29
  234.6 0.1 divide_select_fusion
  234.7 84.0 %all-to-all-done.1 = bf16[16,2,32,1792]{3,2,1,0:T(8,128)(2,1)} async-done(((bf16[16,2,32,1792]{3,2,1,0:T(8,128)(2,1)}), bf16[16,2,32,1792]{3,2,1,0:T(8,128)(2,1)}, u32[]{:S(2)}, u32[]{:S(2)}) %all-to-all-start.1) | async-done | bytes 3670048 | tf_op jit(solution)/shard_map/all_to_all | solution.py:49
  318.7 4.1 %concatenate.7 = bf16[1025,1792]{1,0:T(8,128)(2,1)} pad(bf16[1024,1792]{1,0:T(8,128)(2,1)} %bitcast.14, bf16[]{:T(256)} %constant.17.clone.1), padding=0_1x0_0 | pad | bytes 7343618 | tf_op jit(solution)/shard_map/concatenate | solution.py:51
  322.8 6.5 %gather_fusion.1 = bf16[512,1792]{1,0:T(8,128)(2,1)S(1)} fusion(bf16[1025,1792]{1,0:T(8,128)(2,1)} %concatenate.7, s32[1024]{0:T(1024)S(1)} %pad_clamp_fusion), kind=kCustom, calls=%fused_computation.1 | custom fusion | bytes 3672064 | tf_op jit(solution)/shard_map/gather | solution.py:54
  329.2 2.3 fusion.2
  (9 shorter events, 0.1 us)
Async XLA Ops:
  6.5 216.5 %reduce-scatter.2.cloned.1.call-start = ((), (), s32[]{:S(2)}) async-start(), calls=%async_computation.3 | async-start | bytes 11010048 | tf_op jit(solution)/shard_map/reduce_scatter | solution.py:46
  188.4 4.3 %copy-start.1 = (bf16[1,3584,512]{2,1,0:T(8,128)(2,1)S(1)}, bf16[1,3584,512]{2,1,0:T(8,128)(2,1)}, u32[]{:S(2)}) copy-start(bf16[1,3584,512]{2,1,0:T(8,128)(2,1)} %param.11) | copy-start | bytes 11010052
  192.7 2.1 copy-start.2
  196.9 2.2 copy-start.3
  227.2 7.2 %copy-start = (f32[64,8]{0,1:T(8,128)S(1)}, f32[64,8]{0,1:T(8,128)}, u32[]{:S(2)}) copy-start(f32[64,8]{0,1:T(8,128)} %param.8) | copy-start | bytes 6148
  227.2 91.5 %all-to-all-start.1 = ((bf16[16,2,32,1792]{3,2,1,0:T(8,128)(2,1)}), bf16[16,2,32,1792]{3,2,1,0:T(8,128)(2,1)}, u32[]{:S(2)}, u32[]{:S(2)}) async-start(bf16[16,2,32,1792]{3,2,1,0:T(8,128)(2,1)} %copy.19), calls=%async_computation.2 | async-start | bytes 7340032 | tf_op jit(solution)/shard_map/all_to_all | solution.py:49
Sparse Core Ops, SparseCore 0:
  207.0 16.0 reduce-scatter.1
where the time goes:
time: 339 us; the launch traced here: 338 us
  blocking collectives  166 us (49%)
  waiting for transfers between devices  100 us (29%)
  local copies, waits for them, and re-layouts  27.8 us (8%)
  matrix products  14.7 us (4%)
  between operations  13.6 us (4%)
  other arithmetic  8.79 us (3%)
  starting transfers between devices  7.09 us (2%)
    all_to_all x1, blocking collectives, body(): lax.all_to_all(outgoing, 'ep', split_axis=0, concat_axis=0, tiled=True)  166 us
    all_to_all x1, waiting for transfers between devices, body(): lax.all_to_all(summed, 'ep', split_axis=0, concat_axis=0, tiled=True)  84 us
    reduce_scatter x1, waiting for transfers between devices, body(): lax.psum_scatter(partial_out.astype(jnp.bfloat16), 'tp', scatter_dimensio...  16.2 us
    gather x1, local copies, waits for them, and re-layouts, body(): outgoing = padded[row_table].reshape(ep_size, 2, capacity, width)  7.3 us
    all_to_all x1, starting transfers between devices, body(): lax.all_to_all(summed, 'ep', split_axis=0, concat_axis=0, tiled=True)  7.09 us
  transfers between devices with their start and end apart: 2, of which 2 were waited for; matrix products, arithmetic and copies ran while one was open for 0% of the time, Pallas kernels for 0%

commit v1 on v0

v1 whole, which is shorter than its diff:
```python
import jax
import jax.numpy as jnp
from jax import lax
from jax.sharding import PartitionSpec as P

BF16 = jnp.bfloat16
F32 = jnp.float32
QUAD = 4


def route_weights(scores, expert_ids, copied, experts, capacity):
    rows = scores.shape[0]
    affinity = jax.nn.sigmoid(scores)
    gate_weight = 2.5 * affinity / jnp.sum(affinity, axis=1, keepdims=True)
    chosen = expert_ids[:, :, None] == jnp.arange(experts, dtype=jnp.int32)[None, None, :]
    member = jnp.any(chosen, axis=1)
    weight = jnp.sum(jnp.where(chosen, gate_weight[:, :, None], 0.0), axis=1)
    at = jnp.arange(rows, dtype=jnp.int32)
    below = (at[:, None] > at[None, :]).astype(BF16)
    rank = jnp.dot(below, member.astype(BF16), preferred_element_type=F32)
    kept = (rank < capacity) | (copied[None, :] == 1)
    return jnp.where(kept, weight, 0.0)


def body(tokens, scores, expert_ids, copied, w_gate, w_up, w_down):
    ep = lax.axis_size("ep")
    me = lax.axis_index("ep")
    core = lax.axis_index("tp")
    rows, width = tokens.shape
    top = expert_ids.shape[1]
    planes = ep // QUAD
    half = rows // 2
    share = width // 2
    capacity = min(rows * top // ep, rows // 2)

    def first_link(a):
        pairs = [(2 * e + c, 2 * (e ^ (1 + c)) + c) for e in range(ep) for c in range(2)]
        return lax.ppermute(a, ("ep", "tp"), pairs)

    def second_link(a):
        pairs = [(2 * e + c, 2 * (e ^ (2 - c)) + c) for e in range(ep) for c in range(2)]
        return lax.ppermute(a, ("ep", "tp"), pairs)

    def ring(a):
        return lax.ppermute(a, "ep", [(e, (e + QUAD) % ep) for e in range(ep)])

    def other_core(a):
        return lax.ppermute(a, "tp", [(0, 1), (1, 0)])

    down_mine = lax.dynamic_slice_in_dim(w_down[0], core * share, share, 1)
    down_sent = lax.dynamic_slice_in_dim(w_down[0], (1 - core) * share, share, 1)
    down = jnp.concatenate([down_mine, other_core(down_sent)], axis=0)

    weight = route_weights(scores, expert_ids, copied, ep, capacity)
    high = weight.astype(BF16)
    low = (weight - high.astype(F32)).astype(BF16)
    pad = -(2 * ep) % 128
    wide = jnp.concatenate([tokens, high, low, jnp.zeros((rows, pad), BF16)], axis=1)
    block = lax.dynamic_slice_in_dim(wide, core * half, half, 0)

    lane = jnp.arange(2 * ep + pad, dtype=jnp.int32)
    mine = ((lane == me) | (lane == me + ep)).astype(F32)

    def gather(block):
        pair = jnp.concatenate([block, first_link(block)], axis=0)
        far = second_link(pair)
        held = jnp.concatenate([pair, far], axis=0)
        theirs = other_core(held)
        m = held.reshape(QUAD, half, -1)
        o = theirs.reshape(QUAD, half, -1)
        kept = jnp.concatenate([m[0], m[2], o[0], o[1]], axis=0)
        sent = jnp.concatenate([m[1], m[3], o[2], o[3]], axis=0)
        return jnp.concatenate([kept, sent], axis=0)

    def experts(x):
        flat = x[:, :width]
        gate = jnp.dot(flat, w_gate[0], preferred_element_type=F32)
        up = jnp.dot(flat, w_up[0], preferred_element_type=F32)
        hidden = (jax.nn.silu(gate) * up).astype(BF16)
        r = other_core(hidden).reshape(2 * QUAD, half, -1)
        swapped = jnp.concatenate([r[2], r[6], r[0], r[4], r[3], r[7], r[1], r[5]], axis=0)
        both = jnp.concatenate([hidden, swapped], axis=1)
        scale = jnp.sum(x[:, width:].astype(F32) * mine[None, :], axis=1, keepdims=True)
        return jnp.dot(both, down, preferred_element_type=F32) * scale

    def scatter(y):
        n = y.shape[0] // 2
        got = first_link(y[n:].astype(BF16))
        part = (y[:n] + got.astype(F32)).reshape(2, 2, half, share)
        far = second_link(part[:, 1].reshape(2 * half, share).astype(BF16))
        return part[:, 0].reshape(2 * half, share) + far.astype(F32)

    blocks = [block]
    for _ in range(planes - 1):
        blocks.append(ring(blocks[-1]))
    outs = [experts(gather(b)) for b in blocks]
    total = None
    for step in list(range(1, planes)) + [0]:
        part = scatter(outs[step])
        total = part if total is None else ring(total.astype(BF16)).astype(F32) + part
    mine_rows, other_rows = total[:half], total[half:]
    first = jnp.where(core == 0, mine_rows, other_rows)
    second = jnp.where(core == 0, other_rows, mine_rows)
    return jnp.concatenate([first, second], axis=0).astype(BF16)


def solution(mesh):
    in_specs = (
        P(("grp", "ep"), None),
        P(("grp", "ep"), None),
        P(("grp", "ep"), None),
        P("grp"),
        P("ep", None, "tp"),
        P("ep", None, "tp"),
        P("ep", "tp", None),
    )
    out_specs = P(("grp", "ep"), "tp")
    return jax.shard_map(body, mesh=mesh, in_specs=in_specs, out_specs=out_specs, check_vma=False)
```

time: 339 us -> 115 us (0.34)
  the two profiles are of different devices: /device:TPU:14 before, /device:TPU:0 now
where the time goes in v1:
time: 115 us
  waiting for transfers between devices  49.8 us (43%)
  starting transfers between devices  29.4 us (26%)
  matrix products  19.6 us (17%)
  local copies, waits for them, and re-layouts  10.1 us (9%)
  other arithmetic  4.84 us (4%)
    ppermute x8, waiting for transfers between devices, first_link(): return lax.ppermute(a, ('ep', 'tp'), pairs)  26.8 us
    ppermute x6, waiting for transfers between devices, ring(): return lax.ppermute(a, 'ep', [(e, (e + QUAD) % ep) for e in range(ep)])  12.5 us
    dot_general x4, matrix products, experts(): return jnp.dot(both, down, preferred_element_type=F32) * scale  10.5 us
    ppermute x8, waiting for transfers between devices, second_link(): return lax.ppermute(a, ('ep', 'tp'), pairs)  10.4 us
    ppermute x8, starting transfers between devices, first_link(): return lax.ppermute(a, ('ep', 'tp'), pairs)  10.3 us
    ppermute x6, starting transfers between devices, ring(): return lax.ppermute(a, 'ep', [(e, (e + QUAD) % ep) for e in range(ep)])  9.52 us
    ppermute x8, starting transfers between devices, second_link(): return lax.ppermute(a, ('ep', 'tp'), pairs)  8.56 us
    unnamed x56, local copies, waits for them, and re-layouts  4.65 us
  transfers between devices with their start and end apart: 31, of which 15 were waited for; matrix products, arithmetic and copies ran while one was open for 22% of the time, Pallas kernels for 0%

profile of v1, /device:TPU:0, one launch (start us, length us, event | category | flops | bytes accessed | tf_op | source)
XLA Modules:
  0.0 114.6 jit_solution(5170322975359166121)
XLA Ops:
  0.0 0.7 fusion.45
  0.7 0.7 multiply_divide_fusion
  1.4 0.7 fusion.44
  2.1 0.7 select_reduce_fusion
  2.8 0.7 broadcast_compare_fusion
  3.5 0.1 subtract_convert_fusion
  3.6 0.1 copy.12
  3.7 0.1 copy.13
  3.8 1.1 concatenate.78
  5.0 0.7 constant_dynamic-update-slice_fusion.31
  5.7 3.0 %collective-permute-start = (bf16[32,3712]{1,0:T(8,128)(2,1)S(1)}, bf16[32,3712]{1,0:T(8,128)(2,1)S(1)}, u32[]{:S(2)}, u32[]{:S(2)}) collective-permute-start(bf16[32,3712]{1,0:T(8,128)(2,1)S(1)} %get-tuple-element.10), channel_id=1, source_target_pairs={{0,8},{2,10},{4,12},{6,14},{8,16},{10,18},{12,20},{14,22},{16,24},... | collective-permute-start | bytes 712712 | tf_op jit(solution)/shard_map/ppermute | solution.py:45
  8.7 1.5 %collective-permute-start.25 = (bf16[32,3712]{1,0:T(8,128)(2,1)S(1)}, bf16[32,3712]{1,0:T(8,128)(2,1)S(1)}, u32[]{:S(2)}, u32[]{:S(2)}) collective-permute-start(bf16[32,3712]{1,0:T(8,128)(2,1)S(1)} %get-tuple-element.10), channel_id=1, source_target_pairs={{0,2},{1,5},{2,0},{3,7},{4,6},{5,1},{6,4},{7,3},{8,10},{9,13},{10,... | collective-permute-start | bytes 712712 | tf_op jit(solution)/shard_map/ppermute | solution.py:38
  10.2 3.5 %dynamic-slice_bitcast_fusion.1 = (bf16[512,1792]{1,0:T(8,128)(2,1)S(1)}, bf16[512,1792]{1,0:T(8,128)(2,1)}) fusion(bf16[1,512,3584]{2,1,0:T(8,128)(2,1)} %param.13, s32[]{:T(128)S(6)} %select_n.33, s32[]{:T(128)S(6)} %select_n.34), kind=kLoop, calls=%fused_computation.22 | loop fusion | bytes 7340040 | tf_op jit(solution)/shard_map/dynamic_slice | solution.py:50
  13.7 1.1 collective-permute-done.25
  14.9 1.6 %collective-permute-start.26 = (bf16[64,3712]{1,0:T(8,128)(2,1)S(1)}, bf16[64,3712]{1,0:T(8,128)(2,1)S(1)}, u32[]{:S(2)}, u32[]{:S(2)}) collective-permute-start(bf16[64,3712]{1,0:T(8,128)(2,1)S(1)} %pad_maximum_fusion.8), channel_id=1, source_target_pairs={{0,4},{1,3},{2,6},{3,1},{4,0},{5,7},{6,2},{7,5},{8,12},{9,11},{10,... | collective-permute-start | bytes 1425416 | tf_op jit(solution)/shard_map/ppermute | solution.py:42
  16.5 1.5 %collective-permute-start.1 = (bf16[32,3712]{1,0:T(8,128)(2,1)S(1)}, bf16[32,3712]{1,0:T(8,128)(2,1)S(1)}, u32[]{:S(2)}, u32[]{:S(2)}) collective-permute-start(bf16[32,3712]{1,0:T(8,128)(2,1)S(1)} %collective-permute-done), channel_id=1, source_target_pairs={{0,2},{1,5},{2,0},{3,7},{4,6},{5,1},{6,4},{7,3},{8,10},{9,13},{10,... | collective-permute-start | bytes 712712 | tf_op jit(solution)/shard_map/ppermute | solution.py:38
  18.0 1.5 %collective-permute-start.9 = (bf16[32,3712]{1,0:T(8,128)(2,1)S(1)}, bf16[32,3712]{1,0:T(8,128)(2,1)S(1)}, u32[]{:S(2)}, u32[]{:S(2)}) collective-permute-start(bf16[32,3712]{1,0:T(8,128)(2,1)S(1)} %collective-permute-done), channel_id=1, source_target_pairs={{0,8},{2,10},{4,12},{6,14},{8,16},{10,18},{12,20},{14,22},{16,24},... | collective-permute-start | bytes 712712 | tf_op jit(solution)/shard_map/ppermute | solution.py:45
  19.6 5.0 %collective-permute-done.1 = bf16[32,3712]{1,0:T(8,128)(2,1)S(1)} collective-permute-done((bf16[32,3712]{1,0:T(8,128)(2,1)S(1)}, bf16[32,3712]{1,0:T(8,128)(2,1)S(1)}, u32[]{:S(2)}, u32[]{:S(2)}) %collective-permute-start.1) | collective-permute-done | bytes 237600 | tf_op jit(solution)/shard_map/ppermute | solution.py:38
  24.6 1.6 %collective-permute-start.2 = (bf16[64,3712]{1,0:T(8,128)(2,1)S(1)}, bf16[64,3712]{1,0:T(8,128)(2,1)S(1)}, u32[]{:S(2)}, u32[]{:S(2)}) collective-permute-start(bf16[64,3712]{1,0:T(8,128)(2,1)S(1)} %pad_maximum_fusion.5), channel_id=1, source_target_pairs={{0,4},{1,3},{2,6},{3,1},{4,0},{5,7},{6,2},{7,5},{8,12},{9,11},{10,... | collective-permute-start | bytes 1425416 | tf_op jit(solution)/shard_map/ppermute | solution.py:42
  26.3 1.1 collective-permute-start.17
  27.4 1.2 %collective-permute-start.10 = (bf16[32,3712]{1,0:T(8,128)(2,1)S(1)}, bf16[32,3712]{1,0:T(8,128)(2,1)S(1)}, u32[]{:S(2)}, u32[]{:S(2)}) collective-permute-start(bf16[32,3712]{1,0:T(8,128)(2,1)S(1)} %collective-permute-done.9), channel_id=1, source_target_pairs={{0,2},{1,5},{2,0},{3,7},{4,6},{5,1},{6,4},{7,3},{8,10},{9,13},{10,... | collective-permute-start | bytes 712712 | tf_op jit(solution)/shard_map/ppermute | solution.py:38
  28.8 5.0 %collective-permute-done.10 = bf16[32,3712]{1,0:T(8,128)(2,1)S(1)} collective-permute-done((bf16[32,3712]{1,0:T(8,128)(2,1)S(1)}, bf16[32,3712]{1,0:T(8,128)(2,1)S(1)}, u32[]{:S(2)}, u32[]{:S(2)}) %collective-permute-start.10) | collective-permute-done | bytes 237600 | tf_op jit(solution)/shard_map/ppermute | solution.py:38
  33.9 1.2 %collective-permute-start.11 = (bf16[64,3712]{1,0:T(8,128)(2,1)S(1)}, bf16[64,3712]{1,0:T(8,128)(2,1)S(1)}, u32[]{:S(2)}, u32[]{:S(2)}) collective-permute-start(bf16[64,3712]{1,0:T(8,128)(2,1)S(1)} %pad_maximum_fusion.6), channel_id=1, source_target_pairs={{0,4},{1,3},{2,6},{3,1},{4,0},{5,7},{6,2},{7,5},{8,12},{9,11},{10,... | collective-permute-start | bytes 1425416 | tf_op jit(solution)/shard_map/ppermute | solution.py:42
  35.1 1.6 %collective-permute-start.18 = (bf16[32,3712]{1,0:T(8,128)(2,1)S(1)}, bf16[32,3712]{1,0:T(8,128)(2,1)S(1)}, u32[]{:S(2)}, u32[]{:S(2)}) collective-permute-start(bf16[32,3712]{1,0:T(8,128)(2,1)S(1)} %collective-permute-done.17), channel_id=1, source_target_pairs={{0,2},{1,5},{2,0},{3,7},{4,6},{5,1},{6,4},{7,3},{8,10},{9,13},{10,... | collective-permute-start | bytes 712712 | tf_op jit(solution)/shard_map/ppermute | solution.py:38
  36.9 6.2 %collective-permute-done.18 = bf16[32,3712]{1,0:T(8,128)(2,1)S(1)} collective-permute-done((bf16[32,3712]{1,0:T(8,128)(2,1)S(1)}, bf16[32,3712]{1,0:T(8,128)(2,1)S(1)}, u32[]{:S(2)}, u32[]{:S(2)}) %collective-permute-start.18) | collective-permute-done | bytes 237600 | tf_op jit(solution)/shard_map/ppermute | solution.py:38
  43.2 1.4 %collective-permute-done.11 = bf16[64,3712]{1,0:T(8,128)(2,1)S(1)} collective-permute-done((bf16[64,3712]{1,0:T(8,128)(2,1)S(1)}, bf16[64,3712]{1,0:T(8,128)(2,1)S(1)}, u32[]{:S(2)}, u32[]{:S(2)}) %collective-permute-start.11) | collective-permute-done | bytes 475168 | tf_op jit(solution)/shard_map/ppermute | solution.py:42
  44.8 7.0 %collective-permute-done.19 = bf16[64,3712]{1,0:T(8,128)(2,1)S(1)} collective-permute-done((bf16[64,3712]{1,0:T(8,128)(2,1)S(1)}, bf16[64,3712]{1,0:T(8,128)(2,1)S(1)}, u32[]{:S(2)}, u32[]{:S(2)}) %collective-permute-start.19) | collective-permute-done | bytes 475168 | tf_op jit(solution)/shard_map/ppermute | solution.py:42
  52.2 1.7 %copy-done.1 = bf16[1,3584,512]{2,1,0:T(8,128)(2,1)S(1)} copy-done((bf16[1,3584,512]{2,1,0:T(8,128)(2,1)S(1)}, bf16[1,3584,512]{2,1,0:T(8,128)(2,1)}, u32[]{:S(2)}) %copy-start.1) | copy-done | bytes 3670040
  53.8 1.1 fusion.8
  55.0 0.9 copy-done.2
  55.9 1.1 multiply_convert_fusion
  57.3 1.1 fusion.14
  58.4 1.1 multiply_convert_fusion.3
  59.5 0.5 collective-permute-start.4
  60.4 1.1 fusion.12
  61.5 1.1 multiply_convert_fusion.2
  62.6 0.1 collective-permute-start.13
  63.0 0.2 multiply_reduce_fusion.3
  63.2 1.1 fusion.10
  64.3 2.6 %convolution_multiply_fusion.3 = f32[256,1792]{1,0:T(8,128)S(1)} fusion(f32[256]{0:T(256)S(1)} %get-tuple-element.5, bf16[256,512]{1,0:T(8,128)(2,1)S(1)} %constant_dynamic-update-slice_fusion.2, bf16[256,512]{1,0:T(8,128)(2,1)S(1)} %multiply_convert_fusion.3, bf16[512,1792]{1,0:T(8,128)(2,1)} %collective-permute-done.5, ...), kind=kOutput, calls=%fused_computation.20 | convolution fusion | flops 948371456 | bytes 6030336 | tf_op jit(solution)/shard_map/dot_general | solution.py:84
  67.0 1.8 %collective-permute-start.6 = (bf16[128,1792]{1,0:T(8,128)(2,1)S(1)}, bf16[128,1792]{1,0:T(8,128)(2,1)S(1)}, u32[]{:S(2)}, u32[]{:S(2)}) collective-permute-start(bf16[128,1792]{1,0:T(8,128)(2,1)S(1)} %slice.561), channel_id=1, source_target_pairs={{0,2},{1,5},{2,0},{3,7},{4,6},{5,1},{6,4},{7,3},{8,10},{9,13},{10,... | collective-permute-start | bytes 1376264 | tf_op jit(solution)/shard_map/ppermute | solution.py:38
  68.8 1.1 multiply_convert_fusion.1
  70.1 2.6 %convolution_multiply_fusion = f32[256,1792]{1,0:T(8,128)S(1)} fusion(f32[256]{0:T(256)S(1)} %get-tuple-element.8, bf16[256,512]{1,0:T(8,128)(2,1)S(1)} %constant_dynamic-update-slice_fusion.32, bf16[256,512]{1,0:T(8,128)(2,1)S(1)} %multiply_convert_fusion, bf16[512,1792]{1,0:T(8,128)(2,1)} %collective-permute-done.5, ...), kind=kOutput, calls=%fused_computation.17 | convolution fusion | flops 948371456 | bytes 6030336 | tf_op jit(solution)/shard_map/dot_general | solution.py:84
  72.8 0.5 collective-permute-start.29
  73.4 2.6 %convolution_multiply_fusion.2 = f32[256,1792]{1,0:T(8,128)S(1)} fusion(f32[256]{0:T(256)S(1)} %get-tuple-element.6, bf16[256,512]{1,0:T(8,128)(2,1)S(1)} %constant_dynamic-update-slice_fusion.12, bf16[256,512]{1,0:T(8,128)(2,1)S(1)} %multiply_convert_fusion.2, bf16[512,1792]{1,0:T(8,128)(2,1)} %collective-permute-done.5, ...), kind=kOutput, calls=%fused_computation.19 | convolution fusion | flops 948371456 | bytes 6030336 | tf_op jit(solution)/shard_map/dot_general | solution.py:84
  76.1 1.6 %collective-permute-start.14 = (bf16[128,1792]{1,0:T(8,128)(2,1)S(1)}, bf16[128,1792]{1,0:T(8,128)(2,1)S(1)}, u32[]{:S(2)}, u32[]{:S(2)}) collective-permute-start(bf16[128,1792]{1,0:T(8,128)(2,1)S(1)} %slice.560), channel_id=1, source_target_pairs={{0,2},{1,5},{2,0},{3,7},{4,6},{5,1},{6,4},{7,3},{8,10},{9,13},{10,... | collective-permute-start | bytes 1376264 | tf_op jit(solution)/shard_map/ppermute | solution.py:38
  77.8 2.6 %convolution_multiply_fusion.1 = f32[256,1792]{1,0:T(8,128)S(1)} fusion(f32[256]{0:T(256)S(1)} %get-tuple-element.7, bf16[256,512]{1,0:T(8,128)(2,1)S(1)} %constant_dynamic-update-slice_fusion.22, bf16[256,512]{1,0:T(8,128)(2,1)S(1)} %multiply_convert_fusion.1, bf16[512,1792]{1,0:T(8,128)(2,1)} %collective-permute-done.5, ...), kind=kOutput, calls=%fused_computation.18 | convolution fusion | flops 948371456 | bytes 6030336 | tf_op jit(solution)/shard_map/dot_general | solution.py:84
  80.5 0.5 collective-permute-start.22
  81.2 1.8 %collective-permute-start.7 = (bf16[64,1792]{1,0:T(8,128)(2,1)S(1)}, bf16[64,1792]{1,0:T(8,128)(2,1)S(1)}, u32[]{:S(2)}, u32[]{:S(2)}) collective-permute-start(bf16[64,1792]{1,0:T(8,128)(2,1)S(1)} %bitcast.70), channel_id=1, source_target_pairs={{0,4},{1,3},{2,6},{3,1},{4,0},{5,7},{6,2},{7,5},{8,12},{9,11},{10,... | collective-permute-start | bytes 688136 | tf_op jit(solution)/shard_map/ppermute | solution.py:42
  83.0 5.7 %collective-permute-done.14 = bf16[128,1792]{1,0:T(8,128)(2,1)S(1)} collective-permute-done((bf16[128,1792]{1,0:T(8,128)(2,1)S(1)}, bf16[128,1792]{1,0:T(8,128)(2,1)S(1)}, u32[]{:S(2)}, u32[]{:S(2)}) %collective-permute-start.14) | collective-permute-done | bytes 458784 | tf_op jit(solution)/shard_map/ppermute | solution.py:38
  88.9 0.9 collective-permute-done.7
  89.8 2.5 %collective-permute-start.8 = (bf16[64,1792]{1,0:T(8,128)(2,1)S(1)}, bf16[64,1792]{1,0:T(8,128)(2,1)S(1)}, u32[]{:S(2)}, u32[]{:S(2)}) collective-permute-start(bf16[64,1792]{1,0:T(8,128)(2,1)S(1)} %fusion.43), channel_id=1, source_target_pairs={{0,8},{2,10},{4,12},{6,14},{8,16},{10,18},{12,20},{14,22},{16,24},... | collective-permute-start | bytes 688136 | tf_op jit(solution)/shard_map/ppermute | solution.py:45
  92.3 3.7 %collective-permute-done.22 = bf16[128,1792]{1,0:T(8,128)(2,1)S(1)} collective-permute-done((bf16[128,1792]{1,0:T(8,128)(2,1)S(1)}, bf16[128,1792]{1,0:T(8,128)(2,1)S(1)}, u32[]{:S(2)}, u32[]{:S(2)}) %collective-permute-start.22) | collective-permute-done | bytes 458784 | tf_op jit(solution)/shard_map/ppermute | solution.py:38
  96.1 0.1 slice_add_fusion.1
  96.2 0.5 collective-permute-start.23
  96.7 1.1 collective-permute-done.8
  97.9 0.1 fusion.42
  97.9 1.3 %collective-permute-start.16 = (bf16[64,1792]{1,0:T(8,128)(2,1)S(1)}, bf16[64,1792]{1,0:T(8,128)(2,1)S(1)}, u32[]{:S(2)}, u32[]{:S(2)}) collective-permute-start(bf16[64,1792]{1,0:T(8,128)(2,1)S(1)} %fusion.42), channel_id=1, source_target_pairs={{0,8},{2,10},{4,12},{6,14},{8,16},{10,18},{12,20},{14,22},{16,24},... | collective-permute-start | bytes 688136 | tf_op jit(solution)/shard_map/ppermute | solution.py:45
  99.4 1.7 %collective-permute-start.30 = (bf16[64,1792]{1,0:T(8,128)(2,1)S(1)}, bf16[64,1792]{1,0:T(8,128)(2,1)S(1)}, u32[]{:S(2)}, u32[]{:S(2)}) collective-permute-start(bf16[64,1792]{1,0:T(8,128)(2,1)S(1)} %bitcast.69), channel_id=1, source_target_pairs={{0,4},{1,3},{2,6},{3,1},{4,0},{5,7},{6,2},{7,5},{8,12},{9,11},{10,... | collective-permute-start | bytes 688136 | tf_op jit(solution)/shard_map/ppermute | solution.py:42
  101.2 1.1 collective-permute-done.23
  102.3 3.5 %collective-permute-done.16 = bf16[64,1792]{1,0:T(8,128)(2,1)S(1)} collective-permute-done((bf16[64,1792]{1,0:T(8,128)(2,1)S(1)}, bf16[64,1792]{1,0:T(8,128)(2,1)S(1)}, u32[]{:S(2)}, u32[]{:S(2)}) %collective-permute-start.16) | collective-permute-done | bytes 229408 | tf_op jit(solution)/shard_map/ppermute | solution.py:45
  105.8 0.1 fusion.40
  106.0 7.7 %collective-permute-done.24 = bf16[64,1792]{1,0:T(8,128)(2,1)S(1)} collective-permute-done((bf16[64,1792]{1,0:T(8,128)(2,1)S(1)}, bf16[64,1792]{1,0:T(8,128)(2,1)S(1)}, u32[]{:S(2)}, u32[]{:S(2)}) %collective-permute-start.24) | collective-permute-done | bytes 229408 | tf_op jit(solution)/shard_map/ppermute | solution.py:45
  113.9 0.7 copy-done.3
  (117 shorter events, 2.9 us)
Async XLA Ops:
  5.7 10.8 %collective-permute-start = (bf16[32,3712]{1,0:T(8,128)(2,1)S(1)}, bf16[32,3712]{1,0:T(8,128)(2,1)S(1)}, u32[]{:S(2)}, u32[]{:S(2)}) collective-permute-start(bf16[32,3712]{1,0:T(8,128)(2,1)S(1)} %get-tuple-element.10), channel_id=1, source_target_pairs={{0,8},{2,10},{4,12},{6,14},{8,16},{10,18},{12,20},{14,22},{16,24},... | collective-permute-start | bytes 712712 | tf_op jit(solution)/shard_map/ppermute | solution.py:45
  8.7 6.1 %collective-permute-start.25 = (bf16[32,3712]{1,0:T(8,128)(2,1)S(1)}, bf16[32,3712]{1,0:T(8,128)(2,1)S(1)}, u32[]{:S(2)}, u32[]{:S(2)}) collective-permute-start(bf16[32,3712]{1,0:T(8,128)(2,1)S(1)} %get-tuple-element.10), channel_id=1, source_target_pairs={{0,2},{1,5},{2,0},{3,7},{4,6},{5,1},{6,4},{7,3},{8,10},{9,13},{10,... | collective-permute-start | bytes 712712 | tf_op jit(solution)/shard_map/ppermute | solution.py:38
  13.7 50.6 %collective-permute-start.5 = (bf16[512,1792]{1,0:T(8,128)(2,1)}, bf16[512,1792]{1,0:T(8,128)(2,1)}, u32[]{:S(2)}, u32[]{:S(2)}) collective-permute-start(bf16[512,1792]{1,0:T(8,128)(2,1)} %get-tuple-element.14), channel_id=1, source_target_pairs={{0,1},{1,0},{2,3},{3,2},{4,5},{5,4},{6,7},{7,6},{8,9},{9,8},{10,11... | collective-permute-start | bytes 5505032 | tf_op jit(solution)/shard_map/ppermute | solution.py:48
  14.9 13.8 %collective-permute-start.26 = (bf16[64,3712]{1,0:T(8,128)(2,1)S(1)}, bf16[64,3712]{1,0:T(8,128)(2,1)S(1)}, u32[]{:S(2)}, u32[]{:S(2)}) collective-permute-start(bf16[64,3712]{1,0:T(8,128)(2,1)S(1)} %pad_maximum_fusion.8), channel_id=1, source_target_pairs={{0,4},{1,3},{2,6},{3,1},{4,0},{5,7},{6,2},{7,5},{8,12},{9,11},{10,... | collective-permute-start | bytes 1425416 | tf_op jit(solution)/shard_map/ppermute | solution.py:42
  16.5 8.1 %collective-permute-start.1 = (bf16[32,3712]{1,0:T(8,128)(2,1)S(1)}, bf16[32,3712]{1,0:T(8,128)(2,1)S(1)}, u32[]{:S(2)}, u32[]{:S(2)}) collective-permute-start(bf16[32,3712]{1,0:T(8,128)(2,1)S(1)} %collective-permute-done), channel_id=1, source_target_pairs={{0,2},{1,5},{2,0},{3,7},{4,6},{5,1},{6,4},{7,3},{8,10},{9,13},{10,... | collective-permute-start | bytes 712712 | tf_op jit(solution)/shard_map/ppermute | solution.py:38
  18.0 8.3 %collective-permute-start.9 = (bf16[32,3712]{1,0:T(8,128)(2,1)S(1)}, bf16[32,3712]{1,0:T(8,128)(2,1)S(1)}, u32[]{:S(2)}, u32[]{:S(2)}) collective-permute-start(bf16[32,3712]{1,0:T(8,128)(2,1)S(1)} %collective-permute-done), channel_id=1, source_target_pairs={{0,8},{2,10},{4,12},{6,14},{8,16},{10,18},{12,20},{14,22},{16,24},... | collective-permute-start | bytes 712712 | tf_op jit(solution)/shard_map/ppermute | solution.py:45
  24.6 10.5 %copy-start = (bf16[256,3712]{1,0:T(8,128)(2,1)S(1)}, bf16[256,3712]{1,0:T(8,128)(2,1)}, u32[]{:S(2)}) copy-start(bf16[256,3712]{1,0:T(8,128)(2,1)} %get-tuple-element.9) | copy-start | bytes 5701636
  24.6 12.1 %collective-permute-start.2 = (bf16[64,3712]{1,0:T(8,128)(2,1)S(1)}, bf16[64,3712]{1,0:T(8,128)(2,1)S(1)}, u32[]{:S(2)}, u32[]{:S(2)}) collective-permute-start(bf16[64,3712]{1,0:T(8,128)(2,1)S(1)} %pad_maximum_fusion.5), channel_id=1, source_target_pairs={{0,4},{1,3},{2,6},{3,1},{4,0},{5,7},{6,2},{7,5},{8,12},{9,11},{10,... | collective-permute-start | bytes 1425416 | tf_op jit(solution)/shard_map/ppermute | solution.py:42
  26.3 8.8 %collective-permute-start.17 = (bf16[32,3712]{1,0:T(8,128)(2,1)S(1)}, bf16[32,3712]{1,0:T(8,128)(2,1)S(1)}, u32[]{:S(2)}, u32[]{:S(2)}) collective-permute-start(bf16[32,3712]{1,0:T(8,128)(2,1)S(1)} %collective-permute-done.9), channel_id=1, source_target_pairs={{0,8},{2,10},{4,12},{6,14},{8,16},{10,18},{12,20},{14,22},{16,24},... | collective-permute-start | bytes 712712 | tf_op jit(solution)/shard_map/ppermute | solution.py:45
  27.4 6.5 %collective-permute-start.10 = (bf16[32,3712]{1,0:T(8,128)(2,1)S(1)}, bf16[32,3712]{1,0:T(8,128)(2,1)S(1)}, u32[]{:S(2)}, u32[]{:S(2)}) collective-permute-start(bf16[32,3712]{1,0:T(8,128)(2,1)S(1)} %collective-permute-done.9), channel_id=1, source_target_pairs={{0,2},{1,5},{2,0},{3,7},{4,6},{5,1},{6,4},{7,3},{8,10},{9,13},{10,... | collective-permute-start | bytes 712712 | tf_op jit(solution)/shard_map/ppermute | solution.py:38
  28.7 23.3 %collective-permute-start.27 = (bf16[128,3712]{1,0:T(8,128)(2,1)S(1)}, bf16[128,3712]{1,0:T(8,128)(2,1)S(1)}, u32[]{:S(2)}, u32[]{:S(2)}) collective-permute-start(bf16[128,3712]{1,0:T(8,128)(2,1)S(1)} %pad_maximum_fusion.4), channel_id=1, source_target_pairs={{0,1},{1,0},{2,3},{3,2},{4,5},{5,4},{6,7},{7,6},{8,9},{9,8},{10,11... | collective-permute-start | bytes 2850824 | tf_op jit(solution)/shard_map/ppermute | solution.py:48
  33.9 10.7 %collective-permute-start.11 = (bf16[64,3712]{1,0:T(8,128)(2,1)S(1)}, bf16[64,3712]{1,0:T(8,128)(2,1)S(1)}, u32[]{:S(2)}, u32[]{:S(2)}) collective-permute-start(bf16[64,3712]{1,0:T(8,128)(2,1)S(1)} %pad_maximum_fusion.6), channel_id=1, source_target_pairs={{0,4},{1,3},{2,6},{3,1},{4,0},{5,7},{6,2},{7,5},{8,12},{9,11},{10,... | collective-permute-start | bytes 1425416 | tf_op jit(solution)/shard_map/ppermute | solution.py:42
  35.1 7.9 %collective-permute-start.18 = (bf16[32,3712]{1,0:T(8,128)(2,1)S(1)}, bf16[32,3712]{1,0:T(8,128)(2,1)S(1)}, u32[]{:S(2)}, u32[]{:S(2)}) collective-permute-start(bf16[32,3712]{1,0:T(8,128)(2,1)S(1)} %collective-permute-done.17), channel_id=1, source_target_pairs={{0,2},{1,5},{2,0},{3,7},{4,6},{5,1},{6,4},{7,3},{8,10},{9,13},{10,... | collective-permute-start | bytes 712712 | tf_op jit(solution)/shard_map/ppermute | solution.py:38
  36.8 20.3 %collective-permute-start.3 = (bf16[128,3712]{1,0:T(8,128)(2,1)S(1)}, bf16[128,3712]{1,0:T(8,128)(2,1)S(1)}, u32[]{:S(2)}, u32[]{:S(2)}) collective-permute-start(bf16[128,3712]{1,0:T(8,128)(2,1)S(1)} %pad_maximum_fusion.1), channel_id=1, source_target_pairs={{0,1},{1,0},{2,3},{3,2},{4,5},{5,4},{6,7},{7,6},{8,9},{9,8},{10,11... | collective-permute-start | bytes 2850824 | tf_op jit(solution)/shard_map/ppermute | solution.py:48
  43.1 8.7 %collective-permute-start.19 = (bf16[64,3712]{1,0:T(8,128)(2,1)S(1)}, bf16[64,3712]{1,0:T(8,128)(2,1)S(1)}, u32[]{:S(2)}, u32[]{:S(2)}) collective-permute-start(bf16[64,3712]{1,0:T(8,128)(2,1)S(1)} %pad_maximum_fusion.7), channel_id=1, source_target_pairs={{0,4},{1,3},{2,6},{3,1},{4,0},{5,7},{6,2},{7,5},{8,12},{9,11},{10,... | collective-permute-start | bytes 1425416 | tf_op jit(solution)/shard_map/ppermute | solution.py:42
  44.7 15.5 %collective-permute-start.12 = (bf16[128,3712]{1,0:T(8,128)(2,1)S(1)}, bf16[128,3712]{1,0:T(8,128)(2,1)S(1)}, u32[]{:S(2)}, u32[]{:S(2)}) collective-permute-start(bf16[128,3712]{1,0:T(8,128)(2,1)S(1)} %pad_maximum_fusion.2), channel_id=1, source_target_pairs={{0,1},{1,0},{2,3},{3,2},{4,5},{5,4},{6,7},{7,6},{8,9},{9,8},{10,11... | collective-permute-start | bytes 2850824 | tf_op jit(solution)/shard_map/ppermute | solution.py:48
  51.8 2.0 %copy-start.1 = (bf16[1,3584,512]{2,1,0:T(8,128)(2,1)S(1)}, bf16[1,3584,512]{2,1,0:T(8,128)(2,1)}, u32[]{:S(2)}) copy-start(bf16[1,3584,512]{2,1,0:T(8,128)(2,1)} %param.11) | copy-start | bytes 11010052
  51.9 10.9 %collective-permute-start.20 = (bf16[128,3712]{1,0:T(8,128)(2,1)S(1)}, bf16[128,3712]{1,0:T(8,128)(2,1)S(1)}, u32[]{:S(2)}, u32[]{:S(2)}) collective-permute-start(bf16[128,3712]{1,0:T(8,128)(2,1)S(1)} %pad_maximum_fusion.3), channel_id=1, source_target_pairs={{0,1},{1,0},{2,3},{3,2},{4,5},{5,4},{6,7},{7,6},{8,9},{9,8},{10,11... | collective-permute-start | bytes 2850824 | tf_op jit(solution)/shard_map/ppermute | solution.py:48
  53.8 2.0 %copy-start.2 = (bf16[1,3584,512]{2,1,0:T(8,128)(2,1)S(1)}, bf16[1,3584,512]{2,1,0:T(8,128)(2,1)}, u32[]{:S(2)}) copy-start(bf16[1,3584,512]{2,1,0:T(8,128)(2,1)} %param.12) | copy-start | bytes 11010052
  57.0 3.1 %collective-permute-start.28 = (bf16[256,512]{1,0:T(8,128)(2,1)S(1)}, bf16[256,512]{1,0:T(8,128)(2,1)S(1)}, u32[]{:S(2)}, u32[]{:S(2)}) collective-permute-start(bf16[256,512]{1,0:T(8,128)(2,1)S(1)} %multiply_convert_fusion), channel_id=1, source_target_pairs={{0,1},{1,0},{2,3},{3,2},{4,5},{5,4},{6,7},{7,6},{8,9},{9,8},{10,11... | collective-permute-start | bytes 786440 | tf_op jit(solution)/shard_map/ppermute | solution.py:48
  59.5 3.2 %collective-permute-start.4 = (bf16[256,512]{1,0:T(8,128)(2,1)S(1)}, bf16[256,512]{1,0:T(8,128)(2,1)S(1)}, u32[]{:S(2)}, u32[]{:S(2)}) collective-permute-start(bf16[256,512]{1,0:T(8,128)(2,1)S(1)} %multiply_convert_fusion.3), channel_id=1, source_target_pairs={{0,1},{1,0},{2,3},{3,2},{4,5},{5,4},{6,7},{7,6},{8,9},{9,8},{10,11... | collective-permute-start | bytes 786440 | tf_op jit(solution)/shard_map/ppermute | solution.py:48
  62.6 10.7 %collective-permute-start.13 = (bf16[256,512]{1,0:T(8,128)(2,1)S(1)}, bf16[256,512]{1,0:T(8,128)(2,1)S(1)}, u32[]{:S(2)}, u32[]{:S(2)}) collective-permute-start(bf16[256,512]{1,0:T(8,128)(2,1)S(1)} %multiply_convert_fusion.2), channel_id=1, source_target_pairs={{0,1},{1,0},{2,3},{3,2},{4,5},{5,4},{6,7},{7,6},{8,9},{9,8},{10,11... | collective-permute-start | bytes 786440 | tf_op jit(solution)/shard_map/ppermute | solution.py:48
  67.0 14.0 %collective-permute-start.6 = (bf16[128,1792]{1,0:T(8,128)(2,1)S(1)}, bf16[128,1792]{1,0:T(8,128)(2,1)S(1)}, u32[]{:S(2)}, u32[]{:S(2)}) collective-permute-start(bf16[128,1792]{1,0:T(8,128)(2,1)S(1)} %slice.561), channel_id=1, source_target_pairs={{0,2},{1,5},{2,0},{3,7},{4,6},{5,1},{6,4},{7,3},{8,10},{9,13},{10,... | collective-permute-start | bytes 1376264 | tf_op jit(solution)/shard_map/ppermute | solution.py:38
  70.0 7.7 %collective-permute-start.21 = (bf16[256,512]{1,0:T(8,128)(2,1)S(1)}, bf16[256,512]{1,0:T(8,128)(2,1)S(1)}, u32[]{:S(2)}, u32[]{:S(2)}) collective-permute-start(bf16[256,512]{1,0:T(8,128)(2,1)S(1)} %multiply_convert_fusion.1), channel_id=1, source_target_pairs={{0,1},{1,0},{2,3},{3,2},{4,5},{5,4},{6,7},{7,6},{8,9},{9,8},{10,11... | collective-permute-start | bytes 786440 | tf_op jit(solution)/shard_map/ppermute | solution.py:48
  72.8 26.5 %collective-permute-start.29 = (bf16[128,1792]{1,0:T(8,128)(2,1)S(1)}, bf16[128,1792]{1,0:T(8,128)(2,1)S(1)}, u32[]{:S(2)}, u32[]{:S(2)}) collective-permute-start(bf16[128,1792]{1,0:T(8,128)(2,1)S(1)} %slice.558), channel_id=1, source_target_pairs={{0,2},{1,5},{2,0},{3,7},{4,6},{5,1},{6,4},{7,3},{8,10},{9,13},{10,... | collective-permute-start | bytes 1376264 | tf_op jit(solution)/shard_map/ppermute | solution.py:38
  76.1 12.6 %collective-permute-start.14 = (bf16[128,1792]{1,0:T(8,128)(2,1)S(1)}, bf16[128,1792]{1,0:T(8,128)(2,1)S(1)}, u32[]{:S(2)}, u32[]{:S(2)}) collective-permute-start(bf16[128,1792]{1,0:T(8,128)(2,1)S(1)} %slice.560), channel_id=1, source_target_pairs={{0,2},{1,5},{2,0},{3,7},{4,6},{5,1},{6,4},{7,3},{8,10},{9,13},{10,... | collective-permute-start | bytes 1376264 | tf_op jit(solution)/shard_map/ppermute | solution.py:38
  80.5 15.6 %collective-permute-start.22 = (bf16[128,1792]{1,0:T(8,128)(2,1)S(1)}, bf16[128,1792]{1,0:T(8,128)(2,1)S(1)}, u32[]{:S(2)}, u32[]{:S(2)}) collective-permute-start(bf16[128,1792]{1,0:T(8,128)(2,1)S(1)} %slice.559), channel_id=1, source_target_pairs={{0,2},{1,5},{2,0},{3,7},{4,6},{5,1},{6,4},{7,3},{8,10},{9,13},{10,... | collective-permute-start | bytes 1376264 | tf_op jit(solution)/shard_map/ppermute | solution.py:38
  81.2 8.6 %collective-permute-start.7 = (bf16[64,1792]{1,0:T(8,128)(2,1)S(1)}, bf16[64,1792]{1,0:T(8,128)(2,1)S(1)}, u32[]{:S(2)}, u32[]{:S(2)}) collective-permute-start(bf16[64,1792]{1,0:T(8,128)(2,1)S(1)} %bitcast.70), channel_id=1, source_target_pairs={{0,4},{1,3},{2,6},{3,1},{4,0},{5,7},{6,2},{7,5},{8,12},{9,11},{10,... | collective-permute-start | bytes 688136 | tf_op jit(solution)/shard_map/ppermute | solution.py:42
  88.8 7.9 %collective-permute-start.15 = (bf16[64,1792]{1,0:T(8,128)(2,1)S(1)}, bf16[64,1792]{1,0:T(8,128)(2,1)S(1)}, u32[]{:S(2)}, u32[]{:S(2)}) collective-permute-start(bf16[64,1792]{1,0:T(8,128)(2,1)S(1)} %bitcast.68), channel_id=1, source_target_pairs={{0,4},{1,3},{2,6},{3,1},{4,0},{5,7},{6,2},{7,5},{8,12},{9,11},{10,... | collective-permute-start | bytes 688136 | tf_op jit(solution)/shard_map/ppermute | solution.py:42
  89.8 8.0 %collective-permute-start.8 = (bf16[64,1792]{1,0:T(8,128)(2,1)S(1)}, bf16[64,1792]{1,0:T(8,128)(2,1)S(1)}, u32[]{:S(2)}, u32[]{:S(2)}) collective-permute-start(bf16[64,1792]{1,0:T(8,128)(2,1)S(1)} %fusion.43), channel_id=1, source_target_pairs={{0,8},{2,10},{4,12},{6,14},{8,16},{10,18},{12,20},{14,22},{16,24},... | collective-permute-start | bytes 688136 | tf_op jit(solution)/shard_map/ppermute | solution.py:45
  96.2 6.1 %collective-permute-start.23 = (bf16[64,1792]{1,0:T(8,128)(2,1)S(1)}, bf16[64,1792]{1,0:T(8,128)(2,1)S(1)}, u32[]{:S(2)}, u32[]{:S(2)}) collective-permute-start(bf16[64,1792]{1,0:T(8,128)(2,1)S(1)} %bitcast.67), channel_id=1, source_target_pairs={{0,4},{1,3},{2,6},{3,1},{4,0},{5,7},{6,2},{7,5},{8,12},{9,11},{10,... | collective-permute-start | bytes 688136 | tf_op jit(solution)/shard_map/ppermute | solution.py:42
  97.9 7.9 %collective-permute-start.16 = (bf16[64,1792]{1,0:T(8,128)(2,1)S(1)}, bf16[64,1792]{1,0:T(8,128)(2,1)S(1)}, u32[]{:S(2)}, u32[]{:S(2)}) collective-permute-start(bf16[64,1792]{1,0:T(8,128)(2,1)S(1)} %fusion.42), channel_id=1, source_target_pairs={{0,8},{2,10},{4,12},{6,14},{8,16},{10,18},{12,20},{14,22},{16,24},... | collective-permute-start | bytes 688136 | tf_op jit(solution)/shard_map/ppermute | solution.py:45
  99.4 6.6 %collective-permute-start.30 = (bf16[64,1792]{1,0:T(8,128)(2,1)S(1)}, bf16[64,1792]{1,0:T(8,128)(2,1)S(1)}, u32[]{:S(2)}, u32[]{:S(2)}) collective-permute-start(bf16[64,1792]{1,0:T(8,128)(2,1)S(1)} %bitcast.69), channel_id=1, source_target_pairs={{0,4},{1,3},{2,6},{3,1},{4,0},{5,7},{6,2},{7,5},{8,12},{9,11},{10,... | collective-permute-start | bytes 688136 | tf_op jit(solution)/shard_map/ppermute | solution.py:42
  105.9 7.9 %collective-permute-start.24 = (bf16[64,1792]{1,0:T(8,128)(2,1)S(1)}, bf16[64,1792]{1,0:T(8,128)(2,1)S(1)}, u32[]{:S(2)}, u32[]{:S(2)}) collective-permute-start(bf16[64,1792]{1,0:T(8,128)(2,1)S(1)} %fusion.40), channel_id=1, source_target_pairs={{0,8},{2,10},{4,12},{6,14},{8,16},{10,18},{12,20},{14,22},{16,24},... | collective-permute-start | bytes 688136 | tf_op jit(solution)/shard_map/ppermute | solution.py:45
  113.9 0.7 copy-start.3

commit v2 on v1

v2 whole, which is shorter than its diff:
```python
import functools

import jax
import jax.numpy as jnp
from jax import lax
from jax.experimental import pallas as pl
from jax.experimental.pallas import tpu as pltpu
from jax.sharding import PartitionSpec as P

BF16 = jnp.bfloat16
F32 = jnp.float32
QUAD = 4
LANES = 128
VMEM = pltpu.VMEM


def route_kernel(experts, capacity, aside, core_ref, copied_ref, tokens_ref, scores_ref, ids_ref, block_ref):
    rows, top = scores_ref.shape
    half, width = tokens_ref.shape
    affinity = 1.0 / (1.0 + jnp.exp(-scores_ref[...]))
    gate = 2.5 * affinity / jnp.sum(affinity, axis=1, keepdims=True)
    ids = ids_ref[...]
    lane = lax.broadcasted_iota(jnp.int32, (rows, aside), 1)
    expert = jnp.where(lane < experts, lane, jnp.where(lane < 2 * experts, lane - experts, -1))
    member = jnp.zeros((rows, aside), F32)
    weight = jnp.zeros((rows, aside), F32)
    for k in range(top):
        here = ids[:, k : k + 1] == expert
        member = jnp.where(here, 1.0, member)
        weight = jnp.where(here, gate[:, k : k + 1], weight)
    copied = jnp.zeros((1, aside), jnp.int32)
    for e in range(experts):
        copied = jnp.where(expert[:1] == e, copied_ref[e], copied)
    below = lax.broadcasted_iota(jnp.int32, (rows, rows), 0) > lax.broadcasted_iota(jnp.int32, (rows, rows), 1)
    rank = jnp.dot(below.astype(F32).astype(BF16), member.astype(BF16), preferred_element_type=F32)
    kept = (rank < capacity) | (copied == 1)
    weight = jnp.where(kept, weight, 0.0)
    weight = jnp.where(core_ref[0] == 0, weight[:half], weight[half:])
    high = weight.astype(BF16).astype(F32)
    block_ref[:, :width] = tokens_ref[...]
    block_ref[:, width:] = jnp.where(lane[:half] < experts, high, weight - high).astype(BF16)


def hidden_kernel(experts, me_ref, *refs):
    pieces, (gate_ref, up_ref, hidden_ref, scale_ref) = refs[:4], refs[4:]
    width, units = gate_ref.shape
    n = pieces[0].shape[0]
    x = jnp.concatenate([p[:, :width] for p in pieces], axis=0)
    step = 256 if units % 256 == 0 else units
    for at in range(0, units, step):
        gate = jnp.dot(x, gate_ref[:, at : at + step], preferred_element_type=F32)
        up = jnp.dot(x, up_ref[:, at : at + step], preferred_element_type=F32)
        hidden_ref[:, at : at + step] = (gate / (1.0 + jnp.exp(-gate)) * up).astype(BF16)
    for i, p in enumerate(pieces):
        beside = p[:, width:].astype(F32)
        lane = lax.broadcasted_iota(jnp.int32, beside.shape, 1)
        mine = (lane == me_ref[0]) | (lane == me_ref[0] + experts)
        total = jnp.sum(jnp.where(mine, beside, 0.0), axis=1, keepdims=True)
        scale_ref[i * n : (i + 1) * n, :] = jnp.broadcast_to(total, (n, LANES))


def down_kernel(half, hidden_ref, other_ref, scale_ref, mine_ref, received_ref, kept_ref, sent_ref):
    n = hidden_ref.shape[0] // 2
    share = mine_ref.shape[1]
    hidden = hidden_ref[...]
    other = jnp.concatenate([other_ref[n:, :], other_ref[:n, :]], axis=0)
    scale = scale_ref[:, :1]
    step = 256 if share % 256 == 0 else share
    for at in range(0, share, step):
        y = jnp.dot(hidden, mine_ref[:, at : at + step], preferred_element_type=F32)
        y = y + jnp.dot(other, received_ref[:, at : at + step], preferred_element_type=F32)
        y = y * scale
        for ref, order in ((kept_ref, (0, 2, 4, 5)), (sent_ref, (1, 3, 6, 7))):
            for i, j in enumerate(order):
                ref[i * half : (i + 1) * half, at : at + step] = y[j * half : (j + 1) * half].astype(ref.dtype)


def call(kernel, outs, args, scalars=0, flops=0):
    spaces = [pltpu.SMEM] * scalars + [VMEM] * (len(args) - scalars)
    return pl.pallas_call(
        kernel,
        out_shape=outs,
        in_specs=[pl.BlockSpec(memory_space=s) for s in spaces],
        out_specs=jax.tree.map(lambda _: pl.BlockSpec(memory_space=VMEM), outs),
        compiler_params=pltpu.CompilerParams(vmem_limit_bytes=32 << 20),
        cost_estimate=pl.CostEstimate(flops=flops, bytes_accessed=sum(a.size * a.dtype.itemsize for a in args), transcendentals=0),
    )(*args)


def after(a, *deps):
    return lax.optimization_barrier((a,) + deps)[0]


def body(tokens, scores, expert_ids, copied, w_gate, w_up, w_down):
    ep = lax.axis_size("ep")
    me = lax.axis_index("ep").astype(jnp.int32)[None]
    core = lax.axis_index("tp")
    rows, width = tokens.shape
    top = expert_ids.shape[1]
    units = w_gate.shape[2]
    planes = ep // QUAD
    half = rows // 2
    share = width // 2
    quad_rows = QUAD * rows
    capacity = min(rows * top // ep, rows // 2)
    aside = -(-2 * ep // LANES) * LANES

    def first_link(a):
        pairs = [(2 * e + c, 2 * (e ^ (1 + c)) + c) for e in range(ep) for c in range(2)]
        return lax.ppermute(a, ("ep", "tp"), pairs)

    def second_link(a):
        pairs = [(2 * e + c, 2 * (e ^ (2 - c)) + c) for e in range(ep) for c in range(2)]
        return lax.ppermute(a, ("ep", "tp"), pairs)

    def ring(a):
        return lax.ppermute(a, "ep", [(e, (e + QUAD) % ep) for e in range(ep)])

    def other_core(a):
        return lax.ppermute(a, "tp", [(0, 1), (1, 0)])

    block = pl.pallas_call(
        functools.partial(route_kernel, ep, capacity, aside),
        out_shape=jax.ShapeDtypeStruct((half, width + aside), BF16),
        grid_spec=pltpu.PrefetchScalarGridSpec(
            num_scalar_prefetch=1,
            grid=(1,),
            in_specs=[
                pl.BlockSpec(memory_space=pltpu.SMEM),
                pl.BlockSpec((half, width), lambda i, c: (c[0], 0)),
                pl.BlockSpec((rows, top), lambda i, c: (0, 0)),
                pl.BlockSpec((rows, top), lambda i, c: (0, 0)),
            ],
            out_specs=pl.BlockSpec((half, width + aside), lambda i, c: (0, 0)),
        ),
    )(core.astype(jnp.int32)[None], copied, tokens, scores, expert_ids)

    def experts(pair, far, tpair, tfar):
        hidden, scale = call(
            functools.partial(hidden_kernel, ep),
            (
                jax.ShapeDtypeStruct((quad_rows, units), BF16),
                jax.ShapeDtypeStruct((quad_rows, LANES), F32),
            ),
            (me, pair, far, tpair, tfar, w_gate[0], w_up[0]),
            scalars=1,
            flops=4 * quad_rows * width * units,
        )
        return hidden, scale, other_core(hidden)

    def finish(hidden, scale, other):
        return call(
            functools.partial(down_kernel, half),
            (
                jax.ShapeDtypeStruct((quad_rows // 2, share), F32),
                jax.ShapeDtypeStruct((quad_rows // 2, share), BF16),
            ),
            (hidden, other, scale, down_mine, down_received),
            flops=4 * quad_rows * share * units,
        )

    def scatter(kept, sent):
        got = first_link(sent)
        part = (kept + got.astype(F32)).reshape(2, 2, half, share)
        far = second_link(part[:, 1].reshape(2 * half, share).astype(BF16))
        return part[:, 0].reshape(2 * half, share) + far.astype(F32)

    blocks = [block]
    near = [first_link(block)]
    for _ in range(planes - 1):
        blocks.append(ring(blocks[-1]))
        near.append(None)
    w_down_later = after(w_down[0], near[0])
    down_mine = lax.dynamic_slice_in_dim(w_down_later, core * share, share, 1)
    down_received = other_core(lax.dynamic_slice_in_dim(w_down_later, (1 - core) * share, share, 1))

    outs = []
    for s in range(planes):
        pair = jnp.concatenate([blocks[s], near[s]], axis=0)
        far = second_link(pair)
        if s + 1 < planes:
            nxt = blocks[s + 1]
            if s >= 1:
                nxt = after(nxt, outs[s - 1][1])
            near[s + 1] = first_link(nxt)
        outs.append(finish(*experts(pair, far, other_core(pair), other_core(far))))
    total = None
    for s in list(range(1, planes)) + [0]:
        part = scatter(*outs[s])
        total = part if total is None else ring(total.astype(BF16)).astype(F32) + part
    mine_rows, other_rows = total[:half], total[half:]
    first = jnp.where(core == 0, mine_rows, other_rows)
    second = jnp.where(core == 0, other_rows, mine_rows)
    return jnp.concatenate([first, second], axis=0).astype(BF16)


def solution(mesh):
    in_specs = (
        P(("grp", "ep"), None),
        P(("grp", "ep"), None),
        P(("grp", "ep"), None),
        P("grp"),
        P("ep", None, "tp"),
        P("ep", None, "tp"),
        P("ep", "tp", None),
    )
    out_specs = P(("grp", "ep"), "tp")
    return jax.shard_map(body, mesh=mesh, in_specs=in_specs, out_specs=out_specs, check_vma=False)
```

time: 115 us -> 119 us (1.035)
  Pallas kernels: 0 us -> 23.4 us
  matrix products: 19.6 us -> 0 us
  waiting for transfers between devices: 49.8 us -> 55.7 us
  other arithmetic: 4.84 us -> 0.69 us
  starting transfers between devices: 29.4 us -> 27.4 us
  local copies, waits for them, and re-layouts: 10.1 us -> 11.5 us
    pallas_call x0 -> x9, Pallas kernels: none -> 23.4 us  [the longest x8 21.4 us: call(): pl.pallas_call(kernel, out_shape=outs, in_specs=[pl.BlockSpec(memory_spac...]
    dot_general x13 -> x0, matrix products: 19.6 us -> none  [the longest x4 10.5 us: experts(): return jnp.dot(both, down, preferred_element_type=F32) * scale]
    ppermute x8, waiting for transfers between devices: 10.4 us -> 19.7 us  [second_link(): return lax.ppermute(a, ('ep', 'tp'), pairs)]
    unnamed x56 -> x17, local copies, waits for them, and re-layouts: 4.65 us -> 7.58 us
    ppermute x6, starting transfers between devices: 9.52 us -> 7.51 us  [ring(): return lax.ppermute(a, 'ep', [(e, (e + QUAD) % ep) for e in range(ep)])]
    ppermute x8, starting transfers between devices: 8.56 us -> 6.7 us  [second_link(): return lax.ppermute(a, ('ep', 'tp'), pairs)]
    ppermute x8, waiting for transfers between devices: 26.8 us -> 24.9 us  [first_link(): return lax.ppermute(a, ('ep', 'tp'), pairs)]
    reduce_sum x3 -> x0, other arithmetic: 1.63 us -> none  [the longest x1 0.71 us: route_weights(): gate_weight = 2.5 * affinity / jnp.sum(affinity, axis=1, keepdims=True)]
  transfers between devices with their start and end apart: 31 -> 35, of which waited for: 15 -> 14; matrix products, arithmetic and copies ran while one was open for 22% -> 4% of each run, Pallas kernels for 0% -> 18%
where the time goes in v2:
time: 119 us
  waiting for transfers between devices  55.7 us (47%)
  starting transfers between devices  27.4 us (23%)
  Pallas kernels  23.4 us (20%)
  local copies, waits for them, and re-layouts  11.5 us (10%)
    ppermute x8, waiting for transfers between devices, first_link(): return lax.ppermute(a, ('ep', 'tp'), pairs)  24.9 us
    pallas_call x8, Pallas kernels, call(): pl.pallas_call(kernel, out_shape=outs, in_specs=[pl.BlockSpec(memory_spac...  21.4 us
    ppermute x8, waiting for transfers between devices, second_link(): return lax.ppermute(a, ('ep', 'tp'), pairs)  19.7 us
    ppermute x6, waiting for transfers between devices, ring(): return lax.ppermute(a, 'ep', [(e, (e + QUAD) % ep) for e in range(ep)])  11 us
    ppermute x8, starting transfers between devices, first_link(): return lax.ppermute(a, ('ep', 'tp'), pairs)  10.8 us
    unnamed x17, local copies, waits for them, and re-layouts  7.58 us
    ppermute x6, starting transfers between devices, ring(): return lax.ppermute(a, 'ep', [(e, (e + QUAD) % ep) for e in range(ep)])  7.51 us
    ppermute x8, starting transfers between devices, second_link(): return lax.ppermute(a, ('ep', 'tp'), pairs)  6.7 us
  transfers between devices with their start and end apart: 35, of which 14 were waited for; matrix products, arithmetic and copies ran while one was open for 4% of the time, Pallas kernels for 18%

profile of v2, /device:TPU:0, one launch (start us, length us, event | category | flops | bytes accessed | tf_op | source)
XLA Modules:
  0.0 119.1 jit_solution(15227529152382169897)
XLA Ops:
  0.0 1.4 %copy.8.scores_ref = f32[64,8]{1,0:T(8,128)} copy(f32[64,8]{0,1:T(8,128)} %param.8) | data formatting | bytes 4096 | tf_op args[1]
  1.4 1.4 %copy.9.ids_ref = s32[64,8]{1,0:T(8,128)} copy(s32[64,8]{0,1:T(8,128)} %param.9) | data formatting | bytes 4096 | tf_op args[2]
  2.8 2.0 %shard_map.73 = bf16[32,3712]{1,0:T(8,128)(2,1)} custom-call(s32[1]{0:T(128)} %bitcast.1.core_ref, s32[16]{0:T(128)} %copied_ref.1, bf16[64,3584]{1,0:T(8,128)(2,1)} %tokens_ref.1, f32[64,8]{1,0:T(8,128)} %copy.8.scores_ref, s32[64,8]{1,0:T(8,128)} %copy.9.ids_ref), custom_call_target="tpu_custom_call" | custom-call | tf_op jit(solution)/shard_map/pallas_call | solution.py:122
  4.8 2.9 %collective-permute-start.6 = (bf16[32,3712]{1,0:T(8,128)(2,1)}, bf16[32,3712]{1,0:T(8,128)(2,1)S(1)}, u32[]{:S(2)}, u32[]{:S(2)}) collective-permute-start(bf16[32,3712]{1,0:T(8,128)(2,1)} %shard_map.73), channel_id=1, source_target_pairs={{0,2},{1,5},{2,0},{3,7},{4,6},{5,1},{6,4},{7,3},{8,10},{9,13},{10,... | collective-permute-start | bytes 712712 | tf_op jit(solution)/shard_map/ppermute | solution.py:110
  7.7 1.6 %collective-permute-start = (bf16[32,3712]{1,0:T(8,128)(2,1)}, bf16[32,3712]{1,0:T(8,128)(2,1)S(1)}, u32[]{:S(2)}, u32[]{:S(2)}) collective-permute-start(bf16[32,3712]{1,0:T(8,128)(2,1)} %shard_map.73), channel_id=1, source_target_pairs={{0,8},{2,10},{4,12},{6,14},{8,16},{10,18},{12,20},{14,22},{16,24},... | collective-permute-start | bytes 712712 | tf_op jit(solution)/shard_map/ppermute | solution.py:117
  9.3 2.7 %collective-permute-done.6 = bf16[32,3712]{1,0:T(8,128)(2,1)S(1)} collective-permute-done((bf16[32,3712]{1,0:T(8,128)(2,1)}, bf16[32,3712]{1,0:T(8,128)(2,1)S(1)}, u32[]{:S(2)}, u32[]{:S(2)}) %collective-permute-start.6) | collective-permute-done | bytes 237600 | tf_op jit(solution)/shard_map/ppermute | solution.py:110
  12.0 3.6 %constant_dynamic-slice_fusion = (bf16[512,1792]{1,0:T(8,128)(2,1)}, bf16[512,1792]{1,0:T(8,128)(2,1)S(1)}) fusion(bf16[512,3584]{1,0:T(8,128)(2,1)} %bitcast.41, s32[]{:T(128)S(6)} %select_n.20, s32[]{:T(128)S(6)} %select_n.19), kind=kLoop, calls=%fused_computation.28 | loop fusion | bytes 7340040 | tf_op jit(solution)/shard_map/dynamic_slice | solution.py:175
  15.7 2.1 %collective-permute-start.12 = (bf16[64,3712]{1,0:T(8,128)(2,1)S(1)}, bf16[64,3712]{1,0:T(8,128)(2,1)}, u32[]{:S(2)}, u32[]{:S(2)}) collective-permute-start(bf16[64,3712]{1,0:T(8,128)(2,1)S(1)} %pad_maximum_fusion.refs_0_), channel_id=1, source_target_pairs={{0,4},{1,3},{2,6},{3,1},{4,0},{5,7},{6,2},{7,5},{8,12},{9,11},{10,... | collective-permute-start | bytes 1425416 | tf_op jit(solution)/shard_map/ppermute | solution.py:114
  17.8 1.5 %collective-permute-start.1 = (bf16[32,3712]{1,0:T(8,128)(2,1)S(1)}, bf16[32,3712]{1,0:T(8,128)(2,1)S(1)}, u32[]{:S(2)}, u32[]{:S(2)}) collective-permute-start(bf16[32,3712]{1,0:T(8,128)(2,1)S(1)} %collective-permute-done), channel_id=1, source_target_pairs={{0,2},{1,5},{2,0},{3,7},{4,6},{5,1},{6,4},{7,3},{8,10},{9,13},{10,... | collective-permute-start | bytes 712712 | tf_op jit(solution)/shard_map/ppermute | solution.py:110
  19.3 7.2 %collective-permute-done.1 = bf16[32,3712]{1,0:T(8,128)(2,1)S(1)} collective-permute-done((bf16[32,3712]{1,0:T(8,128)(2,1)S(1)}, bf16[32,3712]{1,0:T(8,128)(2,1)S(1)}, u32[]{:S(2)}, u32[]{:S(2)}) %collective-permute-start.1) | collective-permute-done | bytes 237600 | tf_op jit(solution)/shard_map/ppermute | solution.py:110
  26.6 0.1 collective-permute-start.13
  26.7 0.4 collective-permute-done.12.refs_1_
  27.1 0.1 collective-permute-start.14
  27.2 0.4 collective-permute-start.3
  27.6 7.7 %collective-permute-done.2.refs_1_ = bf16[64,3712]{1,0:T(8,128)(2,1)S(1)} collective-permute-done((bf16[64,3712]{1,0:T(8,128)(2,1)S(1)}, bf16[64,3712]{1,0:T(8,128)(2,1)S(1)}, u32[]{:S(2)}, u32[]{:S(2)}) %collective-permute-start.2) | collective-permute-done | bytes 475168 | tf_op jit(solution)/shard_map/ppermute | solution.py:114
  35.3 1.6 %collective-permute-start.11 = (bf16[32,3712]{1,0:T(8,128)(2,1)S(1)}, bf16[32,3712]{1,0:T(8,128)(2,1)S(1)}, u32[]{:S(2)}, u32[]{:S(2)}) collective-permute-start(bf16[32,3712]{1,0:T(8,128)(2,1)S(1)} %collective-permute-done), channel_id=1, source_target_pairs={{0,8},{2,10},{4,12},{6,14},{8,16},{10,18},{12,20},{14,22},{16,24},... | collective-permute-start | bytes 712712 | tf_op jit(solution)/shard_map/ppermute | solution.py:117
  36.9 2.0 %copy-done = bf16[1,3584,512]{2,1,0:T(8,128)(2,1)S(1)} copy-done((bf16[1,3584,512]{2,1,0:T(8,128)(2,1)S(1)}, bf16[1,3584,512]{2,1,0:T(8,128)(2,1)}, u32[]{:S(2)}) %copy-start) | copy-done | bytes 3670040
  38.9 2.0 %copy-done.2 = bf16[1,3584,512]{2,1,0:T(8,128)(2,1)S(1)} copy-done((bf16[1,3584,512]{2,1,0:T(8,128)(2,1)S(1)}, bf16[1,3584,512]{2,1,0:T(8,128)(2,1)}, u32[]{:S(2)}) %copy-start.2) | copy-done | bytes 3670040
  40.9 3.5 %shard_map.76 = (bf16[256,512]{1,0:T(8,128)(2,1)S(1)}, f32[256,128]{1,0:T(8,128)S(1)}) custom-call(s32[1]{0:T(128)} %bitcast.me_ref, bf16[64,3712]{1,0:T(8,128)(2,1)S(1)} %pad_maximum_fusion.refs_0_, bf16[64,3712]{1,0:T(8,128)(2,1)} %collective-permute-done.12.refs_1_, bf16[64,3712]{1,0:T(8,128)(2,1)} %collective-permute-done.13.refs_2_, ...), custom_call_target="tpu_custom_call" | custom-call | flops 1879048192 | bytes 9240580 | tf_op jit(solution)/shard_map/pallas_call | solution.py:80
  44.5 0.3 collective-permute-start.15
  44.8 0.6 collective-permute-done.11
  45.3 1.0 collective-permute-start.24
  46.4 3.2 %shard_map.74 = (bf16[256,512]{1,0:T(8,128)(2,1)S(1)}, f32[256,128]{1,0:T(8,128)S(1)}) custom-call(s32[1]{0:T(128)} %bitcast.me_ref, bf16[64,3712]{1,0:T(8,128)(2,1)S(1)} %constant_dynamic-update-slice_fusion.refs_0_, bf16[64,3712]{1,0:T(8,128)(2,1)S(1)} %collective-permute-done.2.refs_1_, bf16[64,3712]{1,0:T(8,128)(2,1)} %collective-permute-done.3.refs_2_, ...), custom_call_target="tpu_custom_call" | custom-call | flops 1879048192 | bytes 9240580 | tf_op jit(solution)/shard_map/pallas_call | solution.py:80
  49.6 0.1 collective-permute-start.5
  49.7 2.6 %shard_map.77 = (f32[128,1792]{1,0:T(8,128)S(1)}, bf16[128,1792]{1,0:T(8,128)(2,1)S(1)}) custom-call(bf16[256,512]{1,0:T(8,128)(2,1)S(1)} %get-tuple-element.29.hidden_ref, bf16[256,512]{1,0:T(8,128)(2,1)S(1)} %collective-permute-done.15.other_ref, f32[256,128]{1,0:T(8,128)S(1)} %get-tuple-element.30.scale_ref, ...), custom_call_target="tpu_custom_call" | custom-call | flops 939524096 | bytes 4325376 | tf_op jit(solution)/shard_map/pallas_call | solution.py:80
  52.4 1.6 %collective-permute-start.16 = (bf16[32,3712]{1,0:T(8,128)(2,1)S(1)}, bf16[32,3712]{1,0:T(8,128)(2,1)S(1)}, u32[]{:S(2)}, u32[]{:S(2)}) collective-permute-start(bf16[32,3712]{1,0:T(8,128)(2,1)S(1)} %collective-permute-done.11), channel_id=1, source_target_pairs={{0,2},{1,5},{2,0},{3,7},{4,6},{5,1},{6,4},{7,3},{8,10},{9,13},{10,... | collective-permute-start | bytes 712712 | tf_op jit(solution)/shard_map/ppermute | solution.py:110
  53.9 2.6 %shard_map.75 = (f32[128,1792]{1,0:T(8,128)S(1)}, bf16[128,1792]{1,0:T(8,128)(2,1)S(1)}) custom-call(bf16[256,512]{1,0:T(8,128)(2,1)S(1)} %get-tuple-element.24.hidden_ref, bf16[256,512]{1,0:T(8,128)(2,1)S(1)} %collective-permute-done.5.other_ref, f32[256,128]{1,0:T(8,128)S(1)} %get-tuple-element.25.scale_ref, ...), custom_call_target="tpu_custom_call" | custom-call | flops 939524096 | bytes 4325376 | tf_op jit(solution)/shard_map/pallas_call | solution.py:80
  56.6 0.6 collective-permute-start.25
  57.2 1.4 %collective-permute-done.16 = bf16[32,3712]{1,0:T(8,128)(2,1)S(1)} collective-permute-done((bf16[32,3712]{1,0:T(8,128)(2,1)S(1)}, bf16[32,3712]{1,0:T(8,128)(2,1)S(1)}, u32[]{:S(2)}, u32[]{:S(2)}) %collective-permute-start.16) | collective-permute-done | bytes 237600 | tf_op jit(solution)/shard_map/ppermute | solution.py:110
  58.5 0.5 collective-permute-start.17
  59.1 0.5 collective-permute-start.18
  59.5 5.2 %collective-permute-done.25 = bf16[32,3712]{1,0:T(8,128)(2,1)S(1)} collective-permute-done((bf16[32,3712]{1,0:T(8,128)(2,1)S(1)}, bf16[32,3712]{1,0:T(8,128)(2,1)S(1)}, u32[]{:S(2)}, u32[]{:S(2)}) %collective-permute-start.25) | collective-permute-done | bytes 237600 | tf_op jit(solution)/shard_map/ppermute | solution.py:110
  64.7 0.5 collective-permute-start.26
  65.2 2.0 %collective-permute-done.17.refs_1_ = bf16[64,3712]{1,0:T(8,128)(2,1)S(1)} collective-permute-done((bf16[64,3712]{1,0:T(8,128)(2,1)S(1)}, bf16[64,3712]{1,0:T(8,128)(2,1)S(1)}, u32[]{:S(2)}, u32[]{:S(2)}) %collective-permute-start.17) | collective-permute-done | bytes 475168 | tf_op jit(solution)/shard_map/ppermute | solution.py:114
  67.3 0.4 collective-permute-start.19
  67.7 1.1 collective-permute-start.8
  68.8 0.9 collective-permute-start.33
  69.7 6.8 %collective-permute-done.26.refs_1_ = bf16[64,3712]{1,0:T(8,128)(2,1)S(1)} collective-permute-done((bf16[64,3712]{1,0:T(8,128)(2,1)S(1)}, bf16[64,3712]{1,0:T(8,128)(2,1)S(1)}, u32[]{:S(2)}, u32[]{:S(2)}) %collective-permute-start.26) | collective-permute-done | bytes 475168 | tf_op jit(solution)/shard_map/ppermute | solution.py:114
  76.5 2.1 %shard_map.78 = (bf16[256,512]{1,0:T(8,128)(2,1)S(1)}, f32[256,128]{1,0:T(8,128)S(1)}) custom-call(s32[1]{0:T(128)} %bitcast.me_ref, bf16[64,3712]{1,0:T(8,128)(2,1)S(1)} %constant_dynamic-update-slice_fusion.2.refs_0_, bf16[64,3712]{1,0:T(8,128)(2,1)S(1)} %collective-permute-done.17.refs_1_, bf16[64,3712]{1,0:T(8,128)(2,1)S(1)} %collective-permute-done.18.refs_2_, ...), custom_call_target="tpu_custom_call" | custom-call | flops 1879048192 | bytes 9240580 | tf_op jit(solution)/shard_map/pallas_call | solution.py:80
  78.6 0.6 collective-permute-start.20
  79.1 0.1 convert_add_fusion.3
  79.3 0.5 collective-permute-start.9
  79.8 2.1 %shard_map.80 = (bf16[256,512]{1,0:T(8,128)(2,1)S(1)}, f32[256,128]{1,0:T(8,128)S(1)}) custom-call(s32[1]{0:T(128)} %bitcast.me_ref, bf16[64,3712]{1,0:T(8,128)(2,1)S(1)} %constant_dynamic-update-slice_fusion.4.refs_0_, bf16[64,3712]{1,0:T(8,128)(2,1)S(1)} %collective-permute-done.26.refs_1_, bf16[64,3712]{1,0:T(8,128)(2,1)S(1)} %collective-permute-done.27.refs_2_, ...), custom_call_target="tpu_custom_call" | custom-call | flops 1879048192 | bytes 9240580 | tf_op jit(solution)/shard_map/pallas_call | solution.py:80
  81.9 0.1 collective-permute-start.29
  82.0 2.6 %shard_map.79 = (f32[128,1792]{1,0:T(8,128)S(1)}, bf16[128,1792]{1,0:T(8,128)(2,1)S(1)}) custom-call(bf16[256,512]{1,0:T(8,128)(2,1)S(1)} %get-tuple-element.33.hidden_ref, bf16[256,512]{1,0:T(8,128)(2,1)S(1)} %collective-permute-done.20.other_ref, f32[256,128]{1,0:T(8,128)S(1)} %get-tuple-element.34.scale_ref, ...), custom_call_target="tpu_custom_call" | custom-call | flops 939524096 | bytes 4325376 | tf_op jit(solution)/shard_map/pallas_call | solution.py:80
  84.6 1.4 %collective-permute-start.21 = (bf16[128,1792]{1,0:T(8,128)(2,1)S(1)}, bf16[128,1792]{1,0:T(8,128)(2,1)S(1)}, u32[]{:S(2)}, u32[]{:S(2)}) collective-permute-start(bf16[128,1792]{1,0:T(8,128)(2,1)S(1)} %get-tuple-element.36), channel_id=1, source_target_pairs={{0,2},{1,5},{2,0},{3,7},{4,6},{5,1},{6,4},{7,3},{8,10},{9,13},{10,... | collective-permute-start | bytes 1376264 | tf_op jit(solution)/shard_map/ppermute | solution.py:110
  86.1 1.6 %collective-permute-start.10 = (bf16[64,1792]{1,0:T(8,128)(2,1)S(1)}, bf16[64,1792]{1,0:T(8,128)(2,1)S(1)}, u32[]{:S(2)}, u32[]{:S(2)}) collective-permute-start(bf16[64,1792]{1,0:T(8,128)(2,1)S(1)} %fusion.5), channel_id=1, source_target_pairs={{0,8},{2,10},{4,12},{6,14},{8,16},{10,18},{12,20},{14,22},{16,24},... | collective-permute-start | bytes 688136 | tf_op jit(solution)/shard_map/ppermute | solution.py:117
  87.7 2.6 %shard_map.81 = (f32[128,1792]{1,0:T(8,128)S(1)}, bf16[128,1792]{1,0:T(8,128)(2,1)S(1)}) custom-call(bf16[256,512]{1,0:T(8,128)(2,1)S(1)} %get-tuple-element.38.hidden_ref, bf16[256,512]{1,0:T(8,128)(2,1)S(1)} %collective-permute-done.29.other_ref, f32[256,128]{1,0:T(8,128)S(1)} %get-tuple-element.39.scale_ref, ...), custom_call_target="tpu_custom_call" | custom-call | flops 939524096 | bytes 4325376 | tf_op jit(solution)/shard_map/pallas_call | solution.py:80
  90.3 0.8 collective-permute-start.30
  91.1 2.1 %collective-permute-done.21 = bf16[128,1792]{1,0:T(8,128)(2,1)S(1)} collective-permute-done((bf16[128,1792]{1,0:T(8,128)(2,1)S(1)}, bf16[128,1792]{1,0:T(8,128)(2,1)S(1)}, u32[]{:S(2)}, u32[]{:S(2)}) %collective-permute-start.21) | collective-permute-done | bytes 458784 | tf_op jit(solution)/shard_map/ppermute | solution.py:110
  93.2 0.1 convert_add_fusion.2
  93.3 1.7 %collective-permute-start.22 = (bf16[64,1792]{1,0:T(8,128)(2,1)S(1)}, bf16[64,1792]{1,0:T(8,128)(2,1)S(1)}, u32[]{:S(2)}, u32[]{:S(2)}) collective-permute-start(bf16[64,1792]{1,0:T(8,128)(2,1)S(1)} %bitcast.53), channel_id=1, source_target_pairs={{0,4},{1,3},{2,6},{3,1},{4,0},{5,7},{6,2},{7,5},{8,12},{9,11},{10,... | collective-permute-start | bytes 688136 | tf_op jit(solution)/shard_map/ppermute | solution.py:114
  94.9 6.4 %collective-permute-done.30 = bf16[128,1792]{1,0:T(8,128)(2,1)S(1)} collective-permute-done((bf16[128,1792]{1,0:T(8,128)(2,1)S(1)}, bf16[128,1792]{1,0:T(8,128)(2,1)S(1)}, u32[]{:S(2)}, u32[]{:S(2)}) %collective-permute-start.30) | collective-permute-done | bytes 458784 | tf_op jit(solution)/shard_map/ppermute | solution.py:110
  101.3 0.1 convert_add_fusion.1
  101.5 0.9 collective-permute-start.31
  102.3 0.1 fusion.4
  102.4 1.6 %collective-permute-start.23 = (bf16[64,1792]{1,0:T(8,128)(2,1)S(1)}, bf16[64,1792]{1,0:T(8,128)(2,1)S(1)}, u32[]{:S(2)}, u32[]{:S(2)}) collective-permute-start(bf16[64,1792]{1,0:T(8,128)(2,1)S(1)} %fusion.4), channel_id=1, source_target_pairs={{0,8},{2,10},{4,12},{6,14},{8,16},{10,18},{12,20},{14,22},{16,24},... | collective-permute-start | bytes 688136 | tf_op jit(solution)/shard_map/ppermute | solution.py:117
  104.1 0.1 convert_add_fusion
  104.2 0.5 collective-permute-start.34
  104.7 2.8 %collective-permute-done.31 = bf16[64,1792]{1,0:T(8,128)(2,1)S(1)} collective-permute-done((bf16[64,1792]{1,0:T(8,128)(2,1)S(1)}, bf16[64,1792]{1,0:T(8,128)(2,1)S(1)}, u32[]{:S(2)}, u32[]{:S(2)}) %collective-permute-start.31) | collective-permute-done | bytes 229408 | tf_op jit(solution)/shard_map/ppermute | solution.py:114
  107.6 2.7 %collective-permute-done.23 = bf16[64,1792]{1,0:T(8,128)(2,1)S(1)} collective-permute-done((bf16[64,1792]{1,0:T(8,128)(2,1)S(1)}, bf16[64,1792]{1,0:T(8,128)(2,1)S(1)}, u32[]{:S(2)}, u32[]{:S(2)}) %collective-permute-start.23) | collective-permute-done | bytes 229408 | tf_op jit(solution)/shard_map/ppermute | solution.py:117
  110.3 0.1 fusion.2
  110.5 7.7 %collective-permute-done.32 = bf16[64,1792]{1,0:T(8,128)(2,1)S(1)} collective-permute-done((bf16[64,1792]{1,0:T(8,128)(2,1)S(1)}, bf16[64,1792]{1,0:T(8,128)(2,1)S(1)}, u32[]{:S(2)}, u32[]{:S(2)}) %collective-permute-start.32) | collective-permute-done | bytes 229408 | tf_op jit(solution)/shard_map/ppermute | solution.py:117
  118.4 0.7 copy-done.5
  (55 shorter events, 0.8 us)
Async XLA Ops:
  4.8 7.2 %collective-permute-start.6 = (bf16[32,3712]{1,0:T(8,128)(2,1)}, bf16[32,3712]{1,0:T(8,128)(2,1)S(1)}, u32[]{:S(2)}, u32[]{:S(2)}) collective-permute-start(bf16[32,3712]{1,0:T(8,128)(2,1)} %shard_map.73), channel_id=1, source_target_pairs={{0,2},{1,5},{2,0},{3,7},{4,6},{5,1},{6,4},{7,3},{8,10},{9,13},{10,... | collective-permute-start | bytes 712712 | tf_op jit(solution)/shard_map/ppermute | solution.py:110
  7.7 10.1 %collective-permute-start = (bf16[32,3712]{1,0:T(8,128)(2,1)}, bf16[32,3712]{1,0:T(8,128)(2,1)S(1)}, u32[]{:S(2)}, u32[]{:S(2)}) collective-permute-start(bf16[32,3712]{1,0:T(8,128)(2,1)} %shard_map.73), channel_id=1, source_target_pairs={{0,8},{2,10},{4,12},{6,14},{8,16},{10,18},{12,20},{14,22},{16,24},... | collective-permute-start | bytes 712712 | tf_op jit(solution)/shard_map/ppermute | solution.py:117
  12.0 3.6 %copy-start.4 = (bf16[32,3712]{1,0:T(8,128)(2,1)S(1)}, bf16[32,3712]{1,0:T(8,128)(2,1)}, u32[]{:S(2)}) copy-start(bf16[32,3712]{1,0:T(8,128)(2,1)} %shard_map.73) | copy-start | bytes 712708
  15.6 34.1 %collective-permute-start.7 = (bf16[512,1792]{1,0:T(8,128)(2,1)}, bf16[512,1792]{1,0:T(8,128)(2,1)}, u32[]{:S(2)}, u32[]{:S(2)}) collective-permute-start(bf16[512,1792]{1,0:T(8,128)(2,1)} %get-tuple-element.43), channel_id=1, source_target_pairs={{0,1},{1,0},{2,3},{3,2},{4,5},{5,4},{6,7},{7,6},{8,9},{9,8},{10,11... | collective-permute-start | bytes 5505032 | tf_op jit(solution)/shard_map/ppermute | solution.py:120
  15.7 11.4 %collective-permute-start.12 = (bf16[64,3712]{1,0:T(8,128)(2,1)S(1)}, bf16[64,3712]{1,0:T(8,128)(2,1)}, u32[]{:S(2)}, u32[]{:S(2)}) collective-permute-start(bf16[64,3712]{1,0:T(8,128)(2,1)S(1)} %pad_maximum_fusion.refs_0_), channel_id=1, source_target_pairs={{0,4},{1,3},{2,6},{3,1},{4,0},{5,7},{6,2},{7,5},{8,12},{9,11},{10,... | collective-permute-start | bytes 1425416 | tf_op jit(solution)/shard_map/ppermute | solution.py:114
  17.8 8.7 %collective-permute-start.1 = (bf16[32,3712]{1,0:T(8,128)(2,1)S(1)}, bf16[32,3712]{1,0:T(8,128)(2,1)S(1)}, u32[]{:S(2)}, u32[]{:S(2)}) collective-permute-start(bf16[32,3712]{1,0:T(8,128)(2,1)S(1)} %collective-permute-done), channel_id=1, source_target_pairs={{0,2},{1,5},{2,0},{3,7},{4,6},{5,1},{6,4},{7,3},{8,10},{9,13},{10,... | collective-permute-start | bytes 712712 | tf_op jit(solution)/shard_map/ppermute | solution.py:110
  26.5 8.7 %collective-permute-start.2 = (bf16[64,3712]{1,0:T(8,128)(2,1)S(1)}, bf16[64,3712]{1,0:T(8,128)(2,1)S(1)}, u32[]{:S(2)}, u32[]{:S(2)}) collective-permute-start(bf16[64,3712]{1,0:T(8,128)(2,1)S(1)} %constant_dynamic-update-slice_fusion.refs_0_), channel_id=1, source_target_pairs={{0,4},{1,3},{2,6},{3,1},{4,0},{5,7},{6,2},{7,5},{8,12},{9,11},{10,... | collective-permute-start | bytes 1425416 | tf_op jit(solution)/shard_map/ppermute | solution.py:114
  26.6 8.6 %collective-permute-start.13 = (bf16[64,3712]{1,0:T(8,128)(2,1)S(1)}, bf16[64,3712]{1,0:T(8,128)(2,1)}, u32[]{:S(2)}, u32[]{:S(2)}) collective-permute-start(bf16[64,3712]{1,0:T(8,128)(2,1)S(1)} %pad_maximum_fusion.refs_0_), channel_id=1, source_target_pairs={{0,1},{1,0},{2,3},{3,2},{4,5},{5,4},{6,7},{7,6},{8,9},{9,8},{10,11... | collective-permute-start | bytes 1425416 | tf_op jit(solution)/shard_map/ppermute | solution.py:120
  27.1 9.8 %collective-permute-start.14 = (bf16[64,3712]{1,0:T(8,128)(2,1)}, bf16[64,3712]{1,0:T(8,128)(2,1)}, u32[]{:S(2)}, u32[]{:S(2)}) collective-permute-start(bf16[64,3712]{1,0:T(8,128)(2,1)} %collective-permute-done.12.refs_1_), channel_id=1, source_target_pairs={{0,1},{1,0},{2,3},{3,2},{4,5},{5,4},{6,7},{7,6},{8,9},{9,8},{10,11... | collective-permute-start | bytes 1425416 | tf_op jit(solution)/shard_map/ppermute | solution.py:120
  27.2 19.2 %collective-permute-start.3 = (bf16[64,3712]{1,0:T(8,128)(2,1)S(1)}, bf16[64,3712]{1,0:T(8,128)(2,1)}, u32[]{:S(2)}, u32[]{:S(2)}) collective-permute-start(bf16[64,3712]{1,0:T(8,128)(2,1)S(1)} %constant_dynamic-update-slice_fusion.refs_0_), channel_id=1, source_target_pairs={{0,1},{1,0},{2,3},{3,2},{4,5},{5,4},{6,7},{7,6},{8,9},{9,8},{10,11... | collective-permute-start | bytes 1425416 | tf_op jit(solution)/shard_map/ppermute | solution.py:120
  35.3 11.1 %collective-permute-start.4 = (bf16[64,3712]{1,0:T(8,128)(2,1)S(1)}, bf16[64,3712]{1,0:T(8,128)(2,1)}, u32[]{:S(2)}, u32[]{:S(2)}) collective-permute-start(bf16[64,3712]{1,0:T(8,128)(2,1)S(1)} %collective-permute-done.2.refs_1_), channel_id=1, source_target_pairs={{0,1},{1,0},{2,3},{3,2},{4,5},{5,4},{6,7},{7,6},{8,9},{9,8},{10,11... | collective-permute-start | bytes 1425416 | tf_op jit(solution)/shard_map/ppermute | solution.py:120
  35.3 10.1 %collective-permute-start.11 = (bf16[32,3712]{1,0:T(8,128)(2,1)S(1)}, bf16[32,3712]{1,0:T(8,128)(2,1)S(1)}, u32[]{:S(2)}, u32[]{:S(2)}) collective-permute-start(bf16[32,3712]{1,0:T(8,128)(2,1)S(1)} %collective-permute-done), channel_id=1, source_target_pairs={{0,8},{2,10},{4,12},{6,14},{8,16},{10,18},{12,20},{14,22},{16,24},... | collective-permute-start | bytes 712712 | tf_op jit(solution)/shard_map/ppermute | solution.py:117
  36.9 2.0 %copy-start = (bf16[1,3584,512]{2,1,0:T(8,128)(2,1)S(1)}, bf16[1,3584,512]{2,1,0:T(8,128)(2,1)}, u32[]{:S(2)}) copy-start(bf16[1,3584,512]{2,1,0:T(8,128)(2,1)} %param.11) | copy-start | bytes 11010052
  38.9 2.0 %copy-start.2 = (bf16[1,3584,512]{2,1,0:T(8,128)(2,1)S(1)}, bf16[1,3584,512]{2,1,0:T(8,128)(2,1)}, u32[]{:S(2)}) copy-start(bf16[1,3584,512]{2,1,0:T(8,128)(2,1)} %param.12) | copy-start | bytes 11010052
  40.9 5.4 %copy-start.1 = (bf16[1,3584,512]{2,1,0:T(8,128)(2,1)S(1)}, bf16[1,3584,512]{2,1,0:T(8,128)(2,1)}, u32[]{:S(2)}) copy-start(bf16[1,3584,512]{2,1,0:T(8,128)(2,1)} %param.11) | copy-start | bytes 11010052
  40.9 5.4 %copy-start.3 = (bf16[1,3584,512]{2,1,0:T(8,128)(2,1)S(1)}, bf16[1,3584,512]{2,1,0:T(8,128)(2,1)}, u32[]{:S(2)}) copy-start(bf16[1,3584,512]{2,1,0:T(8,128)(2,1)} %param.12) | copy-start | bytes 11010052
  44.5 5.2 %collective-permute-start.15 = (bf16[256,512]{1,0:T(8,128)(2,1)S(1)}, bf16[256,512]{1,0:T(8,128)(2,1)S(1)}, u32[]{:S(2)}, u32[]{:S(2)}) collective-permute-start(bf16[256,512]{1,0:T(8,128)(2,1)S(1)} %get-tuple-element.29.hidden_ref), channel_id=1, source_target_pairs={{0,1},{1,0},{2,3},{3,2},{4,5},{5,4},{6,7},{7,6},{8,9},{9,8},{10,11... | collective-permute-start | bytes 786440 | tf_op jit(solution)/shard_map/ppermute | solution.py:120
  45.3 11.2 %collective-permute-start.24 = (bf16[32,3712]{1,0:T(8,128)(2,1)S(1)}, bf16[32,3712]{1,0:T(8,128)(2,1)S(1)}, u32[]{:S(2)}, u32[]{:S(2)}) collective-permute-start(bf16[32,3712]{1,0:T(8,128)(2,1)S(1)} %collective-permute-done.11), channel_id=1, source_target_pairs={{0,8},{2,10},{4,12},{6,14},{8,16},{10,18},{12,20},{14,22},{16,24},... | collective-permute-start | bytes 712712 | tf_op jit(solution)/shard_map/ppermute | solution.py:117
  49.6 4.3 %collective-permute-start.5 = (bf16[256,512]{1,0:T(8,128)(2,1)S(1)}, bf16[256,512]{1,0:T(8,128)(2,1)S(1)}, u32[]{:S(2)}, u32[]{:S(2)}) collective-permute-start(bf16[256,512]{1,0:T(8,128)(2,1)S(1)} %get-tuple-element.24.hidden_ref), channel_id=1, source_target_pairs={{0,1},{1,0},{2,3},{3,2},{4,5},{5,4},{6,7},{7,6},{8,9},{9,8},{10,11... | collective-permute-start | bytes 786440 | tf_op jit(solution)/shard_map/ppermute | solution.py:120
  52.4 6.2 %collective-permute-start.16 = (bf16[32,3712]{1,0:T(8,128)(2,1)S(1)}, bf16[32,3712]{1,0:T(8,128)(2,1)S(1)}, u32[]{:S(2)}, u32[]{:S(2)}) collective-permute-start(bf16[32,3712]{1,0:T(8,128)(2,1)S(1)} %collective-permute-done.11), channel_id=1, source_target_pairs={{0,2},{1,5},{2,0},{3,7},{4,6},{5,1},{6,4},{7,3},{8,10},{9,13},{10,... | collective-permute-start | bytes 712712 | tf_op jit(solution)/shard_map/ppermute | solution.py:110
  56.6 8.1 %collective-permute-start.25 = (bf16[32,3712]{1,0:T(8,128)(2,1)S(1)}, bf16[32,3712]{1,0:T(8,128)(2,1)S(1)}, u32[]{:S(2)}, u32[]{:S(2)}) collective-permute-start(bf16[32,3712]{1,0:T(8,128)(2,1)S(1)} %collective-permute-done.24), channel_id=1, source_target_pairs={{0,2},{1,5},{2,0},{3,7},{4,6},{5,1},{6,4},{7,3},{8,10},{9,13},{10,... | collective-permute-start | bytes 712712 | tf_op jit(solution)/shard_map/ppermute | solution.py:110
  58.5 8.7 %collective-permute-start.17 = (bf16[64,3712]{1,0:T(8,128)(2,1)S(1)}, bf16[64,3712]{1,0:T(8,128)(2,1)S(1)}, u32[]{:S(2)}, u32[]{:S(2)}) collective-permute-start(bf16[64,3712]{1,0:T(8,128)(2,1)S(1)} %constant_dynamic-update-slice_fusion.2.refs_0_), channel_id=1, source_target_pairs={{0,4},{1,3},{2,6},{3,1},{4,0},{5,7},{6,2},{7,5},{8,12},{9,11},{10,... | collective-permute-start | bytes 1425416 | tf_op jit(solution)/shard_map/ppermute | solution.py:114
  59.1 10.6 %collective-permute-start.18 = (bf16[64,3712]{1,0:T(8,128)(2,1)S(1)}, bf16[64,3712]{1,0:T(8,128)(2,1)S(1)}, u32[]{:S(2)}, u32[]{:S(2)}) collective-permute-start(bf16[64,3712]{1,0:T(8,128)(2,1)S(1)} %constant_dynamic-update-slice_fusion.2.refs_0_), channel_id=1, source_target_pairs={{0,1},{1,0},{2,3},{3,2},{4,5},{5,4},{6,7},{7,6},{8,9},{9,8},{10,11... | collective-permute-start | bytes 1425416 | tf_op jit(solution)/shard_map/ppermute | solution.py:120
  64.7 11.7 %collective-permute-start.26 = (bf16[64,3712]{1,0:T(8,128)(2,1)S(1)}, bf16[64,3712]{1,0:T(8,128)(2,1)S(1)}, u32[]{:S(2)}, u32[]{:S(2)}) collective-permute-start(bf16[64,3712]{1,0:T(8,128)(2,1)S(1)} %constant_dynamic-update-slice_fusion.4.refs_0_), channel_id=1, source_target_pairs={{0,4},{1,3},{2,6},{3,1},{4,0},{5,7},{6,2},{7,5},{8,12},{9,11},{10,... | collective-permute-start | bytes 1425416 | tf_op jit(solution)/shard_map/ppermute | solution.py:114
  67.3 9.2 %collective-permute-start.19 = (bf16[64,3712]{1,0:T(8,128)(2,1)S(1)}, bf16[64,3712]{1,0:T(8,128)(2,1)S(1)}, u32[]{:S(2)}, u32[]{:S(2)}) collective-permute-start(bf16[64,3712]{1,0:T(8,128)(2,1)S(1)} %collective-permute-done.17.refs_1_), channel_id=1, source_target_pairs={{0,1},{1,0},{2,3},{3,2},{4,5},{5,4},{6,7},{7,6},{8,9},{9,8},{10,11... | collective-permute-start | bytes 1425416 | tf_op jit(solution)/shard_map/ppermute | solution.py:120
  67.7 11.5 %collective-permute-start.8 = (bf16[128,1792]{1,0:T(8,128)(2,1)S(1)}, bf16[128,1792]{1,0:T(8,128)(2,1)S(1)}, u32[]{:S(2)}, u32[]{:S(2)}) collective-permute-start(bf16[128,1792]{1,0:T(8,128)(2,1)S(1)} %get-tuple-element.28), channel_id=1, source_target_pairs={{0,2},{1,5},{2,0},{3,7},{4,6},{5,1},{6,4},{7,3},{8,10},{9,13},{10,... | collective-permute-start | bytes 1376264 | tf_op jit(solution)/shard_map/ppermute | solution.py:110
  68.8 35.3 %collective-permute-start.33 = (bf16[128,1792]{1,0:T(8,128)(2,1)S(1)}, bf16[128,1792]{1,0:T(8,128)(2,1)S(1)}, u32[]{:S(2)}, u32[]{:S(2)}) collective-permute-start(bf16[128,1792]{1,0:T(8,128)(2,1)S(1)} %get-tuple-element.31), channel_id=1, source_target_pairs={{0,2},{1,5},{2,0},{3,7},{4,6},{5,1},{6,4},{7,3},{8,10},{9,13},{10,... | collective-permute-start | bytes 1376264 | tf_op jit(solution)/shard_map/ppermute | solution.py:110
  69.7 10.1 %collective-permute-start.27 = (bf16[64,3712]{1,0:T(8,128)(2,1)S(1)}, bf16[64,3712]{1,0:T(8,128)(2,1)S(1)}, u32[]{:S(2)}, u32[]{:S(2)}) collective-permute-start(bf16[64,3712]{1,0:T(8,128)(2,1)S(1)} %constant_dynamic-update-slice_fusion.4.refs_0_), channel_id=1, source_target_pairs={{0,1},{1,0},{2,3},{3,2},{4,5},{5,4},{6,7},{7,6},{8,9},{9,8},{10,11... | collective-permute-start | bytes 1425416 | tf_op jit(solution)/shard_map/ppermute | solution.py:120
  76.5 3.3 %collective-permute-start.28 = (bf16[64,3712]{1,0:T(8,128)(2,1)S(1)}, bf16[64,3712]{1,0:T(8,128)(2,1)S(1)}, u32[]{:S(2)}, u32[]{:S(2)}) collective-permute-start(bf16[64,3712]{1,0:T(8,128)(2,1)S(1)} %collective-permute-done.26.refs_1_), channel_id=1, source_target_pairs={{0,1},{1,0},{2,3},{3,2},{4,5},{5,4},{6,7},{7,6},{8,9},{9,8},{10,11... | collective-permute-start | bytes 1425416 | tf_op jit(solution)/shard_map/ppermute | solution.py:120
  78.6 3.4 %collective-permute-start.20 = (bf16[256,512]{1,0:T(8,128)(2,1)S(1)}, bf16[256,512]{1,0:T(8,128)(2,1)S(1)}, u32[]{:S(2)}, u32[]{:S(2)}) collective-permute-start(bf16[256,512]{1,0:T(8,128)(2,1)S(1)} %get-tuple-element.33.hidden_ref), channel_id=1, source_target_pairs={{0,1},{1,0},{2,3},{3,2},{4,5},{5,4},{6,7},{7,6},{8,9},{9,8},{10,11... | collective-permute-start | bytes 786440 | tf_op jit(solution)/shard_map/ppermute | solution.py:120
  79.3 6.7 %collective-permute-start.9 = (bf16[64,1792]{1,0:T(8,128)(2,1)S(1)}, bf16[64,1792]{1,0:T(8,128)(2,1)S(1)}, u32[]{:S(2)}, u32[]{:S(2)}) collective-permute-start(bf16[64,1792]{1,0:T(8,128)(2,1)S(1)} %bitcast.50), channel_id=1, source_target_pairs={{0,4},{1,3},{2,6},{3,1},{4,0},{5,7},{6,2},{7,5},{8,12},{9,11},{10,... | collective-permute-start | bytes 688136 | tf_op jit(solution)/shard_map/ppermute | solution.py:114
  81.9 5.8 %collective-permute-start.29 = (bf16[256,512]{1,0:T(8,128)(2,1)S(1)}, bf16[256,512]{1,0:T(8,128)(2,1)S(1)}, u32[]{:S(2)}, u32[]{:S(2)}) collective-permute-start(bf16[256,512]{1,0:T(8,128)(2,1)S(1)} %get-tuple-element.38.hidden_ref), channel_id=1, source_target_pairs={{0,1},{1,0},{2,3},{3,2},{4,5},{5,4},{6,7},{7,6},{8,9},{9,8},{10,11... | collective-permute-start | bytes 786440 | tf_op jit(solution)/shard_map/ppermute | solution.py:120
  84.6 8.5 %collective-permute-start.21 = (bf16[128,1792]{1,0:T(8,128)(2,1)S(1)}, bf16[128,1792]{1,0:T(8,128)(2,1)S(1)}, u32[]{:S(2)}, u32[]{:S(2)}) collective-permute-start(bf16[128,1792]{1,0:T(8,128)(2,1)S(1)} %get-tuple-element.36), channel_id=1, source_target_pairs={{0,2},{1,5},{2,0},{3,7},{4,6},{5,1},{6,4},{7,3},{8,10},{9,13},{10,... | collective-permute-start | bytes 1376264 | tf_op jit(solution)/shard_map/ppermute | solution.py:110
  86.1 16.3 %collective-permute-start.10 = (bf16[64,1792]{1,0:T(8,128)(2,1)S(1)}, bf16[64,1792]{1,0:T(8,128)(2,1)S(1)}, u32[]{:S(2)}, u32[]{:S(2)}) collective-permute-start(bf16[64,1792]{1,0:T(8,128)(2,1)S(1)} %fusion.5), channel_id=1, source_target_pairs={{0,8},{2,10},{4,12},{6,14},{8,16},{10,18},{12,20},{14,22},{16,24},... | collective-permute-start | bytes 688136 | tf_op jit(solution)/shard_map/ppermute | solution.py:117
  90.3 11.0 %collective-permute-start.30 = (bf16[128,1792]{1,0:T(8,128)(2,1)S(1)}, bf16[128,1792]{1,0:T(8,128)(2,1)S(1)}, u32[]{:S(2)}, u32[]{:S(2)}) collective-permute-start(bf16[128,1792]{1,0:T(8,128)(2,1)S(1)} %get-tuple-element.41), channel_id=1, source_target_pairs={{0,2},{1,5},{2,0},{3,7},{4,6},{5,1},{6,4},{7,3},{8,10},{9,13},{10,... | collective-permute-start | bytes 1376264 | tf_op jit(solution)/shard_map/ppermute | solution.py:110
  93.3 9.1 %collective-permute-start.22 = (bf16[64,1792]{1,0:T(8,128)(2,1)S(1)}, bf16[64,1792]{1,0:T(8,128)(2,1)S(1)}, u32[]{:S(2)}, u32[]{:S(2)}) collective-permute-start(bf16[64,1792]{1,0:T(8,128)(2,1)S(1)} %bitcast.53), channel_id=1, source_target_pairs={{0,4},{1,3},{2,6},{3,1},{4,0},{5,7},{6,2},{7,5},{8,12},{9,11},{10,... | collective-permute-start | bytes 688136 | tf_op jit(solution)/shard_map/ppermute | solution.py:114
  101.5 6.1 %collective-permute-start.31 = (bf16[64,1792]{1,0:T(8,128)(2,1)S(1)}, bf16[64,1792]{1,0:T(8,128)(2,1)S(1)}, u32[]{:S(2)}, u32[]{:S(2)}) collective-permute-start(bf16[64,1792]{1,0:T(8,128)(2,1)S(1)} %bitcast.51), channel_id=1, source_target_pairs={{0,4},{1,3},{2,6},{3,1},{4,0},{5,7},{6,2},{7,5},{8,12},{9,11},{10,... | collective-permute-start | bytes 688136 | tf_op jit(solution)/shard_map/ppermute | solution.py:114
  102.4 7.9 %collective-permute-start.23 = (bf16[64,1792]{1,0:T(8,128)(2,1)S(1)}, bf16[64,1792]{1,0:T(8,128)(2,1)S(1)}, u32[]{:S(2)}, u32[]{:S(2)}) collective-permute-start(bf16[64,1792]{1,0:T(8,128)(2,1)S(1)} %fusion.4), channel_id=1, source_target_pairs={{0,8},{2,10},{4,12},{6,14},{8,16},{10,18},{12,20},{14,22},{16,24},... | collective-permute-start | bytes 688136 | tf_op jit(solution)/shard_map/ppermute | solution.py:117
  104.2 6.3 %collective-permute-start.34 = (bf16[64,1792]{1,0:T(8,128)(2,1)S(1)}, bf16[64,1792]{1,0:T(8,128)(2,1)S(1)}, u32[]{:S(2)}, u32[]{:S(2)}) collective-permute-start(bf16[64,1792]{1,0:T(8,128)(2,1)S(1)} %bitcast.52), channel_id=1, source_target_pairs={{0,4},{1,3},{2,6},{3,1},{4,0},{5,7},{6,2},{7,5},{8,12},{9,11},{10,... | collective-permute-start | bytes 688136 | tf_op jit(solution)/shard_map/ppermute | solution.py:114
  110.4 7.9 %collective-permute-start.32 = (bf16[64,1792]{1,0:T(8,128)(2,1)S(1)}, bf16[64,1792]{1,0:T(8,128)(2,1)S(1)}, u32[]{:S(2)}, u32[]{:S(2)}) collective-permute-start(bf16[64,1792]{1,0:T(8,128)(2,1)S(1)} %fusion.2), channel_id=1, source_target_pairs={{0,8},{2,10},{4,12},{6,14},{8,16},{10,18},{12,20},{14,22},{16,24},... | collective-permute-start | bytes 688136 | tf_op jit(solution)/shard_map/ppermute | solution.py:117
  118.4 0.7 copy-start.5

commit v3 on v2

v3 whole, which is shorter than its diff:
```python
import functools

import jax
import jax.numpy as jnp
from jax import lax
from jax.experimental import pallas as pl
from jax.experimental.pallas import tpu as pltpu
from jax.sharding import PartitionSpec as P

BF16 = jnp.bfloat16
F32 = jnp.float32
QUAD = 4
LANES = 128
VMEM = pltpu.VMEM


def route_kernel(experts, capacity, aside, tokens_ref, copied_ref, scores_ref, ids_ref, block_ref, sem):
    top, rows = scores_ref.shape
    half, width = rows // 2, tokens_ref.shape[1]
    core = lax.axis_index("tp")
    copy = pltpu.make_async_copy(
        tokens_ref.at[pl.ds(pl.multiple_of(core * half, half), half), :], block_ref.at[:, :width], sem
    )
    copy.start()
    affinity = 1.0 / (1.0 + jnp.exp(-scores_ref[...]))
    gate = 2.5 * affinity / jnp.sum(affinity, axis=0, keepdims=True)
    ids = ids_ref[...]
    lane = lax.broadcasted_iota(jnp.int32, (aside, rows), 0)
    expert = jnp.where(lane < experts, lane, jnp.where(lane < 2 * experts, lane - experts, -1))
    member = jnp.zeros((aside, rows), F32)
    weight = jnp.zeros((aside, rows), F32)
    for k in range(top):
        here = ids[k : k + 1, :] == expert
        member = jnp.where(here, 1.0, member)
        weight = jnp.where(here, gate[k : k + 1, :], weight)
    copied = jnp.zeros((aside, 1), jnp.int32)
    for e in range(experts):
        copied = jnp.where(expert[:, :1] == e, copied_ref[e], copied)
    above = lax.broadcasted_iota(jnp.int32, (rows, rows), 0) < lax.broadcasted_iota(jnp.int32, (rows, rows), 1)
    rank = jnp.dot(member.astype(BF16), above.astype(F32).astype(BF16), preferred_element_type=F32)
    kept = (rank < capacity) | (copied == 1)
    weight = jnp.where(kept, weight, 0.0)
    high = weight.astype(BF16).astype(F32)
    beside = jnp.where(lane < experts, high, weight - high).T
    beside = jnp.where(core == 0, beside[:half], beside[half:])
    block_ref[:, width:] = beside.astype(BF16)
    copy.wait()


def load_kernel(gate_hbm, up_hbm, down_hbm, gate_ref, up_ref, mine_ref, sent_ref, sems):
    share = mine_ref.shape[1]
    core = lax.axis_index("tp")
    here = pl.multiple_of(core * share, LANES)
    there = pl.multiple_of((1 - core) * share, LANES)
    copies = [
        pltpu.make_async_copy(down_hbm.at[0, :, pl.ds(there, share)], sent_ref, sems.at[0]),
        pltpu.make_async_copy(gate_hbm.at[0], gate_ref, sems.at[1]),
        pltpu.make_async_copy(up_hbm.at[0], up_ref, sems.at[2]),
        pltpu.make_async_copy(down_hbm.at[0, :, pl.ds(here, share)], mine_ref, sems.at[3]),
    ]
    for c in copies:
        c.start()
    for c in copies:
        c.wait()


def hidden_kernel(experts, *refs):
    pieces, (gate_ref, up_ref, hidden_ref, scale_ref) = refs[:4], refs[4:]
    width, units = gate_ref.shape
    me = lax.axis_index("ep")
    n = pieces[0].shape[0]
    x = jnp.concatenate([p[:, :width] for p in pieces], axis=0)
    step = 256 if units % 256 == 0 else units
    for at in range(0, units, step):
        gate = jnp.dot(x, gate_ref[:, at : at + step], preferred_element_type=F32)
        up = jnp.dot(x, up_ref[:, at : at + step], preferred_element_type=F32)
        hidden_ref[:, at : at + step] = (gate / (1.0 + jnp.exp(-gate)) * up).astype(BF16)
    for i, p in enumerate(pieces):
        beside = p[:, width:].astype(F32)
        lane = lax.broadcasted_iota(jnp.int32, beside.shape, 1)
        mine = (lane == me) | (lane == me + experts)
        total = jnp.sum(jnp.where(mine, beside, 0.0), axis=1, keepdims=True)
        scale_ref[i * n : (i + 1) * n, :] = jnp.broadcast_to(total, (n, LANES))


def down_kernel(half, hidden_ref, other_ref, scale_ref, mine_ref, received_ref, kept_ref, sent_ref):
    n = hidden_ref.shape[0] // 2
    share = mine_ref.shape[1]
    hidden = hidden_ref[...]
    other = jnp.concatenate([other_ref[n:, :], other_ref[:n, :]], axis=0)
    scale = scale_ref[:, :1]
    step = 256 if share % 256 == 0 else share
    for at in range(0, share, step):
        y = jnp.dot(hidden, mine_ref[:, at : at + step], preferred_element_type=F32)
        y = y + jnp.dot(other, received_ref[:, at : at + step], preferred_element_type=F32)
        y = y * scale
        for ref, order in ((kept_ref, (0, 2, 4, 5)), (sent_ref, (1, 3, 6, 7))):
            for i, j in enumerate(order):
                ref[i * half : (i + 1) * half, at : at + step] = y[j * half : (j + 1) * half].astype(ref.dtype)


def call(kernel, outs, args, spaces=None, scratch=(), flops=0, limit=32 << 20):
    spaces = spaces or [VMEM] * len(args)
    return pl.pallas_call(
        kernel,
        out_shape=outs,
        in_specs=[pl.BlockSpec(memory_space=s) for s in spaces],
        out_specs=jax.tree.map(lambda _: pl.BlockSpec(memory_space=VMEM), outs),
        scratch_shapes=scratch,
        compiler_params=pltpu.CompilerParams(vmem_limit_bytes=limit),
        cost_estimate=pl.CostEstimate(flops=flops, bytes_accessed=sum(a.size * a.dtype.itemsize for a in args), transcendentals=0),
    )(*args)


def after(a, *deps):
    return lax.optimization_barrier((a,) + deps)[0]


def body(tokens, scores, expert_ids, copied, w_gate, w_up, w_down):
    ep = lax.axis_size("ep")
    core = lax.axis_index("tp")
    rows, width = tokens.shape
    top = expert_ids.shape[1]
    units = w_gate.shape[2]
    planes = ep // QUAD
    half = rows // 2
    share = width // 2
    quad_rows = QUAD * rows
    capacity = min(rows * top // ep, rows // 2)
    aside = -(-2 * ep // LANES) * LANES

    def first_link(a):
        pairs = [(2 * e + c, 2 * (e ^ (1 + c)) + c) for e in range(ep) for c in range(2)]
        return lax.ppermute(a, ("ep", "tp"), pairs)

    def second_link(a):
        pairs = [(2 * e + c, 2 * (e ^ (2 - c)) + c) for e in range(ep) for c in range(2)]
        return lax.ppermute(a, ("ep", "tp"), pairs)

    def ring(a):
        return lax.ppermute(a, "ep", [(e, (e + QUAD) % ep) for e in range(ep)])

    def other_core(a):
        return lax.ppermute(a, "tp", [(0, 1), (1, 0)])

    block = call(
        functools.partial(route_kernel, ep, capacity, aside),
        jax.ShapeDtypeStruct((half, width + aside), BF16),
        (tokens, copied, scores.T, expert_ids.T),
        spaces=[pl.ANY, pltpu.SMEM, VMEM, VMEM],
        scratch=[pltpu.SemaphoreType.DMA],
        limit=None,
    )

    def load(gate, up, down):
        return call(
            load_kernel,
            (
                jax.ShapeDtypeStruct((width, units), BF16),
                jax.ShapeDtypeStruct((width, units), BF16),
                jax.ShapeDtypeStruct((units, share), BF16),
                jax.ShapeDtypeStruct((units, share), BF16),
            ),
            (gate, up, down),
            spaces=[pl.ANY] * 3,
            scratch=[pltpu.SemaphoreType.DMA((4,))],
            limit=41 << 20,
        )

    def experts(pair, far, tpair, tfar):
        hidden, scale = call(
            functools.partial(hidden_kernel, ep),
            (
                jax.ShapeDtypeStruct((quad_rows, units), BF16),
                jax.ShapeDtypeStruct((quad_rows, LANES), F32),
            ),
            (pair, far, tpair, tfar, gate, up),
            flops=4 * quad_rows * width * units,
        )
        return hidden, scale, other_core(hidden)

    def finish(hidden, scale, other):
        return call(
            functools.partial(down_kernel, half),
            (
                jax.ShapeDtypeStruct((quad_rows // 2, share), F32),
                jax.ShapeDtypeStruct((quad_rows // 2, share), BF16),
            ),
            (hidden, other, scale, down_mine, down_received),
            flops=4 * quad_rows * share * units,
        )

    def join(a, b):
        return jnp.concatenate([a, b], axis=0)

    def add_up(p, *ties):
        part = after(sums[p][0], *ties) + gots[p].astype(F32)
        part = part.reshape(2, 2, half, share)
        passes[p] = part[:, 1].reshape(2 * half, share).astype(BF16)
        parts[p] = part[:, 0].reshape(2 * half, share), second_link(passes[p])

    coming = ring(block)
    near = first_link(block)
    gate, up, down_mine, down_sent = load(*lax.optimization_barrier((w_gate, w_up, w_down, block))[:3])
    down_received = other_core(down_sent)
    blocks, pairs, fars = [block, coming], {}, {}
    held, sums, gots, parts, passes = {}, {}, {}, {}, {}
    marks = [down_mine]
    for i in range(planes + 2):
        if i < planes:
            if 1 <= i < planes - 1:
                blocks.append(coming)
                marks.append(coming)
            pairs[i] = join(after(blocks[i], *marks), near)
            fars[i] = second_link(pairs[i])
            marks = [fars[i]]
            if i + 1 < planes:
                if i == 0:
                    blocks[1] = after(coming, pairs[0])
                if i + 2 < planes:
                    coming = ring(blocks[i + 1])
                near = first_link(blocks[i + 1])
        p = i - 1
        if 0 <= p < planes:
            ties = [pairs[i]] if i < planes else []
            ties += [sums[p - 1][1]] if p - 1 in sums else []
            far = after(fars[p], *ties) if ties else fars[p]
            held[p] = experts(pairs[p], far, other_core(pairs[p]), other_core(far))
            marks.append(held[p][0])
        p = i - 2
        if 1 <= p < planes:
            ties = [pairs[i]] if i in pairs else []
            sums[p] = finish(after(held[p][0], *ties) if ties else held[p][0], *held[p][1:])
            gots[p] = first_link(sums[p][1])
            if p > 1:
                add_up(p - 1, sums[p][1])
    add_up(planes - 1)
    sums[0] = finish(after(held[0][0], passes[planes - 1]), *held[0][1:])
    gots[0] = first_link(sums[0][1])
    carried = None
    for p in range(1, planes):
        total = parts[p][0] + parts[p][1].astype(F32)
        passing = (total if carried is None else carried.astype(F32) + total).astype(BF16)
        carried = ring(passing)
    add_up(0, passing)
    total = carried.astype(F32) + parts[0][0] + parts[0][1].astype(F32)
    mine_rows, other_rows = total[:half], total[half:]
    first = jnp.where(core == 0, mine_rows, other_rows)
    second = jnp.where(core == 0, other_rows, mine_rows)
    return jnp.concatenate([first, second], axis=0).astype(BF16)


def solution(mesh):
    in_specs = (
        P(("grp", "ep"), None),
        P(("grp", "ep"), None),
        P(("grp", "ep"), None),
        P("grp"),
        P("ep", None, "tp"),
        P("ep", None, "tp"),
        P("ep", "tp", None),
    )
    out_specs = P(("grp", "ep"), "tp")
    return jax.shard_map(body, mesh=mesh, in_specs=in_specs, out_specs=out_specs, check_vma=False)
```

time: 119 us -> 98.9 us (0.83)
  local copies, waits for them, and re-layouts: 11.5 us -> 1.08 us
  waiting for transfers between devices: 55.7 us -> 50.8 us
  Pallas kernels: 23.4 us -> 19.4 us
    ppermute x8, waiting for transfers between devices: 24.9 us -> 6.3 us  [first_link(): return lax.ppermute(a, ('ep', 'tp'), pairs)]
    ppermute x6, waiting for transfers between devices: 11 us -> 23.3 us  [ring(): return lax.ppermute(a, 'ep', [(e, (e + QUAD) % ep) for e in range(ep)])]
    unnamed x17 -> x8, local copies, waits for them, and re-layouts: 7.58 us -> 0.76 us
    dynamic_slice x1 -> x0, local copies, waits for them, and re-layouts: 3.6 us -> none  [body(): lax.dynamic_slice_in_dim(w_down_later, (1 - core) * share, share, 1)]
    ppermute x6, starting transfers between devices: 7.51 us -> 4.58 us  [ring(): return lax.ppermute(a, 'ep', [(e, (e + QUAD) % ep) for e in range(ep)])]
    ppermute x8, starting transfers between devices: 6.7 us -> 9.05 us  [second_link(): return lax.ppermute(a, ('ep', 'tp'), pairs)]
    pallas_call x8 -> x10, Pallas kernels: 21.4 us -> 19.4 us  [call(): pl.pallas_call(kernel, out_shape=outs, in_specs=[pl.BlockSpec(memory_spac...]
    pallas_call x1 -> x0, Pallas kernels: 2.03 us -> none  [body(): pl.pallas_call(functools.partial(route_kernel, ep, capacity, aside), out_...]
  transfers between devices with their start and end apart: 35 -> 35, of which waited for: 14 -> 17; matrix products, arithmetic and copies ran while one was open for 4% -> 1% of each run, Pallas kernels for 18% -> 17%
where the time goes in v3:
time: 98.9 us; the launch traced here: 98.7 us
  waiting for transfers between devices  50.8 us (51%)
  starting transfers between devices  26.5 us (27%)
  Pallas kernels  19.4 us (20%)
  local copies, waits for them, and re-layouts  1.08 us (1%)
    ppermute x6, waiting for transfers between devices, ring(): return lax.ppermute(a, 'ep', [(e, (e + QUAD) % ep) for e in range(ep)])  23.3 us
    ppermute x8, waiting for transfers between devices, second_link(): return lax.ppermute(a, ('ep', 'tp'), pairs)  20.5 us
    pallas_call x10, Pallas kernels, call(): pl.pallas_call(kernel, out_shape=outs, in_specs=[pl.BlockSpec(memory_spac...  19.4 us
    ppermute x8, starting transfers between devices, first_link(): return lax.ppermute(a, ('ep', 'tp'), pairs)  10.8 us
    ppermute x8, starting transfers between devices, second_link(): return lax.ppermute(a, ('ep', 'tp'), pairs)  9.05 us
    ppermute x8, waiting for transfers between devices, first_link(): return lax.ppermute(a, ('ep', 'tp'), pairs)  6.3 us
    ppermute x6, starting transfers between devices, ring(): return lax.ppermute(a, 'ep', [(e, (e + QUAD) % ep) for e in range(ep)])  4.58 us
    ppermute x13, starting transfers between devices, other_core(): return lax.ppermute(a, 'tp', [(0, 1), (1, 0)])  2.06 us
  transfers between devices with their start and end apart: 35, of which 17 were waited for; matrix products, arithmetic and copies ran while one was open for 1% of the time, Pallas kernels for 17%

profile of v3, /device:TPU:0, one launch (start us, length us, event | category | flops | bytes accessed | tf_op | source)
XLA Modules:
  0.0 98.7 jit_solution(14914001873578565044)
XLA Ops:
  0.0 2.4 %shard_map.73 = bf16[32,3712]{1,0:T(8,128)(2,1)} custom-call(bf16[64,3584]{1,0:T(8,128)(2,1)} %tokens_ref.1, s32[16]{0:T(128)} %copied_ref.1, f32[8,64]{1,0:T(8,128)} %bitcast.42, s32[8,64]{1,0:T(8,128)} %bitcast.43), custom_call_target="tpu_custom_call" | custom-call | bytes 462912 | tf_op jit(solution)/shard_map/pallas_call | solution.py:104
  2.4 3.0 %collective-permute-start.1 = (bf16[32,3712]{1,0:T(8,128)(2,1)}, bf16[32,3712]{1,0:T(8,128)(2,1)S(1)}, u32[]{:S(2)}, u32[]{:S(2)}) collective-permute-start(bf16[32,3712]{1,0:T(8,128)(2,1)} %shard_map.73), channel_id=1, source_target_pairs={{0,2},{1,5},{2,0},{3,7},{4,6},{5,1},{6,4},{7,3},{8,10},{9,13},{10,... | collective-permute-start | bytes 712712 | tf_op jit(solution)/shard_map/ppermute | solution.py:134
  5.4 1.6 %collective-permute-start = (bf16[32,3712]{1,0:T(8,128)(2,1)}, bf16[32,3712]{1,0:T(8,128)(2,1)S(1)}, u32[]{:S(2)}, u32[]{:S(2)}) collective-permute-start(bf16[32,3712]{1,0:T(8,128)(2,1)} %shard_map.73), channel_id=1, source_target_pairs={{0,8},{2,10},{4,12},{6,14},{8,16},{10,18},{12,20},{14,22},{16,24},... | collective-permute-start | bytes 712712 | tf_op jit(solution)/shard_map/ppermute | solution.py:141
  7.0 4.2 %shard_map.74 = (bf16[3584,512]{1,0:T(8,128)(2,1)S(1)}, bf16[3584,512]{1,0:T(8,128)(2,1)S(1)}, bf16[512,1792]{1,0:T(8,128)(2,1)S(1)}, bf16[512,1792]{1,0:T(8,128)(2,1)S(1)}) custom-call(bf16[1,3584,512]{2,1,0:T(8,128)(2,1)} %gate_hbm, bf16[1,3584,512]{2,1,0:T(8,128)(2,1)} %up_hbm, bf16[1,512,3584]{2,1,0:T(8,128)(2,1)} %down_hbm), custom_call_target="tpu_custom_call" | custom-call | bytes 11010048 | tf_op jit(solution)/shard_map/pallas_call | solution.py:104
  11.3 1.6 %collective-permute-start.2 = (bf16[64,3712]{1,0:T(8,128)(2,1)S(1)}, bf16[64,3712]{1,0:T(8,128)(2,1)S(1)}, u32[]{:S(2)}, u32[]{:S(2)}) collective-permute-start(bf16[64,3712]{1,0:T(8,128)(2,1)S(1)} %constant_dynamic-update-slice_fusion.refs_0_), channel_id=1, source_target_pairs={{0,4},{1,3},{2,6},{3,1},{4,0},{5,7},{6,2},{7,5},{8,12},{9,11},{10,... | collective-permute-start | bytes 1425416 | tf_op jit(solution)/shard_map/ppermute | solution.py:138
  12.8 1.9 %collective-permute-done = bf16[32,3712]{1,0:T(8,128)(2,1)S(1)} collective-permute-done((bf16[32,3712]{1,0:T(8,128)(2,1)}, bf16[32,3712]{1,0:T(8,128)(2,1)S(1)}, u32[]{:S(2)}, u32[]{:S(2)}) %collective-permute-start) | collective-permute-done | bytes 237600 | tf_op jit(solution)/shard_map/ppermute | solution.py:141
  14.8 1.5 %collective-permute-start.4 = (bf16[32,3712]{1,0:T(8,128)(2,1)S(1)}, bf16[32,3712]{1,0:T(8,128)(2,1)S(1)}, u32[]{:S(2)}, u32[]{:S(2)}) collective-permute-start(bf16[32,3712]{1,0:T(8,128)(2,1)S(1)} %collective-permute-done), channel_id=1, source_target_pairs={{0,2},{1,5},{2,0},{3,7},{4,6},{5,1},{6,4},{7,3},{8,10},{9,13},{10,... | collective-permute-start | bytes 712712 | tf_op jit(solution)/shard_map/ppermute | solution.py:134
  16.3 6.8 %collective-permute-done.3 = bf16[32,3712]{1,0:T(8,128)(2,1)S(1)} collective-permute-done((bf16[32,3712]{1,0:T(8,128)(2,1)S(1)}, bf16[32,3712]{1,0:T(8,128)(2,1)S(1)}, u32[]{:S(2)}, u32[]{:S(2)}) %collective-permute-start.3) | collective-permute-done | bytes 237600 | tf_op jit(solution)/shard_map/ppermute | solution.py:141
  23.1 0.1 collective-permute-start.7
  23.2 1.1 %collective-permute-start.5 = (bf16[64,3712]{1,0:T(8,128)(2,1)S(1)}, bf16[64,3712]{1,0:T(8,128)(2,1)S(1)}, u32[]{:S(2)}, u32[]{:S(2)}) collective-permute-start(bf16[64,3712]{1,0:T(8,128)(2,1)S(1)} %constant_dynamic-update-slice_fusion.2.refs_0_), channel_id=1, source_target_pairs={{0,4},{1,3},{2,6},{3,1},{4,0},{5,7},{6,2},{7,5},{8,12},{9,11},{10,... | collective-permute-start | bytes 1425416 | tf_op jit(solution)/shard_map/ppermute | solution.py:138
  24.3 1.4 %collective-permute-start.8 = (bf16[32,3712]{1,0:T(8,128)(2,1)S(1)}, bf16[32,3712]{1,0:T(8,128)(2,1)S(1)}, u32[]{:S(2)}, u32[]{:S(2)}) collective-permute-start(bf16[32,3712]{1,0:T(8,128)(2,1)S(1)} %collective-permute-done.3), channel_id=1, source_target_pairs={{0,8},{2,10},{4,12},{6,14},{8,16},{10,18},{12,20},{14,22},{16,24},... | collective-permute-start | bytes 712712 | tf_op jit(solution)/shard_map/ppermute | solution.py:141
  25.7 0.7 collective-permute-start.9
  26.4 2.1 %shard_map.75 = (bf16[256,512]{1,0:T(8,128)(2,1)S(1)}, f32[256,128]{1,0:T(8,128)S(1)}) custom-call(bf16[64,3712]{1,0:T(8,128)(2,1)S(1)} %constant_dynamic-update-slice_fusion.refs_0_, bf16[64,3712]{1,0:T(8,128)(2,1)S(1)} %collective-permute-done.2.refs_1_, bf16[64,3712]{1,0:T(8,128)(2,1)S(1)} %collective-permute-done.6.refs_2_, ...), custom_call_target="tpu_custom_call" | custom-call | flops 1879048192 | bytes 9240576 | tf_op jit(solution)/shard_map/pallas_call | solution.py:104
  28.5 5.4 %collective-permute-done.8 = bf16[32,3712]{1,0:T(8,128)(2,1)S(1)} collective-permute-done((bf16[32,3712]{1,0:T(8,128)(2,1)S(1)}, bf16[32,3712]{1,0:T(8,128)(2,1)S(1)}, u32[]{:S(2)}, u32[]{:S(2)}) %collective-permute-start.8) | collective-permute-done | bytes 237600 | tf_op jit(solution)/shard_map/ppermute | solution.py:141
  33.9 0.5 collective-permute-done.5.refs_1_
  34.5 0.3 collective-permute-start.11
  34.8 0.3 collective-permute-start.15
  35.1 1.0 %collective-permute-start.12 = (bf16[64,3712]{1,0:T(8,128)(2,1)S(1)}, bf16[64,3712]{1,0:T(8,128)(2,1)S(1)}, u32[]{:S(2)}, u32[]{:S(2)}) collective-permute-start(bf16[64,3712]{1,0:T(8,128)(2,1)S(1)} %constant_dynamic-update-slice_fusion.4.refs_0_), channel_id=1, source_target_pairs={{0,4},{1,3},{2,6},{3,1},{4,0},{5,7},{6,2},{7,5},{8,12},{9,11},{10,... | collective-permute-start | bytes 1425416 | tf_op jit(solution)/shard_map/ppermute | solution.py:138
  36.1 1.7 %collective-permute-start.13 = (bf16[32,3712]{1,0:T(8,128)(2,1)S(1)}, bf16[32,3712]{1,0:T(8,128)(2,1)S(1)}, u32[]{:S(2)}, u32[]{:S(2)}) collective-permute-start(bf16[32,3712]{1,0:T(8,128)(2,1)S(1)} %collective-permute-done.8), channel_id=1, source_target_pairs={{0,2},{1,5},{2,0},{3,7},{4,6},{5,1},{6,4},{7,3},{8,10},{9,13},{10,... | collective-permute-start | bytes 712712 | tf_op jit(solution)/shard_map/ppermute | solution.py:134
  37.8 2.1 %shard_map.76 = (bf16[256,512]{1,0:T(8,128)(2,1)S(1)}, f32[256,128]{1,0:T(8,128)S(1)}) custom-call(bf16[64,3712]{1,0:T(8,128)(2,1)S(1)} %constant_dynamic-update-slice_fusion.2.refs_0_, bf16[64,3712]{1,0:T(8,128)(2,1)S(1)} %collective-permute-done.5.refs_1_, bf16[64,3712]{1,0:T(8,128)(2,1)S(1)} %collective-permute-done.10.refs_2_, ...), custom_call_target="tpu_custom_call" | custom-call | flops 1879048192 | bytes 9240576 | tf_op jit(solution)/shard_map/pallas_call | solution.py:104
  39.8 6.4 %collective-permute-done.12.refs_1_ = bf16[64,3712]{1,0:T(8,128)(2,1)S(1)} collective-permute-done((bf16[64,3712]{1,0:T(8,128)(2,1)S(1)}, bf16[64,3712]{1,0:T(8,128)(2,1)S(1)}, u32[]{:S(2)}, u32[]{:S(2)}) %collective-permute-start.12) | collective-permute-done | bytes 475168 | tf_op jit(solution)/shard_map/ppermute | solution.py:138
  46.3 0.1 collective-permute-start.17
  46.4 0.5 collective-permute-start.14
  46.9 1.0 %collective-permute-start.22 = (bf16[64,3712]{1,0:T(8,128)(2,1)S(1)}, bf16[64,3712]{1,0:T(8,128)(2,1)S(1)}, u32[]{:S(2)}, u32[]{:S(2)}) collective-permute-start(bf16[64,3712]{1,0:T(8,128)(2,1)S(1)} %constant_dynamic-update-slice_fusion.6.refs_0_), channel_id=1, source_target_pairs={{0,4},{1,3},{2,6},{3,1},{4,0},{5,7},{6,2},{7,5},{8,12},{9,11},{10,... | collective-permute-start | bytes 1425416 | tf_op jit(solution)/shard_map/ppermute | solution.py:138
  47.9 0.7 collective-permute-done.14.other_ref
  48.6 1.1 %shard_map.77 = (f32[128,1792]{1,0:T(8,128)S(1)}, bf16[128,1792]{1,0:T(8,128)(2,1)S(1)}) custom-call(bf16[256,512]{1,0:T(8,128)(2,1)S(1)} %get-tuple-element.56.hidden_ref, bf16[256,512]{1,0:T(8,128)(2,1)S(1)} %collective-permute-done.14.other_ref, f32[256,128]{1,0:T(8,128)S(1)} %get-tuple-element.57.scale_ref, ...), custom_call_target="tpu_custom_call" | custom-call | flops 939524096 | bytes 4325376 | tf_op jit(solution)/shard_map/pallas_call | solution.py:104
  49.7 1.3 %collective-permute-start.19 = (bf16[128,1792]{1,0:T(8,128)(2,1)S(1)}, bf16[128,1792]{1,0:T(8,128)(2,1)S(1)}, u32[]{:S(2)}, u32[]{:S(2)}) collective-permute-start(bf16[128,1792]{1,0:T(8,128)(2,1)S(1)} %get-tuple-element.65), channel_id=1, source_target_pairs={{0,2},{1,5},{2,0},{3,7},{4,6},{5,1},{6,4},{7,3},{8,10},{9,13},{10,... | collective-permute-start | bytes 1376264 | tf_op jit(solution)/shard_map/ppermute | solution.py:134
  51.1 2.1 %shard_map.78 = (bf16[256,512]{1,0:T(8,128)(2,1)S(1)}, f32[256,128]{1,0:T(8,128)S(1)}) custom-call(bf16[64,3712]{1,0:T(8,128)(2,1)S(1)} %constant_dynamic-update-slice_fusion.4.refs_0_, bf16[64,3712]{1,0:T(8,128)(2,1)S(1)} %collective-permute-done.12.refs_1_, bf16[64,3712]{1,0:T(8,128)(2,1)S(1)} %collective-permute-done.16.refs_2_, ...), custom_call_target="tpu_custom_call" | custom-call | flops 1879048192 | bytes 9240576 | tf_op jit(solution)/shard_map/pallas_call | solution.py:104
  53.2 0.1 collective-permute-start.18
  53.2 0.5 collective-permute-start.23
  53.7 4.8 %collective-permute-done.22.refs_1_ = bf16[64,3712]{1,0:T(8,128)(2,1)S(1)} collective-permute-done((bf16[64,3712]{1,0:T(8,128)(2,1)S(1)}, bf16[64,3712]{1,0:T(8,128)(2,1)S(1)}, u32[]{:S(2)}, u32[]{:S(2)}) %collective-permute-start.22) | collective-permute-done | bytes 475168 | tf_op jit(solution)/shard_map/ppermute | solution.py:138
  58.5 1.1 %shard_map.79 = (f32[128,1792]{1,0:T(8,128)S(1)}, bf16[128,1792]{1,0:T(8,128)(2,1)S(1)}) custom-call(bf16[256,512]{1,0:T(8,128)(2,1)S(1)} %get-tuple-element.61.hidden_ref, bf16[256,512]{1,0:T(8,128)(2,1)S(1)} %collective-permute-done.18.other_ref, f32[256,128]{1,0:T(8,128)S(1)} %get-tuple-element.62.scale_ref, ...), custom_call_target="tpu_custom_call" | custom-call | flops 939524096 | bytes 4325376 | tf_op jit(solution)/shard_map/pallas_call | solution.py:104
  59.7 0.1 convert_add_fusion.3
  59.8 1.1 %collective-permute-start.20 = (bf16[64,1792]{1,0:T(8,128)(2,1)S(1)}, bf16[64,1792]{1,0:T(8,128)(2,1)S(1)}, u32[]{:S(2)}, u32[]{:S(2)}) collective-permute-start(bf16[64,1792]{1,0:T(8,128)(2,1)S(1)} %bitcast.38), channel_id=1, source_target_pairs={{0,4},{1,3},{2,6},{3,1},{4,0},{5,7},{6,2},{7,5},{8,12},{9,11},{10,... | collective-permute-start | bytes 688136 | tf_op jit(solution)/shard_map/ppermute | solution.py:138
  60.9 0.9 collective-permute-start.26
  61.8 2.1 %shard_map.80 = (bf16[256,512]{1,0:T(8,128)(2,1)S(1)}, f32[256,128]{1,0:T(8,128)S(1)}) custom-call(bf16[64,3712]{1,0:T(8,128)(2,1)S(1)} %constant_dynamic-update-slice_fusion.6.refs_0_, bf16[64,3712]{1,0:T(8,128)(2,1)S(1)} %collective-permute-done.22.refs_1_, bf16[64,3712]{1,0:T(8,128)(2,1)S(1)} %collective-permute-done.23.refs_2_, ...), custom_call_target="tpu_custom_call" | custom-call | flops 1879048192 | bytes 9240576 | tf_op jit(solution)/shard_map/pallas_call | solution.py:104
  63.9 0.1 collective-permute-start.25
  64.1 3.6 %collective-permute-done.20 = bf16[64,1792]{1,0:T(8,128)(2,1)S(1)} collective-permute-done((bf16[64,1792]{1,0:T(8,128)(2,1)S(1)}, bf16[64,1792]{1,0:T(8,128)(2,1)S(1)}, u32[]{:S(2)}, u32[]{:S(2)}) %collective-permute-start.20) | collective-permute-done | bytes 229408 | tf_op jit(solution)/shard_map/ppermute | solution.py:138
  67.7 0.5 collective-permute-start.21
  68.2 1.1 %shard_map.81 = (f32[128,1792]{1,0:T(8,128)S(1)}, bf16[128,1792]{1,0:T(8,128)(2,1)S(1)}) custom-call(bf16[256,512]{1,0:T(8,128)(2,1)S(1)} %get-tuple-element.67.hidden_ref, bf16[256,512]{1,0:T(8,128)(2,1)S(1)} %collective-permute-done.25.other_ref, f32[256,128]{1,0:T(8,128)S(1)} %get-tuple-element.68.scale_ref, ...), custom_call_target="tpu_custom_call" | custom-call | flops 939524096 | bytes 4325376 | tf_op jit(solution)/shard_map/pallas_call | solution.py:104
  69.3 1.1 %collective-permute-done.26 = bf16[128,1792]{1,0:T(8,128)(2,1)S(1)} collective-permute-done((bf16[128,1792]{1,0:T(8,128)(2,1)S(1)}, bf16[128,1792]{1,0:T(8,128)(2,1)S(1)}, u32[]{:S(2)}, u32[]{:S(2)}) %collective-permute-start.26) | collective-permute-done | bytes 458784 | tf_op jit(solution)/shard_map/ppermute | solution.py:134
  70.4 0.1 convert_add_fusion.2
  70.6 1.1 %collective-permute-start.27 = (bf16[64,1792]{1,0:T(8,128)(2,1)S(1)}, bf16[64,1792]{1,0:T(8,128)(2,1)S(1)}, u32[]{:S(2)}, u32[]{:S(2)}) collective-permute-start(bf16[64,1792]{1,0:T(8,128)(2,1)S(1)} %bitcast.41), channel_id=1, source_target_pairs={{0,4},{1,3},{2,6},{3,1},{4,0},{5,7},{6,2},{7,5},{8,12},{9,11},{10,... | collective-permute-start | bytes 688136 | tf_op jit(solution)/shard_map/ppermute | solution.py:138
  71.6 0.1 collective-permute-start.32
  71.8 0.8 collective-permute-start.29
  72.6 3.4 %collective-permute-done.21 = bf16[64,1792]{1,0:T(8,128)(2,1)S(1)} collective-permute-done((bf16[64,1792]{1,0:T(8,128)(2,1)S(1)}, bf16[64,1792]{1,0:T(8,128)(2,1)S(1)}, u32[]{:S(2)}, u32[]{:S(2)}) %collective-permute-start.21) | collective-permute-done | bytes 229408 | tf_op jit(solution)/shard_map/ppermute | solution.py:141
  76.0 2.6 %collective-permute-done.27 = bf16[64,1792]{1,0:T(8,128)(2,1)S(1)} collective-permute-done((bf16[64,1792]{1,0:T(8,128)(2,1)S(1)}, bf16[64,1792]{1,0:T(8,128)(2,1)S(1)}, u32[]{:S(2)}, u32[]{:S(2)}) %collective-permute-start.27) | collective-permute-done | bytes 229408 | tf_op jit(solution)/shard_map/ppermute | solution.py:138
  78.6 0.1 fusion.4
  78.7 0.4 collective-permute-start.28
  79.0 1.7 %collective-permute-done.29 = bf16[128,1792]{1,0:T(8,128)(2,1)S(1)} collective-permute-done((bf16[128,1792]{1,0:T(8,128)(2,1)S(1)}, bf16[128,1792]{1,0:T(8,128)(2,1)S(1)}, u32[]{:S(2)}, u32[]{:S(2)}) %collective-permute-start.29) | collective-permute-done | bytes 458784 | tf_op jit(solution)/shard_map/ppermute | solution.py:134
  80.8 0.1 convert_add_fusion.1
  80.9 1.1 %collective-permute-start.30 = (bf16[64,1792]{1,0:T(8,128)(2,1)S(1)}, bf16[64,1792]{1,0:T(8,128)(2,1)S(1)}, u32[]{:S(2)}, u32[]{:S(2)}) collective-permute-start(bf16[64,1792]{1,0:T(8,128)(2,1)S(1)} %bitcast.39), channel_id=1, source_target_pairs={{0,4},{1,3},{2,6},{3,1},{4,0},{5,7},{6,2},{7,5},{8,12},{9,11},{10,... | collective-permute-start | bytes 688136 | tf_op jit(solution)/shard_map/ppermute | solution.py:138
  82.0 1.1 %shard_map.82 = (f32[128,1792]{1,0:T(8,128)S(1)}, bf16[128,1792]{1,0:T(8,128)(2,1)S(1)}) custom-call(bf16[256,512]{1,0:T(8,128)(2,1)S(1)} %get-tuple-element.72.hidden_ref, bf16[256,512]{1,0:T(8,128)(2,1)S(1)} %collective-permute-done.32.other_ref, f32[256,128]{1,0:T(8,128)S(1)} %get-tuple-element.73.scale_ref, ...), custom_call_target="tpu_custom_call" | custom-call | flops 939524096 | bytes 4325376 | tf_op jit(solution)/shard_map/pallas_call | solution.py:104
  83.1 0.9 collective-permute-start.33
  84.0 2.5 %collective-permute-done.28 = bf16[64,1792]{1,0:T(8,128)(2,1)S(1)} collective-permute-done((bf16[64,1792]{1,0:T(8,128)(2,1)S(1)}, bf16[64,1792]{1,0:T(8,128)(2,1)S(1)}, u32[]{:S(2)}, u32[]{:S(2)}) %collective-permute-start.28) | collective-permute-done | bytes 229408 | tf_op jit(solution)/shard_map/ppermute | solution.py:141
  86.5 0.9 collective-permute-done.30
  87.5 0.7 collective-permute-start.31
  88.3 3.4 %collective-permute-done.33 = bf16[128,1792]{1,0:T(8,128)(2,1)S(1)} collective-permute-done((bf16[128,1792]{1,0:T(8,128)(2,1)S(1)}, bf16[128,1792]{1,0:T(8,128)(2,1)S(1)}, u32[]{:S(2)}, u32[]{:S(2)}) %collective-permute-start.33) | collective-permute-done | bytes 458784 | tf_op jit(solution)/shard_map/ppermute | solution.py:134
  91.7 0.1 convert_add_fusion
  91.8 1.1 %collective-permute-start.34 = (bf16[64,1792]{1,0:T(8,128)(2,1)S(1)}, bf16[64,1792]{1,0:T(8,128)(2,1)S(1)}, u32[]{:S(2)}, u32[]{:S(2)}) collective-permute-start(bf16[64,1792]{1,0:T(8,128)(2,1)S(1)} %bitcast.40), channel_id=1, source_target_pairs={{0,4},{1,3},{2,6},{3,1},{4,0},{5,7},{6,2},{7,5},{8,12},{9,11},{10,... | collective-permute-start | bytes 688136 | tf_op jit(solution)/shard_map/ppermute | solution.py:138
  92.9 3.3 %collective-permute-done.31 = bf16[64,1792]{1,0:T(8,128)(2,1)S(1)} collective-permute-done((bf16[64,1792]{1,0:T(8,128)(2,1)S(1)}, bf16[64,1792]{1,0:T(8,128)(2,1)S(1)}, u32[]{:S(2)}, u32[]{:S(2)}) %collective-permute-start.31) | collective-permute-done | bytes 229408 | tf_op jit(solution)/shard_map/ppermute | solution.py:141
  96.2 1.7 %collective-permute-done.34 = bf16[64,1792]{1,0:T(8,128)(2,1)S(1)} collective-permute-done((bf16[64,1792]{1,0:T(8,128)(2,1)S(1)}, bf16[64,1792]{1,0:T(8,128)(2,1)S(1)}, u32[]{:S(2)}, u32[]{:S(2)}) %collective-permute-start.34) | collective-permute-done | bytes 229408 | tf_op jit(solution)/shard_map/ppermute | solution.py:138
  97.9 0.1 fusion
  98.0 0.7 copy-done.1
  (46 shorter events, 0.6 us)
Async XLA Ops:
  2.4 8.8 %copy-start = (bf16[32,3712]{1,0:T(8,128)(2,1)S(1)}, bf16[32,3712]{1,0:T(8,128)(2,1)}, u32[]{:S(2)}) copy-start(bf16[32,3712]{1,0:T(8,128)(2,1)} %shard_map.73) | copy-start | bytes 712708
  2.4 8.8 %collective-permute-start.1 = (bf16[32,3712]{1,0:T(8,128)(2,1)}, bf16[32,3712]{1,0:T(8,128)(2,1)S(1)}, u32[]{:S(2)}, u32[]{:S(2)}) collective-permute-start(bf16[32,3712]{1,0:T(8,128)(2,1)} %shard_map.73), channel_id=1, source_target_pairs={{0,2},{1,5},{2,0},{3,7},{4,6},{5,1},{6,4},{7,3},{8,10},{9,13},{10,... | collective-permute-start | bytes 712712 | tf_op jit(solution)/shard_map/ppermute | solution.py:134
  5.4 9.4 %collective-permute-start = (bf16[32,3712]{1,0:T(8,128)(2,1)}, bf16[32,3712]{1,0:T(8,128)(2,1)S(1)}, u32[]{:S(2)}, u32[]{:S(2)}) collective-permute-start(bf16[32,3712]{1,0:T(8,128)(2,1)} %shard_map.73), channel_id=1, source_target_pairs={{0,8},{2,10},{4,12},{6,14},{8,16},{10,18},{12,20},{14,22},{16,24},... | collective-permute-start | bytes 712712 | tf_op jit(solution)/shard_map/ppermute | solution.py:141
  11.3 11.8 %collective-permute-start.2 = (bf16[64,3712]{1,0:T(8,128)(2,1)S(1)}, bf16[64,3712]{1,0:T(8,128)(2,1)S(1)}, u32[]{:S(2)}, u32[]{:S(2)}) collective-permute-start(bf16[64,3712]{1,0:T(8,128)(2,1)S(1)} %constant_dynamic-update-slice_fusion.refs_0_), channel_id=1, source_target_pairs={{0,4},{1,3},{2,6},{3,1},{4,0},{5,7},{6,2},{7,5},{8,12},{9,11},{10,... | collective-permute-start | bytes 1425416 | tf_op jit(solution)/shard_map/ppermute | solution.py:138
  14.8 8.3 %collective-permute-start.3 = (bf16[32,3712]{1,0:T(8,128)(2,1)S(1)}, bf16[32,3712]{1,0:T(8,128)(2,1)S(1)}, u32[]{:S(2)}, u32[]{:S(2)}) collective-permute-start(bf16[32,3712]{1,0:T(8,128)(2,1)S(1)} %collective-permute-done), channel_id=1, source_target_pairs={{0,8},{2,10},{4,12},{6,14},{8,16},{10,18},{12,20},{14,22},{16,24},... | collective-permute-start | bytes 712712 | tf_op jit(solution)/shard_map/ppermute | solution.py:141
  14.8 8.3 %collective-permute-start.4 = (bf16[32,3712]{1,0:T(8,128)(2,1)S(1)}, bf16[32,3712]{1,0:T(8,128)(2,1)S(1)}, u32[]{:S(2)}, u32[]{:S(2)}) collective-permute-start(bf16[32,3712]{1,0:T(8,128)(2,1)S(1)} %collective-permute-done), channel_id=1, source_target_pairs={{0,2},{1,5},{2,0},{3,7},{4,6},{5,1},{6,4},{7,3},{8,10},{9,13},{10,... | collective-permute-start | bytes 712712 | tf_op jit(solution)/shard_map/ppermute | solution.py:134
  16.3 10.1 %collective-permute-start.6 = (bf16[64,3712]{1,0:T(8,128)(2,1)S(1)}, bf16[64,3712]{1,0:T(8,128)(2,1)S(1)}, u32[]{:S(2)}, u32[]{:S(2)}) collective-permute-start(bf16[64,3712]{1,0:T(8,128)(2,1)S(1)} %constant_dynamic-update-slice_fusion.refs_0_), channel_id=1, source_target_pairs={{0,1},{1,0},{2,3},{3,2},{4,5},{5,4},{6,7},{7,6},{8,9},{9,8},{10,11... | collective-permute-start | bytes 1425416 | tf_op jit(solution)/shard_map/ppermute | solution.py:144
  23.1 3.3 %collective-permute-start.7 = (bf16[64,3712]{1,0:T(8,128)(2,1)S(1)}, bf16[64,3712]{1,0:T(8,128)(2,1)S(1)}, u32[]{:S(2)}, u32[]{:S(2)}) collective-permute-start(bf16[64,3712]{1,0:T(8,128)(2,1)S(1)} %collective-permute-done.2.refs_1_), channel_id=1, source_target_pairs={{0,1},{1,0},{2,3},{3,2},{4,5},{5,4},{6,7},{7,6},{8,9},{9,8},{10,11... | collective-permute-start | bytes 1425416 | tf_op jit(solution)/shard_map/ppermute | solution.py:144
  23.2 11.3 %collective-permute-start.5 = (bf16[64,3712]{1,0:T(8,128)(2,1)S(1)}, bf16[64,3712]{1,0:T(8,128)(2,1)S(1)}, u32[]{:S(2)}, u32[]{:S(2)}) collective-permute-start(bf16[64,3712]{1,0:T(8,128)(2,1)S(1)} %constant_dynamic-update-slice_fusion.2.refs_0_), channel_id=1, source_target_pairs={{0,4},{1,3},{2,6},{3,1},{4,0},{5,7},{6,2},{7,5},{8,12},{9,11},{10,... | collective-permute-start | bytes 1425416 | tf_op jit(solution)/shard_map/ppermute | solution.py:138
  24.3 9.6 %collective-permute-start.8 = (bf16[32,3712]{1,0:T(8,128)(2,1)S(1)}, bf16[32,3712]{1,0:T(8,128)(2,1)S(1)}, u32[]{:S(2)}, u32[]{:S(2)}) collective-permute-start(bf16[32,3712]{1,0:T(8,128)(2,1)S(1)} %collective-permute-done.3), channel_id=1, source_target_pairs={{0,8},{2,10},{4,12},{6,14},{8,16},{10,18},{12,20},{14,22},{16,24},... | collective-permute-start | bytes 712712 | tf_op jit(solution)/shard_map/ppermute | solution.py:141
  25.7 8.8 %collective-permute-start.9 = (bf16[32,3712]{1,0:T(8,128)(2,1)S(1)}, bf16[32,3712]{1,0:T(8,128)(2,1)S(1)}, u32[]{:S(2)}, u32[]{:S(2)}) collective-permute-start(bf16[32,3712]{1,0:T(8,128)(2,1)S(1)} %collective-permute-done.3), channel_id=1, source_target_pairs={{0,2},{1,5},{2,0},{3,7},{4,6},{5,1},{6,4},{7,3},{8,10},{9,13},{10,... | collective-permute-start | bytes 712712 | tf_op jit(solution)/shard_map/ppermute | solution.py:134
  26.4 11.4 %collective-permute-start.10 = (bf16[64,3712]{1,0:T(8,128)(2,1)S(1)}, bf16[64,3712]{1,0:T(8,128)(2,1)S(1)}, u32[]{:S(2)}, u32[]{:S(2)}) collective-permute-start(bf16[64,3712]{1,0:T(8,128)(2,1)S(1)} %constant_dynamic-update-slice_fusion.2.refs_0_), channel_id=1, source_target_pairs={{0,1},{1,0},{2,3},{3,2},{4,5},{5,4},{6,7},{7,6},{8,9},{9,8},{10,11... | collective-permute-start | bytes 1425416 | tf_op jit(solution)/shard_map/ppermute | solution.py:144
  34.5 3.3 %collective-permute-start.11 = (bf16[64,3712]{1,0:T(8,128)(2,1)S(1)}, bf16[64,3712]{1,0:T(8,128)(2,1)S(1)}, u32[]{:S(2)}, u32[]{:S(2)}) collective-permute-start(bf16[64,3712]{1,0:T(8,128)(2,1)S(1)} %collective-permute-done.5.refs_1_), channel_id=1, source_target_pairs={{0,1},{1,0},{2,3},{3,2},{4,5},{5,4},{6,7},{7,6},{8,9},{9,8},{10,11... | collective-permute-start | bytes 1425416 | tf_op jit(solution)/shard_map/ppermute | solution.py:144
  34.8 13.2 %collective-permute-start.15 = (bf16[512,1792]{1,0:T(8,128)(2,1)S(1)}, bf16[512,1792]{1,0:T(8,128)(2,1)S(1)}, u32[]{:S(2)}, u32[]{:S(2)}) collective-permute-start(bf16[512,1792]{1,0:T(8,128)(2,1)S(1)} %get-tuple-element.58), channel_id=1, source_target_pairs={{0,1},{1,0},{2,3},{3,2},{4,5},{5,4},{6,7},{7,6},{8,9},{9,8},{10,11... | collective-permute-start | bytes 5505032 | tf_op jit(solution)/shard_map/ppermute | solution.py:144
  35.1 11.2 %collective-permute-start.12 = (bf16[64,3712]{1,0:T(8,128)(2,1)S(1)}, bf16[64,3712]{1,0:T(8,128)(2,1)S(1)}, u32[]{:S(2)}, u32[]{:S(2)}) collective-permute-start(bf16[64,3712]{1,0:T(8,128)(2,1)S(1)} %constant_dynamic-update-slice_fusion.4.refs_0_), channel_id=1, source_target_pairs={{0,4},{1,3},{2,6},{3,1},{4,0},{5,7},{6,2},{7,5},{8,12},{9,11},{10,... | collective-permute-start | bytes 1425416 | tf_op jit(solution)/shard_map/ppermute | solution.py:138
  36.1 10.2 %collective-permute-start.13 = (bf16[32,3712]{1,0:T(8,128)(2,1)S(1)}, bf16[32,3712]{1,0:T(8,128)(2,1)S(1)}, u32[]{:S(2)}, u32[]{:S(2)}) collective-permute-start(bf16[32,3712]{1,0:T(8,128)(2,1)S(1)} %collective-permute-done.8), channel_id=1, source_target_pairs={{0,2},{1,5},{2,0},{3,7},{4,6},{5,1},{6,4},{7,3},{8,10},{9,13},{10,... | collective-permute-start | bytes 712712 | tf_op jit(solution)/shard_map/ppermute | solution.py:134
  37.7 13.3 %collective-permute-start.16 = (bf16[64,3712]{1,0:T(8,128)(2,1)S(1)}, bf16[64,3712]{1,0:T(8,128)(2,1)S(1)}, u32[]{:S(2)}, u32[]{:S(2)}) collective-permute-start(bf16[64,3712]{1,0:T(8,128)(2,1)S(1)} %constant_dynamic-update-slice_fusion.4.refs_0_), channel_id=1, source_target_pairs={{0,1},{1,0},{2,3},{3,2},{4,5},{5,4},{6,7},{7,6},{8,9},{9,8},{10,11... | collective-permute-start | bytes 1425416 | tf_op jit(solution)/shard_map/ppermute | solution.py:144
  46.3 4.8 %collective-permute-start.17 = (bf16[64,3712]{1,0:T(8,128)(2,1)S(1)}, bf16[64,3712]{1,0:T(8,128)(2,1)S(1)}, u32[]{:S(2)}, u32[]{:S(2)}) collective-permute-start(bf16[64,3712]{1,0:T(8,128)(2,1)S(1)} %collective-permute-done.12.refs_1_), channel_id=1, source_target_pairs={{0,1},{1,0},{2,3},{3,2},{4,5},{5,4},{6,7},{7,6},{8,9},{9,8},{10,11... | collective-permute-start | bytes 1425416 | tf_op jit(solution)/shard_map/ppermute | solution.py:144
  46.4 2.2 %collective-permute-start.14 = (bf16[256,512]{1,0:T(8,128)(2,1)S(1)}, bf16[256,512]{1,0:T(8,128)(2,1)S(1)}, u32[]{:S(2)}, u32[]{:S(2)}) collective-permute-start(bf16[256,512]{1,0:T(8,128)(2,1)S(1)} %get-tuple-element.56.hidden_ref), channel_id=1, source_target_pairs={{0,1},{1,0},{2,3},{3,2},{4,5},{5,4},{6,7},{7,6},{8,9},{9,8},{10,11... | collective-permute-start | bytes 786440 | tf_op jit(solution)/shard_map/ppermute | solution.py:144
  46.9 11.6 %collective-permute-start.22 = (bf16[64,3712]{1,0:T(8,128)(2,1)S(1)}, bf16[64,3712]{1,0:T(8,128)(2,1)S(1)}, u32[]{:S(2)}, u32[]{:S(2)}) collective-permute-start(bf16[64,3712]{1,0:T(8,128)(2,1)S(1)} %constant_dynamic-update-slice_fusion.6.refs_0_), channel_id=1, source_target_pairs={{0,4},{1,3},{2,6},{3,1},{4,0},{5,7},{6,2},{7,5},{8,12},{9,11},{10,... | collective-permute-start | bytes 1425416 | tf_op jit(solution)/shard_map/ppermute | solution.py:138
  49.7 9.9 %collective-permute-start.19 = (bf16[128,1792]{1,0:T(8,128)(2,1)S(1)}, bf16[128,1792]{1,0:T(8,128)(2,1)S(1)}, u32[]{:S(2)}, u32[]{:S(2)}) collective-permute-start(bf16[128,1792]{1,0:T(8,128)(2,1)S(1)} %get-tuple-element.65), channel_id=1, source_target_pairs={{0,2},{1,5},{2,0},{3,7},{4,6},{5,1},{6,4},{7,3},{8,10},{9,13},{10,... | collective-permute-start | bytes 1376264 | tf_op jit(solution)/shard_map/ppermute | solution.py:134
  53.2 5.4 %collective-permute-start.18 = (bf16[256,512]{1,0:T(8,128)(2,1)S(1)}, bf16[256,512]{1,0:T(8,128)(2,1)S(1)}, u32[]{:S(2)}, u32[]{:S(2)}) collective-permute-start(bf16[256,512]{1,0:T(8,128)(2,1)S(1)} %get-tuple-element.61.hidden_ref), channel_id=1, source_target_pairs={{0,1},{1,0},{2,3},{3,2},{4,5},{5,4},{6,7},{7,6},{8,9},{9,8},{10,11... | collective-permute-start | bytes 786440 | tf_op jit(solution)/shard_map/ppermute | solution.py:144
  53.2 8.6 %collective-permute-start.23 = (bf16[64,3712]{1,0:T(8,128)(2,1)S(1)}, bf16[64,3712]{1,0:T(8,128)(2,1)S(1)}, u32[]{:S(2)}, u32[]{:S(2)}) collective-permute-start(bf16[64,3712]{1,0:T(8,128)(2,1)S(1)} %constant_dynamic-update-slice_fusion.6.refs_0_), channel_id=1, source_target_pairs={{0,1},{1,0},{2,3},{3,2},{4,5},{5,4},{6,7},{7,6},{8,9},{9,8},{10,11... | collective-permute-start | bytes 1425416 | tf_op jit(solution)/shard_map/ppermute | solution.py:144
  58.5 3.3 %collective-permute-start.24 = (bf16[64,3712]{1,0:T(8,128)(2,1)S(1)}, bf16[64,3712]{1,0:T(8,128)(2,1)S(1)}, u32[]{:S(2)}, u32[]{:S(2)}) collective-permute-start(bf16[64,3712]{1,0:T(8,128)(2,1)S(1)} %collective-permute-done.22.refs_1_), channel_id=1, source_target_pairs={{0,1},{1,0},{2,3},{3,2},{4,5},{5,4},{6,7},{7,6},{8,9},{9,8},{10,11... | collective-permute-start | bytes 1425416 | tf_op jit(solution)/shard_map/ppermute | solution.py:144
  59.8 7.8 %collective-permute-start.20 = (bf16[64,1792]{1,0:T(8,128)(2,1)S(1)}, bf16[64,1792]{1,0:T(8,128)(2,1)S(1)}, u32[]{:S(2)}, u32[]{:S(2)}) collective-permute-start(bf16[64,1792]{1,0:T(8,128)(2,1)S(1)} %bitcast.38), channel_id=1, source_target_pairs={{0,4},{1,3},{2,6},{3,1},{4,0},{5,7},{6,2},{7,5},{8,12},{9,11},{10,... | collective-permute-start | bytes 688136 | tf_op jit(solution)/shard_map/ppermute | solution.py:138
  60.9 9.5 %collective-permute-start.26 = (bf16[128,1792]{1,0:T(8,128)(2,1)S(1)}, bf16[128,1792]{1,0:T(8,128)(2,1)S(1)}, u32[]{:S(2)}, u32[]{:S(2)}) collective-permute-start(bf16[128,1792]{1,0:T(8,128)(2,1)S(1)} %get-tuple-element.63), channel_id=1, source_target_pairs={{0,2},{1,5},{2,0},{3,7},{4,6},{5,1},{6,4},{7,3},{8,10},{9,13},{10,... | collective-permute-start | bytes 1376264 | tf_op jit(solution)/shard_map/ppermute | solution.py:134
  63.9 4.2 %collective-permute-start.25 = (bf16[256,512]{1,0:T(8,128)(2,1)S(1)}, bf16[256,512]{1,0:T(8,128)(2,1)S(1)}, u32[]{:S(2)}, u32[]{:S(2)}) collective-permute-start(bf16[256,512]{1,0:T(8,128)(2,1)S(1)} %get-tuple-element.67.hidden_ref), channel_id=1, source_target_pairs={{0,1},{1,0},{2,3},{3,2},{4,5},{5,4},{6,7},{7,6},{8,9},{9,8},{10,11... | collective-permute-start | bytes 786440 | tf_op jit(solution)/shard_map/ppermute | solution.py:144
  67.7 8.3 %collective-permute-start.21 = (bf16[64,1792]{1,0:T(8,128)(2,1)S(1)}, bf16[64,1792]{1,0:T(8,128)(2,1)S(1)}, u32[]{:S(2)}, u32[]{:S(2)}) collective-permute-start(bf16[64,1792]{1,0:T(8,128)(2,1)S(1)} %fusion.5), channel_id=1, source_target_pairs={{0,8},{2,10},{4,12},{6,14},{8,16},{10,18},{12,20},{14,22},{16,24},... | collective-permute-start | bytes 688136 | tf_op jit(solution)/shard_map/ppermute | solution.py:141
  70.6 8.0 %collective-permute-start.27 = (bf16[64,1792]{1,0:T(8,128)(2,1)S(1)}, bf16[64,1792]{1,0:T(8,128)(2,1)S(1)}, u32[]{:S(2)}, u32[]{:S(2)}) collective-permute-start(bf16[64,1792]{1,0:T(8,128)(2,1)S(1)} %bitcast.41), channel_id=1, source_target_pairs={{0,4},{1,3},{2,6},{3,1},{4,0},{5,7},{6,2},{7,5},{8,12},{9,11},{10,... | collective-permute-start | bytes 688136 | tf_op jit(solution)/shard_map/ppermute | solution.py:138
  71.6 10.3 %collective-permute-start.32 = (bf16[256,512]{1,0:T(8,128)(2,1)S(1)}, bf16[256,512]{1,0:T(8,128)(2,1)S(1)}, u32[]{:S(2)}, u32[]{:S(2)}) collective-permute-start(bf16[256,512]{1,0:T(8,128)(2,1)S(1)} %get-tuple-element.72.hidden_ref), channel_id=1, source_target_pairs={{0,1},{1,0},{2,3},{3,2},{4,5},{5,4},{6,7},{7,6},{8,9},{9,8},{10,11... | collective-permute-start | bytes 786440 | tf_op jit(solution)/shard_map/ppermute | solution.py:144
  71.8 9.0 %collective-permute-start.29 = (bf16[128,1792]{1,0:T(8,128)(2,1)S(1)}, bf16[128,1792]{1,0:T(8,128)(2,1)S(1)}, u32[]{:S(2)}, u32[]{:S(2)}) collective-permute-start(bf16[128,1792]{1,0:T(8,128)(2,1)S(1)} %get-tuple-element.69), channel_id=1, source_target_pairs={{0,2},{1,5},{2,0},{3,7},{4,6},{5,1},{6,4},{7,3},{8,10},{9,13},{10,... | collective-permute-start | bytes 1376264 | tf_op jit(solution)/shard_map/ppermute | solution.py:134
  78.7 7.9 %collective-permute-start.28 = (bf16[64,1792]{1,0:T(8,128)(2,1)S(1)}, bf16[64,1792]{1,0:T(8,128)(2,1)S(1)}, u32[]{:S(2)}, u32[]{:S(2)}) collective-permute-start(bf16[64,1792]{1,0:T(8,128)(2,1)S(1)} %fusion.4), channel_id=1, source_target_pairs={{0,8},{2,10},{4,12},{6,14},{8,16},{10,18},{12,20},{14,22},{16,24},... | collective-permute-start | bytes 688136 | tf_op jit(solution)/shard_map/ppermute | solution.py:141
  80.9 6.6 %collective-permute-start.30 = (bf16[64,1792]{1,0:T(8,128)(2,1)S(1)}, bf16[64,1792]{1,0:T(8,128)(2,1)S(1)}, u32[]{:S(2)}, u32[]{:S(2)}) collective-permute-start(bf16[64,1792]{1,0:T(8,128)(2,1)S(1)} %bitcast.39), channel_id=1, source_target_pairs={{0,4},{1,3},{2,6},{3,1},{4,0},{5,7},{6,2},{7,5},{8,12},{9,11},{10,... | collective-permute-start | bytes 688136 | tf_op jit(solution)/shard_map/ppermute | solution.py:138
  83.1 8.5 %collective-permute-start.33 = (bf16[128,1792]{1,0:T(8,128)(2,1)S(1)}, bf16[128,1792]{1,0:T(8,128)(2,1)S(1)}, u32[]{:S(2)}, u32[]{:S(2)}) collective-permute-start(bf16[128,1792]{1,0:T(8,128)(2,1)S(1)} %get-tuple-element.76), channel_id=1, source_target_pairs={{0,2},{1,5},{2,0},{3,7},{4,6},{5,1},{6,4},{7,3},{8,10},{9,13},{10,... | collective-permute-start | bytes 1376264 | tf_op jit(solution)/shard_map/ppermute | solution.py:134
  87.5 8.6 %collective-permute-start.31 = (bf16[64,1792]{1,0:T(8,128)(2,1)S(1)}, bf16[64,1792]{1,0:T(8,128)(2,1)S(1)}, u32[]{:S(2)}, u32[]{:S(2)}) collective-permute-start(bf16[64,1792]{1,0:T(8,128)(2,1)S(1)} %fusion.2), channel_id=1, source_target_pairs={{0,8},{2,10},{4,12},{6,14},{8,16},{10,18},{12,20},{14,22},{16,24},... | collective-permute-start | bytes 688136 | tf_op jit(solution)/shard_map/ppermute | solution.py:141
  91.8 6.1 %collective-permute-start.34 = (bf16[64,1792]{1,0:T(8,128)(2,1)S(1)}, bf16[64,1792]{1,0:T(8,128)(2,1)S(1)}, u32[]{:S(2)}, u32[]{:S(2)}) collective-permute-start(bf16[64,1792]{1,0:T(8,128)(2,1)S(1)} %bitcast.40), channel_id=1, source_target_pairs={{0,4},{1,3},{2,6},{3,1},{4,0},{5,7},{6,2},{7,5},{8,12},{9,11},{10,... | collective-permute-start | bytes 688136 | tf_op jit(solution)/shard_map/ppermute | solution.py:138
  98.0 0.7 copy-start.1

commit v4 on v3

--- a/solution.py
+++ b/solution.py
@@ -137,8 +137,8 @@
         pairs = [(2 * e + c, 2 * (e ^ (2 - c)) + c) for e in range(ep) for c in range(2)]
         return lax.ppermute(a, ("ep", "tp"), pairs)
 
-    def ring(a):
-        return lax.ppermute(a, "ep", [(e, (e + QUAD) % ep) for e in range(ep)])
+    def shift(a, steps):
+        return lax.ppermute(a, "ep", [(e, (e + QUAD * steps) % ep) for e in range(ep)])
 
     def other_core(a):
         return lax.ppermute(a, "tp", [(0, 1), (1, 0)])
@@ -193,56 +193,54 @@
     def join(a, b):
         return jnp.concatenate([a, b], axis=0)
 
+    came = {0: block}
+    near = {0: first_link(block)}
+    came[1] = shift(block, 1)
+    gate, up, down_mine, down_sent = load(*lax.optimization_barrier((w_gate, w_up, w_down, block))[:3])
+    down_received = other_core(down_sent)
+    pairs, fars, held, sums, gots, parts, passes = {}, {}, {}, {}, {}, {}, {}
+
     def add_up(p, *ties):
-        part = after(sums[p][0], *ties) + gots[p].astype(F32)
-        part = part.reshape(2, 2, half, share)
+        part = (after(sums[p][0], *ties) + gots[p].astype(F32)).reshape(2, 2, half, share)
         passes[p] = part[:, 1].reshape(2 * half, share).astype(BF16)
         parts[p] = part[:, 0].reshape(2 * half, share), second_link(passes[p])
 
-    coming = ring(block)
-    near = first_link(block)
-    gate, up, down_mine, down_sent = load(*lax.optimization_barrier((w_gate, w_up, w_down, block))[:3])
-    down_received = other_core(down_sent)
-    blocks, pairs, fars = [block, coming], {}, {}
-    held, sums, gots, parts, passes = {}, {}, {}, {}, {}
-    marks = [down_mine]
-    for i in range(planes + 2):
-        if i < planes:
-            if 1 <= i < planes - 1:
-                blocks.append(coming)
-                marks.append(coming)
-            pairs[i] = join(after(blocks[i], *marks), near)
-            fars[i] = second_link(pairs[i])
-            marks = [fars[i]]
-            if i + 1 < planes:
-                if i == 0:
-                    blocks[1] = after(coming, pairs[0])
-                if i + 2 < planes:
-                    coming = ring(blocks[i + 1])
-                near = first_link(blocks[i + 1])
-        p = i - 1
-        if 0 <= p < planes:
-            ties = [pairs[i]] if i < planes else []
-            ties += [sums[p - 1][1]] if p - 1 in sums else []
-            far = after(fars[p], *ties) if ties else fars[p]
-            held[p] = experts(pairs[p], far, other_core(pairs[p]), other_core(far))
-            marks.append(held[p][0])
-        p = i - 2
-        if 1 <= p < planes:
-            ties = [pairs[i]] if i in pairs else []
-            sums[p] = finish(after(held[p][0], *ties) if ties else held[p][0], *held[p][1:])
-            gots[p] = first_link(sums[p][1])
-            if p > 1:
-                add_up(p - 1, sums[p][1])
-    add_up(planes - 1)
-    sums[0] = finish(after(held[0][0], passes[planes - 1]), *held[0][1:])
-    gots[0] = first_link(sums[0][1])
+    def multiply(p, *ties):
+        far = after(fars[p], *ties)
+        held[p] = experts(pairs[p], far, other_core(pairs[p]), other_core(far))
+
+    def down_of(p, *ties):
+        sums[p] = finish(after(held[p][0], *ties), *held[p][1:])
+        gots[p] = first_link(sums[p][1])
+
+    for p in range(planes):
+        ties = [down_mine] if p == 0 else [fars[p - 1]]
+        ties += [came[p + 1]] if 1 <= p < planes - 1 else []
+        ties += [held[p - 2][0]] if p >= 2 else []
+        pairs[p] = join(after(came[p], *ties), near[p])
+        fars[p] = second_link(pairs[p])
+        if p == 0:
+            came[1] = after(came[1], pairs[0])
+        if p + 1 < planes:
+            near[p + 1] = first_link(came[p + 1])
+        if p + 2 < planes:
+            came[p + 2] = shift(came[p + 1], 1)
+        if p >= 1:
+            multiply(p - 1, pairs[p])
+    for p in range(1, planes):
+        if p not in held:
+            multiply(p, sums[p - 1][1])
+        down_of(p, *([pairs[p + 2]] if p + 2 < planes else [pairs[planes - 1]] if p + 2 == planes else []))
+        if p >= 2:
+            add_up(p - 1)
+    down_of(0, sums[planes - 1][1], passes[1])
+    add_up(planes - 1, sums[0][1])
+    add_up(0, passes[planes - 1])
     carried = None
     for p in range(1, planes):
-        total = parts[p][0] + parts[p][1].astype(F32)
+        total = parts[p][0] + after(parts[p][1], passes[(p + 1) % planes]).astype(F32)
         passing = (total if carried is None else carried.astype(F32) + total).astype(BF16)
-        carried = ring(passing)
-    add_up(0, passing)
+        carried = shift(passing, 1)
     total = carried.astype(F32) + parts[0][0] + parts[0][1].astype(F32)
     mine_rows, other_rows = total[:half], total[half:]
     first = jnp.where(core == 0, mine_rows, other_rows)

time: 98.9 us -> 97 us (0.981)
  waiting for transfers between devices: 50.8 us -> 48.3 us
    ppermute x8, waiting for transfers between devices: 20.5 us -> 12.7 us  [second_link(): return lax.ppermute(a, ('ep', 'tp'), pairs)]
    ppermute x8, waiting for transfers between devices: 6.3 us -> 12.5 us  [first_link(): return lax.ppermute(a, ('ep', 'tp'), pairs)]
    ppermute x6, waiting for transfers between devices: 23.3 us -> 21.6 us  [shift(): lax.ppermute(a, 'ep', [(e, (e + QUAD * steps) % ep) for e in range(ep)])]
    ppermute x6, starting transfers between devices: 4.58 us -> 3.58 us  [shift(): lax.ppermute(a, 'ep', [(e, (e + QUAD * steps) % ep) for e in range(ep)])]
  transfers between devices with their start and end apart: 35 -> 35, of which waited for: 17 -> 17; matrix products, arithmetic and copies ran while one was open for 1% -> 1% of each run, Pallas kernels for 17% -> 18%
where the time goes in v4:
time: 97 us; the launch traced here: 96.8 us
  waiting for transfers between devices  48.3 us (50%)
  starting transfers between devices  27.1 us (28%)
  Pallas kernels  19.4 us (20%)
  local copies, waits for them, and re-layouts  1.09 us (1%)
    ppermute x6, waiting for transfers between devices, shift(): lax.ppermute(a, 'ep', [(e, (e + QUAD * steps) % ep) for e in range(ep)])  21.6 us
    pallas_call x10, Pallas kernels, call(): pl.pallas_call(kernel, out_shape=outs, in_specs=[pl.BlockSpec(memory_spac...  19.4 us
    ppermute x8, waiting for transfers between devices, second_link(): return lax.ppermute(a, ('ep', 'tp'), pairs)  12.7 us
    ppermute x8, waiting for transfers between devices, first_link(): return lax.ppermute(a, ('ep', 'tp'), pairs)  12.5 us
    ppermute x8, starting transfers between devices, first_link(): return lax.ppermute(a, ('ep', 'tp'), pairs)  11.3 us
    ppermute x8, starting transfers between devices, second_link(): return lax.ppermute(a, ('ep', 'tp'), pairs)  9.28 us
    ppermute x6, starting transfers between devices, shift(): lax.ppermute(a, 'ep', [(e, (e + QUAD * steps) % ep) for e in range(ep)])  3.58 us
    ppermute x13, starting transfers between devices, other_core(): return lax.ppermute(a, 'tp', [(0, 1), (1, 0)])  2.92 us
  transfers between devices with their start and end apart: 35, of which 17 were waited for; matrix products, arithmetic and copies ran while one was open for 1% of the time, Pallas kernels for 18%

profile of v4, /device:TPU:0, one launch (start us, length us, event | category | flops | bytes accessed | tf_op | source)
XLA Modules:
  0.0 96.8 jit_solution(16837251402368473426)
XLA Ops:
  0.0 2.4 %shard_map.73 = bf16[32,3712]{1,0:T(8,128)(2,1)} custom-call(bf16[64,3584]{1,0:T(8,128)(2,1)} %tokens_ref.1, s32[16]{0:T(128)} %copied_ref.1, f32[8,64]{1,0:T(8,128)} %bitcast.42, s32[8,64]{1,0:T(8,128)} %bitcast.43), custom_call_target="tpu_custom_call" | custom-call | bytes 462912 | tf_op jit(solution)/shard_map/pallas_call | solution.py:104
  2.4 3.0 %collective-permute-start.1 = (bf16[32,3712]{1,0:T(8,128)(2,1)}, bf16[32,3712]{1,0:T(8,128)(2,1)S(1)}, u32[]{:S(2)}, u32[]{:S(2)}) collective-permute-start(bf16[32,3712]{1,0:T(8,128)(2,1)} %shard_map.73), channel_id=1, source_target_pairs={{0,2},{1,5},{2,0},{3,7},{4,6},{5,1},{6,4},{7,3},{8,10},{9,13},{10,... | collective-permute-start | bytes 712712 | tf_op jit(solution)/shard_map/ppermute | solution.py:134
  5.4 1.6 %collective-permute-start = (bf16[32,3712]{1,0:T(8,128)(2,1)}, bf16[32,3712]{1,0:T(8,128)(2,1)S(1)}, u32[]{:S(2)}, u32[]{:S(2)}) collective-permute-start(bf16[32,3712]{1,0:T(8,128)(2,1)} %shard_map.73), channel_id=1, source_target_pairs={{0,8},{2,10},{4,12},{6,14},{8,16},{10,18},{12,20},{14,22},{16,24},... | collective-permute-start | bytes 712712 | tf_op jit(solution)/shard_map/ppermute | solution.py:141
  7.0 4.2 %shard_map.74 = (bf16[3584,512]{1,0:T(8,128)(2,1)S(1)}, bf16[3584,512]{1,0:T(8,128)(2,1)S(1)}, bf16[512,1792]{1,0:T(8,128)(2,1)S(1)}, bf16[512,1792]{1,0:T(8,128)(2,1)S(1)}) custom-call(bf16[1,3584,512]{2,1,0:T(8,128)(2,1)} %gate_hbm, bf16[1,3584,512]{2,1,0:T(8,128)(2,1)} %up_hbm, bf16[1,512,3584]{2,1,0:T(8,128)(2,1)} %down_hbm), custom_call_target="tpu_custom_call" | custom-call | bytes 11010048 | tf_op jit(solution)/shard_map/pallas_call | solution.py:104
  11.3 1.6 %collective-permute-start.2 = (bf16[64,3712]{1,0:T(8,128)(2,1)S(1)}, bf16[64,3712]{1,0:T(8,128)(2,1)S(1)}, u32[]{:S(2)}, u32[]{:S(2)}) collective-permute-start(bf16[64,3712]{1,0:T(8,128)(2,1)S(1)} %constant_dynamic-update-slice_fusion.refs_0_), channel_id=1, source_target_pairs={{0,4},{1,3},{2,6},{3,1},{4,0},{5,7},{6,2},{7,5},{8,12},{9,11},{10,... | collective-permute-start | bytes 1425416 | tf_op jit(solution)/shard_map/ppermute | solution.py:138
  12.8 1.9 %collective-permute-done = bf16[32,3712]{1,0:T(8,128)(2,1)S(1)} collective-permute-done((bf16[32,3712]{1,0:T(8,128)(2,1)}, bf16[32,3712]{1,0:T(8,128)(2,1)S(1)}, u32[]{:S(2)}, u32[]{:S(2)}) %collective-permute-start) | collective-permute-done | bytes 237600 | tf_op jit(solution)/shard_map/ppermute | solution.py:141
  14.8 1.5 %collective-permute-start.4 = (bf16[32,3712]{1,0:T(8,128)(2,1)S(1)}, bf16[32,3712]{1,0:T(8,128)(2,1)S(1)}, u32[]{:S(2)}, u32[]{:S(2)}) collective-permute-start(bf16[32,3712]{1,0:T(8,128)(2,1)S(1)} %collective-permute-done), channel_id=1, source_target_pairs={{0,2},{1,5},{2,0},{3,7},{4,6},{5,1},{6,4},{7,3},{8,10},{9,13},{10,... | collective-permute-start | bytes 712712 | tf_op jit(solution)/shard_map/ppermute | solution.py:134
  16.3 6.8 %collective-permute-done.3 = bf16[32,3712]{1,0:T(8,128)(2,1)S(1)} collective-permute-done((bf16[32,3712]{1,0:T(8,128)(2,1)S(1)}, bf16[32,3712]{1,0:T(8,128)(2,1)S(1)}, u32[]{:S(2)}, u32[]{:S(2)}) %collective-permute-start.3) | collective-permute-done | bytes 237600 | tf_op jit(solution)/shard_map/ppermute | solution.py:141
  23.1 0.1 collective-permute-start.8
  23.2 1.1 %collective-permute-start.5 = (bf16[64,3712]{1,0:T(8,128)(2,1)S(1)}, bf16[64,3712]{1,0:T(8,128)(2,1)S(1)}, u32[]{:S(2)}, u32[]{:S(2)}) collective-permute-start(bf16[64,3712]{1,0:T(8,128)(2,1)S(1)} %constant_dynamic-update-slice_fusion.2.refs_0_), channel_id=1, source_target_pairs={{0,4},{1,3},{2,6},{3,1},{4,0},{5,7},{6,2},{7,5},{8,12},{9,11},{10,... | collective-permute-start | bytes 1425416 | tf_op jit(solution)/shard_map/ppermute | solution.py:138
  24.3 1.4 %collective-permute-start.6 = (bf16[32,3712]{1,0:T(8,128)(2,1)S(1)}, bf16[32,3712]{1,0:T(8,128)(2,1)S(1)}, u32[]{:S(2)}, u32[]{:S(2)}) collective-permute-start(bf16[32,3712]{1,0:T(8,128)(2,1)S(1)} %collective-permute-done.3), channel_id=1, source_target_pairs={{0,8},{2,10},{4,12},{6,14},{8,16},{10,18},{12,20},{14,22},{16,24},... | collective-permute-start | bytes 712712 | tf_op jit(solution)/shard_map/ppermute | solution.py:141
  25.7 0.7 collective-permute-start.9
  26.4 2.1 %shard_map.75 = (bf16[256,512]{1,0:T(8,128)(2,1)S(1)}, f32[256,128]{1,0:T(8,128)S(1)}) custom-call(bf16[64,3712]{1,0:T(8,128)(2,1)S(1)} %constant_dynamic-update-slice_fusion.refs_0_, bf16[64,3712]{1,0:T(8,128)(2,1)S(1)} %collective-permute-done.2.refs_1_, bf16[64,3712]{1,0:T(8,128)(2,1)S(1)} %collective-permute-done.7.refs_2_, ...), custom_call_target="tpu_custom_call" | custom-call | flops 1879048192 | bytes 9240576 | tf_op jit(solution)/shard_map/pallas_call | solution.py:104
  28.5 5.4 %collective-permute-done.6 = bf16[32,3712]{1,0:T(8,128)(2,1)S(1)} collective-permute-done((bf16[32,3712]{1,0:T(8,128)(2,1)S(1)}, bf16[32,3712]{1,0:T(8,128)(2,1)S(1)}, u32[]{:S(2)}, u32[]{:S(2)}) %collective-permute-start.6) | collective-permute-done | bytes 237600 | tf_op jit(solution)/shard_map/ppermute | solution.py:141
  33.9 0.5 collective-permute-done.5.refs_1_
  34.5 0.3 collective-permute-start.11
  34.8 0.3 collective-permute-start.15
  35.1 1.0 %collective-permute-start.12 = (bf16[64,3712]{1,0:T(8,128)(2,1)S(1)}, bf16[64,3712]{1,0:T(8,128)(2,1)S(1)}, u32[]{:S(2)}, u32[]{:S(2)}) collective-permute-start(bf16[64,3712]{1,0:T(8,128)(2,1)S(1)} %constant_dynamic-update-slice_fusion.4.refs_0_), channel_id=1, source_target_pairs={{0,4},{1,3},{2,6},{3,1},{4,0},{5,7},{6,2},{7,5},{8,12},{9,11},{10,... | collective-permute-start | bytes 1425416 | tf_op jit(solution)/shard_map/ppermute | solution.py:138
  36.1 1.7 %collective-permute-start.13 = (bf16[32,3712]{1,0:T(8,128)(2,1)S(1)}, bf16[32,3712]{1,0:T(8,128)(2,1)S(1)}, u32[]{:S(2)}, u32[]{:S(2)}) collective-permute-start(bf16[32,3712]{1,0:T(8,128)(2,1)S(1)} %collective-permute-done.6), channel_id=1, source_target_pairs={{0,2},{1,5},{2,0},{3,7},{4,6},{5,1},{6,4},{7,3},{8,10},{9,13},{10,... | collective-permute-start | bytes 712712 | tf_op jit(solution)/shard_map/ppermute | solution.py:134
  37.8 2.1 %shard_map.76 = (bf16[256,512]{1,0:T(8,128)(2,1)S(1)}, f32[256,128]{1,0:T(8,128)S(1)}) custom-call(bf16[64,3712]{1,0:T(8,128)(2,1)S(1)} %constant_dynamic-update-slice_fusion.2.refs_0_, bf16[64,3712]{1,0:T(8,128)(2,1)S(1)} %collective-permute-done.5.refs_1_, bf16[64,3712]{1,0:T(8,128)(2,1)S(1)} %collective-permute-done.10.refs_2_, ...), custom_call_target="tpu_custom_call" | custom-call | flops 1879048192 | bytes 9240576 | tf_op jit(solution)/shard_map/pallas_call | solution.py:104
  39.8 6.4 %collective-permute-done.12.refs_1_ = bf16[64,3712]{1,0:T(8,128)(2,1)S(1)} collective-permute-done((bf16[64,3712]{1,0:T(8,128)(2,1)S(1)}, bf16[64,3712]{1,0:T(8,128)(2,1)S(1)}, u32[]{:S(2)}, u32[]{:S(2)}) %collective-permute-start.12) | collective-permute-done | bytes 475168 | tf_op jit(solution)/shard_map/ppermute | solution.py:138
  46.3 0.1 collective-permute-start.19
  46.4 0.5 collective-permute-start.14
  46.9 1.0 %collective-permute-start.24 = (bf16[64,3712]{1,0:T(8,128)(2,1)S(1)}, bf16[64,3712]{1,0:T(8,128)(2,1)S(1)}, u32[]{:S(2)}, u32[]{:S(2)}) collective-permute-start(bf16[64,3712]{1,0:T(8,128)(2,1)S(1)} %constant_dynamic-update-slice_fusion.6.refs_0_), channel_id=1, source_target_pairs={{0,4},{1,3},{2,6},{3,1},{4,0},{5,7},{6,2},{7,5},{8,12},{9,11},{10,... | collective-permute-start | bytes 1425416 | tf_op jit(solution)/shard_map/ppermute | solution.py:138
  47.9 0.7 collective-permute-done.14.other_ref
  48.6 1.1 %shard_map.77 = (f32[128,1792]{1,0:T(8,128)S(1)}, bf16[128,1792]{1,0:T(8,128)(2,1)S(1)}) custom-call(bf16[256,512]{1,0:T(8,128)(2,1)S(1)} %get-tuple-element.60.hidden_ref, bf16[256,512]{1,0:T(8,128)(2,1)S(1)} %collective-permute-done.14.other_ref, f32[256,128]{1,0:T(8,128)S(1)} %get-tuple-element.61.scale_ref, ...), custom_call_target="tpu_custom_call" | custom-call | flops 939524096 | bytes 4325376 | tf_op jit(solution)/shard_map/pallas_call | solution.py:104
  49.7 1.3 %collective-permute-start.16 = (bf16[128,1792]{1,0:T(8,128)(2,1)S(1)}, bf16[128,1792]{1,0:T(8,128)(2,1)S(1)}, u32[]{:S(2)}, u32[]{:S(2)}) collective-permute-start(bf16[128,1792]{1,0:T(8,128)(2,1)S(1)} %get-tuple-element.64), channel_id=1, source_target_pairs={{0,2},{1,5},{2,0},{3,7},{4,6},{5,1},{6,4},{7,3},{8,10},{9,13},{10,... | collective-permute-start | bytes 1376264 | tf_op jit(solution)/shard_map/ppermute | solution.py:134
  51.1 2.1 %shard_map.78 = (bf16[256,512]{1,0:T(8,128)(2,1)S(1)}, f32[256,128]{1,0:T(8,128)S(1)}) custom-call(bf16[64,3712]{1,0:T(8,128)(2,1)S(1)} %constant_dynamic-update-slice_fusion.4.refs_0_, bf16[64,3712]{1,0:T(8,128)(2,1)S(1)} %collective-permute-done.12.refs_1_, bf16[64,3712]{1,0:T(8,128)(2,1)S(1)} %collective-permute-done.18.refs_2_, ...), custom_call_target="tpu_custom_call" | custom-call | flops 1879048192 | bytes 9240576 | tf_op jit(solution)/shard_map/pallas_call | solution.py:104
  53.2 0.1 collective-permute-start.20
  53.2 0.5 collective-permute-start.28
  53.7 0.1 collective-permute-start.25
  53.8 0.9 collective-permute-done.20.other_ref
  54.8 1.1 %shard_map.79 = (f32[128,1792]{1,0:T(8,128)S(1)}, bf16[128,1792]{1,0:T(8,128)(2,1)S(1)}) custom-call(bf16[256,512]{1,0:T(8,128)(2,1)S(1)} %get-tuple-element.67.hidden_ref, bf16[256,512]{1,0:T(8,128)(2,1)S(1)} %collective-permute-done.20.other_ref, f32[256,128]{1,0:T(8,128)S(1)} %get-tuple-element.68.scale_ref, ...), custom_call_target="tpu_custom_call" | custom-call | flops 939524096 | bytes 4325376 | tf_op jit(solution)/shard_map/pallas_call | solution.py:104
  55.9 0.8 collective-permute-start.21
  56.7 1.8 %collective-permute-done.24.refs_1_ = bf16[64,3712]{1,0:T(8,128)(2,1)S(1)} collective-permute-done((bf16[64,3712]{1,0:T(8,128)(2,1)S(1)}, bf16[64,3712]{1,0:T(8,128)(2,1)S(1)}, u32[]{:S(2)}, u32[]{:S(2)}) %collective-permute-start.24) | collective-permute-done | bytes 475168 | tf_op jit(solution)/shard_map/ppermute | solution.py:138
  58.5 1.1 %collective-permute-done.16 = bf16[128,1792]{1,0:T(8,128)(2,1)S(1)} collective-permute-done((bf16[128,1792]{1,0:T(8,128)(2,1)S(1)}, bf16[128,1792]{1,0:T(8,128)(2,1)S(1)}, u32[]{:S(2)}, u32[]{:S(2)}) %collective-permute-start.16) | collective-permute-done | bytes 458784 | tf_op jit(solution)/shard_map/ppermute | solution.py:134
  59.6 0.1 convert_add_fusion.3
  59.7 1.1 %collective-permute-start.17 = (bf16[64,1792]{1,0:T(8,128)(2,1)S(1)}, bf16[64,1792]{1,0:T(8,128)(2,1)S(1)}, u32[]{:S(2)}, u32[]{:S(2)}) collective-permute-start(bf16[64,1792]{1,0:T(8,128)(2,1)S(1)} %bitcast.39), channel_id=1, source_target_pairs={{0,4},{1,3},{2,6},{3,1},{4,0},{5,7},{6,2},{7,5},{8,12},{9,11},{10,... | collective-permute-start | bytes 688136 | tf_op jit(solution)/shard_map/ppermute | solution.py:138
  60.8 2.1 %shard_map.80 = (bf16[256,512]{1,0:T(8,128)(2,1)S(1)}, f32[256,128]{1,0:T(8,128)S(1)}) custom-call(bf16[64,3712]{1,0:T(8,128)(2,1)S(1)} %constant_dynamic-update-slice_fusion.6.refs_0_, bf16[64,3712]{1,0:T(8,128)(2,1)S(1)} %collective-permute-done.24.refs_1_, bf16[64,3712]{1,0:T(8,128)(2,1)S(1)} %collective-permute-done.25.refs_2_, ...), custom_call_target="tpu_custom_call" | custom-call | flops 1879048192 | bytes 9240576 | tf_op jit(solution)/shard_map/pallas_call | solution.py:104
  62.9 1.0 %collective-permute-start.27 = (bf16[256,512]{1,0:T(8,128)(2,1)S(1)}, bf16[256,512]{1,0:T(8,128)(2,1)S(1)}, u32[]{:S(2)}, u32[]{:S(2)}) collective-permute-start(bf16[256,512]{1,0:T(8,128)(2,1)S(1)} %get-tuple-element.73.hidden_ref), channel_id=1, source_target_pairs={{0,1},{1,0},{2,3},{3,2},{4,5},{5,4},{6,7},{7,6},{8,9},{9,8},{10,11... | collective-permute-start | bytes 786440 | tf_op jit(solution)/shard_map/ppermute | solution.py:144
  64.0 1.6 %collective-permute-done.21 = bf16[128,1792]{1,0:T(8,128)(2,1)S(1)} collective-permute-done((bf16[128,1792]{1,0:T(8,128)(2,1)S(1)}, bf16[128,1792]{1,0:T(8,128)(2,1)S(1)}, u32[]{:S(2)}, u32[]{:S(2)}) %collective-permute-start.21) | collective-permute-done | bytes 458784 | tf_op jit(solution)/shard_map/ppermute | solution.py:134
  65.5 0.1 convert_add_fusion.2
  65.7 1.1 %collective-permute-start.23 = (bf16[64,1792]{1,0:T(8,128)(2,1)S(1)}, bf16[64,1792]{1,0:T(8,128)(2,1)S(1)}, u32[]{:S(2)}, u32[]{:S(2)}) collective-permute-start(bf16[64,1792]{1,0:T(8,128)(2,1)S(1)} %bitcast.38), channel_id=1, source_target_pairs={{0,4},{1,3},{2,6},{3,1},{4,0},{5,7},{6,2},{7,5},{8,12},{9,11},{10,... | collective-permute-start | bytes 688136 | tf_op jit(solution)/shard_map/ppermute | solution.py:138
  66.8 1.1 %collective-permute-done.17 = bf16[64,1792]{1,0:T(8,128)(2,1)S(1)} collective-permute-done((bf16[64,1792]{1,0:T(8,128)(2,1)S(1)}, bf16[64,1792]{1,0:T(8,128)(2,1)S(1)}, u32[]{:S(2)}, u32[]{:S(2)}) %collective-permute-start.17) | collective-permute-done | bytes 229408 | tf_op jit(solution)/shard_map/ppermute | solution.py:138
  67.8 1.1 %shard_map.81 = (f32[128,1792]{1,0:T(8,128)S(1)}, bf16[128,1792]{1,0:T(8,128)(2,1)S(1)}) custom-call(bf16[256,512]{1,0:T(8,128)(2,1)S(1)} %get-tuple-element.73.hidden_ref, bf16[256,512]{1,0:T(8,128)(2,1)S(1)} %collective-permute-done.27.other_ref, f32[256,128]{1,0:T(8,128)S(1)} %get-tuple-element.74.scale_ref, ...), custom_call_target="tpu_custom_call" | custom-call | flops 939524096 | bytes 4325376 | tf_op jit(solution)/shard_map/pallas_call | solution.py:104
  69.0 1.3 %collective-permute-start.29 = (bf16[128,1792]{1,0:T(8,128)(2,1)S(1)}, bf16[128,1792]{1,0:T(8,128)(2,1)S(1)}, u32[]{:S(2)}, u32[]{:S(2)}) collective-permute-start(bf16[128,1792]{1,0:T(8,128)(2,1)S(1)} %get-tuple-element.76), channel_id=1, source_target_pairs={{0,2},{1,5},{2,0},{3,7},{4,6},{5,1},{6,4},{7,3},{8,10},{9,13},{10,... | collective-permute-start | bytes 1376264 | tf_op jit(solution)/shard_map/ppermute | solution.py:134
  70.4 0.3 collective-permute-start.22
  70.7 1.1 %shard_map.82 = (f32[128,1792]{1,0:T(8,128)S(1)}, bf16[128,1792]{1,0:T(8,128)(2,1)S(1)}) custom-call(bf16[256,512]{1,0:T(8,128)(2,1)S(1)} %get-tuple-element.77.hidden_ref, bf16[256,512]{1,0:T(8,128)(2,1)S(1)} %collective-permute-done.28.other_ref, f32[256,128]{1,0:T(8,128)S(1)} %get-tuple-element.78.scale_ref, ...), custom_call_target="tpu_custom_call" | custom-call | flops 939524096 | bytes 4325376 | tf_op jit(solution)/shard_map/pallas_call | solution.py:104
  71.8 0.9 collective-permute-start.32
  72.7 4.9 %collective-permute-done.29 = bf16[128,1792]{1,0:T(8,128)(2,1)S(1)} collective-permute-done((bf16[128,1792]{1,0:T(8,128)(2,1)S(1)}, bf16[128,1792]{1,0:T(8,128)(2,1)S(1)}, u32[]{:S(2)}, u32[]{:S(2)}) %collective-permute-start.29) | collective-permute-done | bytes 458784 | tf_op jit(solution)/shard_map/ppermute | solution.py:134
  77.6 0.1 convert_add_fusion.1
  77.8 1.1 %collective-permute-start.31 = (bf16[64,1792]{1,0:T(8,128)(2,1)S(1)}, bf16[64,1792]{1,0:T(8,128)(2,1)S(1)}, u32[]{:S(2)}, u32[]{:S(2)}) collective-permute-start(bf16[64,1792]{1,0:T(8,128)(2,1)S(1)} %bitcast.40), channel_id=1, source_target_pairs={{0,4},{1,3},{2,6},{3,1},{4,0},{5,7},{6,2},{7,5},{8,12},{9,11},{10,... | collective-permute-start | bytes 688136 | tf_op jit(solution)/shard_map/ppermute | solution.py:138
  78.8 0.7 collective-permute-done.22
  79.6 0.1 fusion.4
  79.7 0.2 collective-permute-start.30
  79.9 4.9 %collective-permute-done.32 = bf16[128,1792]{1,0:T(8,128)(2,1)S(1)} collective-permute-done((bf16[128,1792]{1,0:T(8,128)(2,1)S(1)}, bf16[128,1792]{1,0:T(8,128)(2,1)S(1)}, u32[]{:S(2)}, u32[]{:S(2)}) %collective-permute-start.32) | collective-permute-done | bytes 458784 | tf_op jit(solution)/shard_map/ppermute | solution.py:134
  84.8 0.1 convert_add_fusion
  85.0 1.3 %collective-permute-start.34 = (bf16[64,1792]{1,0:T(8,128)(2,1)S(1)}, bf16[64,1792]{1,0:T(8,128)(2,1)S(1)}, u32[]{:S(2)}, u32[]{:S(2)}) collective-permute-start(bf16[64,1792]{1,0:T(8,128)(2,1)S(1)} %bitcast.41), channel_id=1, source_target_pairs={{0,4},{1,3},{2,6},{3,1},{4,0},{5,7},{6,2},{7,5},{8,12},{9,11},{10,... | collective-permute-start | bytes 688136 | tf_op jit(solution)/shard_map/ppermute | solution.py:138
  86.3 1.8 %collective-permute-done.30 = bf16[64,1792]{1,0:T(8,128)(2,1)S(1)} collective-permute-done((bf16[64,1792]{1,0:T(8,128)(2,1)S(1)}, bf16[64,1792]{1,0:T(8,128)(2,1)S(1)}, u32[]{:S(2)}, u32[]{:S(2)}) %collective-permute-start.30) | collective-permute-done | bytes 229408 | tf_op jit(solution)/shard_map/ppermute | solution.py:141
  88.0 0.1 fusion.2
  88.2 2.8 %collective-permute-done.34 = bf16[64,1792]{1,0:T(8,128)(2,1)S(1)} collective-permute-done((bf16[64,1792]{1,0:T(8,128)(2,1)S(1)}, bf16[64,1792]{1,0:T(8,128)(2,1)S(1)}, u32[]{:S(2)}, u32[]{:S(2)}) %collective-permute-start.34) | collective-permute-done | bytes 229408 | tf_op jit(solution)/shard_map/ppermute | solution.py:138
  91.0 4.9 %collective-permute-done.33 = bf16[64,1792]{1,0:T(8,128)(2,1)S(1)} collective-permute-done((bf16[64,1792]{1,0:T(8,128)(2,1)S(1)}, bf16[64,1792]{1,0:T(8,128)(2,1)S(1)}, u32[]{:S(2)}, u32[]{:S(2)}) %collective-permute-start.33) | collective-permute-done | bytes 229408 | tf_op jit(solution)/shard_map/ppermute | solution.py:141
  96.0 0.1 fusion
  96.1 0.7 copy-done.1
  (46 shorter events, 0.6 us)
Async XLA Ops:
  2.4 8.8 %copy-start = (bf16[32,3712]{1,0:T(8,128)(2,1)S(1)}, bf16[32,3712]{1,0:T(8,128)(2,1)}, u32[]{:S(2)}) copy-start(bf16[32,3712]{1,0:T(8,128)(2,1)} %shard_map.73) | copy-start | bytes 712708
  2.4 8.8 %collective-permute-start.1 = (bf16[32,3712]{1,0:T(8,128)(2,1)}, bf16[32,3712]{1,0:T(8,128)(2,1)S(1)}, u32[]{:S(2)}, u32[]{:S(2)}) collective-permute-start(bf16[32,3712]{1,0:T(8,128)(2,1)} %shard_map.73), channel_id=1, source_target_pairs={{0,2},{1,5},{2,0},{3,7},{4,6},{5,1},{6,4},{7,3},{8,10},{9,13},{10,... | collective-permute-start | bytes 712712 | tf_op jit(solution)/shard_map/ppermute | solution.py:134
  5.4 9.4 %collective-permute-start = (bf16[32,3712]{1,0:T(8,128)(2,1)}, bf16[32,3712]{1,0:T(8,128)(2,1)S(1)}, u32[]{:S(2)}, u32[]{:S(2)}) collective-permute-start(bf16[32,3712]{1,0:T(8,128)(2,1)} %shard_map.73), channel_id=1, source_target_pairs={{0,8},{2,10},{4,12},{6,14},{8,16},{10,18},{12,20},{14,22},{16,24},... | collective-permute-start | bytes 712712 | tf_op jit(solution)/shard_map/ppermute | solution.py:141
  11.3 11.8 %collective-permute-start.2 = (bf16[64,3712]{1,0:T(8,128)(2,1)S(1)}, bf16[64,3712]{1,0:T(8,128)(2,1)S(1)}, u32[]{:S(2)}, u32[]{:S(2)}) collective-permute-start(bf16[64,3712]{1,0:T(8,128)(2,1)S(1)} %constant_dynamic-update-slice_fusion.refs_0_), channel_id=1, source_target_pairs={{0,4},{1,3},{2,6},{3,1},{4,0},{5,7},{6,2},{7,5},{8,12},{9,11},{10,... | collective-permute-start | bytes 1425416 | tf_op jit(solution)/shard_map/ppermute | solution.py:138
  14.8 8.3 %collective-permute-start.3 = (bf16[32,3712]{1,0:T(8,128)(2,1)S(1)}, bf16[32,3712]{1,0:T(8,128)(2,1)S(1)}, u32[]{:S(2)}, u32[]{:S(2)}) collective-permute-start(bf16[32,3712]{1,0:T(8,128)(2,1)S(1)} %collective-permute-done), channel_id=1, source_target_pairs={{0,8},{2,10},{4,12},{6,14},{8,16},{10,18},{12,20},{14,22},{16,24},... | collective-permute-start | bytes 712712 | tf_op jit(solution)/shard_map/ppermute | solution.py:141
  14.8 8.3 %collective-permute-start.4 = (bf16[32,3712]{1,0:T(8,128)(2,1)S(1)}, bf16[32,3712]{1,0:T(8,128)(2,1)S(1)}, u32[]{:S(2)}, u32[]{:S(2)}) collective-permute-start(bf16[32,3712]{1,0:T(8,128)(2,1)S(1)} %collective-permute-done), channel_id=1, source_target_pairs={{0,2},{1,5},{2,0},{3,7},{4,6},{5,1},{6,4},{7,3},{8,10},{9,13},{10,... | collective-permute-start | bytes 712712 | tf_op jit(solution)/shard_map/ppermute | solution.py:134
  16.3 10.1 %collective-permute-start.7 = (bf16[64,3712]{1,0:T(8,128)(2,1)S(1)}, bf16[64,3712]{1,0:T(8,128)(2,1)S(1)}, u32[]{:S(2)}, u32[]{:S(2)}) collective-permute-start(bf16[64,3712]{1,0:T(8,128)(2,1)S(1)} %constant_dynamic-update-slice_fusion.refs_0_), channel_id=1, source_target_pairs={{0,1},{1,0},{2,3},{3,2},{4,5},{5,4},{6,7},{7,6},{8,9},{9,8},{10,11... | collective-permute-start | bytes 1425416 | tf_op jit(solution)/shard_map/ppermute | solution.py:144
  23.1 3.3 %collective-permute-start.8 = (bf16[64,3712]{1,0:T(8,128)(2,1)S(1)}, bf16[64,3712]{1,0:T(8,128)(2,1)S(1)}, u32[]{:S(2)}, u32[]{:S(2)}) collective-permute-start(bf16[64,3712]{1,0:T(8,128)(2,1)S(1)} %collective-permute-done.2.refs_1_), channel_id=1, source_target_pairs={{0,1},{1,0},{2,3},{3,2},{4,5},{5,4},{6,7},{7,6},{8,9},{9,8},{10,11... | collective-permute-start | bytes 1425416 | tf_op jit(solution)/shard_map/ppermute | solution.py:144
  23.2 11.3 %collective-permute-start.5 = (bf16[64,3712]{1,0:T(8,128)(2,1)S(1)}, bf16[64,3712]{1,0:T(8,128)(2,1)S(1)}, u32[]{:S(2)}, u32[]{:S(2)}) collective-permute-start(bf16[64,3712]{1,0:T(8,128)(2,1)S(1)} %constant_dynamic-update-slice_fusion.2.refs_0_), channel_id=1, source_target_pairs={{0,4},{1,3},{2,6},{3,1},{4,0},{5,7},{6,2},{7,5},{8,12},{9,11},{10,... | collective-permute-start | bytes 1425416 | tf_op jit(solution)/shard_map/ppermute | solution.py:138
  24.3 9.6 %collective-permute-start.6 = (bf16[32,3712]{1,0:T(8,128)(2,1)S(1)}, bf16[32,3712]{1,0:T(8,128)(2,1)S(1)}, u32[]{:S(2)}, u32[]{:S(2)}) collective-permute-start(bf16[32,3712]{1,0:T(8,128)(2,1)S(1)} %collective-permute-done.3), channel_id=1, source_target_pairs={{0,8},{2,10},{4,12},{6,14},{8,16},{10,18},{12,20},{14,22},{16,24},... | collective-permute-start | bytes 712712 | tf_op jit(solution)/shard_map/ppermute | solution.py:141
  25.7 8.8 %collective-permute-start.9 = (bf16[32,3712]{1,0:T(8,128)(2,1)S(1)}, bf16[32,3712]{1,0:T(8,128)(2,1)S(1)}, u32[]{:S(2)}, u32[]{:S(2)}) collective-permute-start(bf16[32,3712]{1,0:T(8,128)(2,1)S(1)} %collective-permute-done.3), channel_id=1, source_target_pairs={{0,2},{1,5},{2,0},{3,7},{4,6},{5,1},{6,4},{7,3},{8,10},{9,13},{10,... | collective-permute-start | bytes 712712 | tf_op jit(solution)/shard_map/ppermute | solution.py:134
  26.4 11.4 %collective-permute-start.10 = (bf16[64,3712]{1,0:T(8,128)(2,1)S(1)}, bf16[64,3712]{1,0:T(8,128)(2,1)S(1)}, u32[]{:S(2)}, u32[]{:S(2)}) collective-permute-start(bf16[64,3712]{1,0:T(8,128)(2,1)S(1)} %constant_dynamic-update-slice_fusion.2.refs_0_), channel_id=1, source_target_pairs={{0,1},{1,0},{2,3},{3,2},{4,5},{5,4},{6,7},{7,6},{8,9},{9,8},{10,11... | collective-permute-start | bytes 1425416 | tf_op jit(solution)/shard_map/ppermute | solution.py:144
  34.5 3.3 %collective-permute-start.11 = (bf16[64,3712]{1,0:T(8,128)(2,1)S(1)}, bf16[64,3712]{1,0:T(8,128)(2,1)S(1)}, u32[]{:S(2)}, u32[]{:S(2)}) collective-permute-start(bf16[64,3712]{1,0:T(8,128)(2,1)S(1)} %collective-permute-done.5.refs_1_), channel_id=1, source_target_pairs={{0,1},{1,0},{2,3},{3,2},{4,5},{5,4},{6,7},{7,6},{8,9},{9,8},{10,11... | collective-permute-start | bytes 1425416 | tf_op jit(solution)/shard_map/ppermute | solution.py:144
  34.8 13.2 %collective-permute-start.15 = (bf16[512,1792]{1,0:T(8,128)(2,1)S(1)}, bf16[512,1792]{1,0:T(8,128)(2,1)S(1)}, u32[]{:S(2)}, u32[]{:S(2)}) collective-permute-start(bf16[512,1792]{1,0:T(8,128)(2,1)S(1)} %get-tuple-element.62), channel_id=1, source_target_pairs={{0,1},{1,0},{2,3},{3,2},{4,5},{5,4},{6,7},{7,6},{8,9},{9,8},{10,11... | collective-permute-start | bytes 5505032 | tf_op jit(solution)/shard_map/ppermute | solution.py:144
  35.1 11.2 %collective-permute-start.12 = (bf16[64,3712]{1,0:T(8,128)(2,1)S(1)}, bf16[64,3712]{1,0:T(8,128)(2,1)S(1)}, u32[]{:S(2)}, u32[]{:S(2)}) collective-permute-start(bf16[64,3712]{1,0:T(8,128)(2,1)S(1)} %constant_dynamic-update-slice_fusion.4.refs_0_), channel_id=1, source_target_pairs={{0,4},{1,3},{2,6},{3,1},{4,0},{5,7},{6,2},{7,5},{8,12},{9,11},{10,... | collective-permute-start | bytes 1425416 | tf_op jit(solution)/shard_map/ppermute | solution.py:138
  36.1 10.2 %collective-permute-start.13 = (bf16[32,3712]{1,0:T(8,128)(2,1)S(1)}, bf16[32,3712]{1,0:T(8,128)(2,1)S(1)}, u32[]{:S(2)}, u32[]{:S(2)}) collective-permute-start(bf16[32,3712]{1,0:T(8,128)(2,1)S(1)} %collective-permute-done.6), channel_id=1, source_target_pairs={{0,2},{1,5},{2,0},{3,7},{4,6},{5,1},{6,4},{7,3},{8,10},{9,13},{10,... | collective-permute-start | bytes 712712 | tf_op jit(solution)/shard_map/ppermute | solution.py:134
  37.7 13.3 %collective-permute-start.18 = (bf16[64,3712]{1,0:T(8,128)(2,1)S(1)}, bf16[64,3712]{1,0:T(8,128)(2,1)S(1)}, u32[]{:S(2)}, u32[]{:S(2)}) collective-permute-start(bf16[64,3712]{1,0:T(8,128)(2,1)S(1)} %constant_dynamic-update-slice_fusion.4.refs_0_), channel_id=1, source_target_pairs={{0,1},{1,0},{2,3},{3,2},{4,5},{5,4},{6,7},{7,6},{8,9},{9,8},{10,11... | collective-permute-start | bytes 1425416 | tf_op jit(solution)/shard_map/ppermute | solution.py:144
  46.3 4.8 %collective-permute-start.19 = (bf16[64,3712]{1,0:T(8,128)(2,1)S(1)}, bf16[64,3712]{1,0:T(8,128)(2,1)S(1)}, u32[]{:S(2)}, u32[]{:S(2)}) collective-permute-start(bf16[64,3712]{1,0:T(8,128)(2,1)S(1)} %collective-permute-done.12.refs_1_), channel_id=1, source_target_pairs={{0,1},{1,0},{2,3},{3,2},{4,5},{5,4},{6,7},{7,6},{8,9},{9,8},{10,11... | collective-permute-start | bytes 1425416 | tf_op jit(solution)/shard_map/ppermute | solution.py:144
  46.4 2.2 %collective-permute-start.14 = (bf16[256,512]{1,0:T(8,128)(2,1)S(1)}, bf16[256,512]{1,0:T(8,128)(2,1)S(1)}, u32[]{:S(2)}, u32[]{:S(2)}) collective-permute-start(bf16[256,512]{1,0:T(8,128)(2,1)S(1)} %get-tuple-element.60.hidden_ref), channel_id=1, source_target_pairs={{0,1},{1,0},{2,3},{3,2},{4,5},{5,4},{6,7},{7,6},{8,9},{9,8},{10,11... | collective-permute-start | bytes 786440 | tf_op jit(solution)/shard_map/ppermute | solution.py:144
  46.9 11.6 %collective-permute-start.24 = (bf16[64,3712]{1,0:T(8,128)(2,1)S(1)}, bf16[64,3712]{1,0:T(8,128)(2,1)S(1)}, u32[]{:S(2)}, u32[]{:S(2)}) collective-permute-start(bf16[64,3712]{1,0:T(8,128)(2,1)S(1)} %constant_dynamic-update-slice_fusion.6.refs_0_), channel_id=1, source_target_pairs={{0,4},{1,3},{2,6},{3,1},{4,0},{5,7},{6,2},{7,5},{8,12},{9,11},{10,... | collective-permute-start | bytes 1425416 | tf_op jit(solution)/shard_map/ppermute | solution.py:138
  49.7 9.8 %collective-permute-start.16 = (bf16[128,1792]{1,0:T(8,128)(2,1)S(1)}, bf16[128,1792]{1,0:T(8,128)(2,1)S(1)}, u32[]{:S(2)}, u32[]{:S(2)}) collective-permute-start(bf16[128,1792]{1,0:T(8,128)(2,1)S(1)} %get-tuple-element.64), channel_id=1, source_target_pairs={{0,2},{1,5},{2,0},{3,7},{4,6},{5,1},{6,4},{7,3},{8,10},{9,13},{10,... | collective-permute-start | bytes 1376264 | tf_op jit(solution)/shard_map/ppermute | solution.py:134
  53.2 1.6 %collective-permute-start.20 = (bf16[256,512]{1,0:T(8,128)(2,1)S(1)}, bf16[256,512]{1,0:T(8,128)(2,1)S(1)}, u32[]{:S(2)}, u32[]{:S(2)}) collective-permute-start(bf16[256,512]{1,0:T(8,128)(2,1)S(1)} %get-tuple-element.67.hidden_ref), channel_id=1, source_target_pairs={{0,1},{1,0},{2,3},{3,2},{4,5},{5,4},{6,7},{7,6},{8,9},{9,8},{10,11... | collective-permute-start | bytes 786440 | tf_op jit(solution)/shard_map/ppermute | solution.py:144
  53.2 17.4 %collective-permute-start.28 = (bf16[256,512]{1,0:T(8,128)(2,1)S(1)}, bf16[256,512]{1,0:T(8,128)(2,1)S(1)}, u32[]{:S(2)}, u32[]{:S(2)}) collective-permute-start(bf16[256,512]{1,0:T(8,128)(2,1)S(1)} %get-tuple-element.77.hidden_ref), channel_id=1, source_target_pairs={{0,1},{1,0},{2,3},{3,2},{4,5},{5,4},{6,7},{7,6},{8,9},{9,8},{10,11... | collective-permute-start | bytes 786440 | tf_op jit(solution)/shard_map/ppermute | solution.py:144
  53.7 7.1 %collective-permute-start.25 = (bf16[64,3712]{1,0:T(8,128)(2,1)S(1)}, bf16[64,3712]{1,0:T(8,128)(2,1)S(1)}, u32[]{:S(2)}, u32[]{:S(2)}) collective-permute-start(bf16[64,3712]{1,0:T(8,128)(2,1)S(1)} %constant_dynamic-update-slice_fusion.6.refs_0_), channel_id=1, source_target_pairs={{0,1},{1,0},{2,3},{3,2},{4,5},{5,4},{6,7},{7,6},{8,9},{9,8},{10,11... | collective-permute-start | bytes 1425416 | tf_op jit(solution)/shard_map/ppermute | solution.py:144
  55.9 9.6 %collective-permute-start.21 = (bf16[128,1792]{1,0:T(8,128)(2,1)S(1)}, bf16[128,1792]{1,0:T(8,128)(2,1)S(1)}, u32[]{:S(2)}, u32[]{:S(2)}) collective-permute-start(bf16[128,1792]{1,0:T(8,128)(2,1)S(1)} %get-tuple-element.70), channel_id=1, source_target_pairs={{0,2},{1,5},{2,0},{3,7},{4,6},{5,1},{6,4},{7,3},{8,10},{9,13},{10,... | collective-permute-start | bytes 1376264 | tf_op jit(solution)/shard_map/ppermute | solution.py:134
  58.5 2.3 %collective-permute-start.26 = (bf16[64,3712]{1,0:T(8,128)(2,1)S(1)}, bf16[64,3712]{1,0:T(8,128)(2,1)S(1)}, u32[]{:S(2)}, u32[]{:S(2)}) collective-permute-start(bf16[64,3712]{1,0:T(8,128)(2,1)S(1)} %collective-permute-done.24.refs_1_), channel_id=1, source_target_pairs={{0,1},{1,0},{2,3},{3,2},{4,5},{5,4},{6,7},{7,6},{8,9},{9,8},{10,11... | collective-permute-start | bytes 1425416 | tf_op jit(solution)/shard_map/ppermute | solution.py:144
  59.7 8.1 %collective-permute-start.17 = (bf16[64,1792]{1,0:T(8,128)(2,1)S(1)}, bf16[64,1792]{1,0:T(8,128)(2,1)S(1)}, u32[]{:S(2)}, u32[]{:S(2)}) collective-permute-start(bf16[64,1792]{1,0:T(8,128)(2,1)S(1)} %bitcast.39), channel_id=1, source_target_pairs={{0,4},{1,3},{2,6},{3,1},{4,0},{5,7},{6,2},{7,5},{8,12},{9,11},{10,... | collective-permute-start | bytes 688136 | tf_op jit(solution)/shard_map/ppermute | solution.py:138
  62.9 4.9 %collective-permute-start.27 = (bf16[256,512]{1,0:T(8,128)(2,1)S(1)}, bf16[256,512]{1,0:T(8,128)(2,1)S(1)}, u32[]{:S(2)}, u32[]{:S(2)}) collective-permute-start(bf16[256,512]{1,0:T(8,128)(2,1)S(1)} %get-tuple-element.73.hidden_ref), channel_id=1, source_target_pairs={{0,1},{1,0},{2,3},{3,2},{4,5},{5,4},{6,7},{7,6},{8,9},{9,8},{10,11... | collective-permute-start | bytes 786440 | tf_op jit(solution)/shard_map/ppermute | solution.py:144
  65.7 13.2 %collective-permute-start.23 = (bf16[64,1792]{1,0:T(8,128)(2,1)S(1)}, bf16[64,1792]{1,0:T(8,128)(2,1)S(1)}, u32[]{:S(2)}, u32[]{:S(2)}) collective-permute-start(bf16[64,1792]{1,0:T(8,128)(2,1)S(1)} %bitcast.38), channel_id=1, source_target_pairs={{0,4},{1,3},{2,6},{3,1},{4,0},{5,7},{6,2},{7,5},{8,12},{9,11},{10,... | collective-permute-start | bytes 688136 | tf_op jit(solution)/shard_map/ppermute | solution.py:138
  69.0 8.7 %collective-permute-start.29 = (bf16[128,1792]{1,0:T(8,128)(2,1)S(1)}, bf16[128,1792]{1,0:T(8,128)(2,1)S(1)}, u32[]{:S(2)}, u32[]{:S(2)}) collective-permute-start(bf16[128,1792]{1,0:T(8,128)(2,1)S(1)} %get-tuple-element.76), channel_id=1, source_target_pairs={{0,2},{1,5},{2,0},{3,7},{4,6},{5,1},{6,4},{7,3},{8,10},{9,13},{10,... | collective-permute-start | bytes 1376264 | tf_op jit(solution)/shard_map/ppermute | solution.py:134
  70.4 9.2 %collective-permute-start.22 = (bf16[64,1792]{1,0:T(8,128)(2,1)S(1)}, bf16[64,1792]{1,0:T(8,128)(2,1)S(1)}, u32[]{:S(2)}, u32[]{:S(2)}) collective-permute-start(bf16[64,1792]{1,0:T(8,128)(2,1)S(1)} %fusion.5), channel_id=1, source_target_pairs={{0,8},{2,10},{4,12},{6,14},{8,16},{10,18},{12,20},{14,22},{16,24},... | collective-permute-start | bytes 688136 | tf_op jit(solution)/shard_map/ppermute | solution.py:141
  71.8 13.0 %collective-permute-start.32 = (bf16[128,1792]{1,0:T(8,128)(2,1)S(1)}, bf16[128,1792]{1,0:T(8,128)(2,1)S(1)}, u32[]{:S(2)}, u32[]{:S(2)}) collective-permute-start(bf16[128,1792]{1,0:T(8,128)(2,1)S(1)} %get-tuple-element.79), channel_id=1, source_target_pairs={{0,2},{1,5},{2,0},{3,7},{4,6},{5,1},{6,4},{7,3},{8,10},{9,13},{10,... | collective-permute-start | bytes 1376264 | tf_op jit(solution)/shard_map/ppermute | solution.py:134
  77.8 8.5 %collective-permute-start.31 = (bf16[64,1792]{1,0:T(8,128)(2,1)S(1)}, bf16[64,1792]{1,0:T(8,128)(2,1)S(1)}, u32[]{:S(2)}, u32[]{:S(2)}) collective-permute-start(bf16[64,1792]{1,0:T(8,128)(2,1)S(1)} %bitcast.40), channel_id=1, source_target_pairs={{0,4},{1,3},{2,6},{3,1},{4,0},{5,7},{6,2},{7,5},{8,12},{9,11},{10,... | collective-permute-start | bytes 688136 | tf_op jit(solution)/shard_map/ppermute | solution.py:138
  79.7 8.4 %collective-permute-start.30 = (bf16[64,1792]{1,0:T(8,128)(2,1)S(1)}, bf16[64,1792]{1,0:T(8,128)(2,1)S(1)}, u32[]{:S(2)}, u32[]{:S(2)}) collective-permute-start(bf16[64,1792]{1,0:T(8,128)(2,1)S(1)} %fusion.4), channel_id=1, source_target_pairs={{0,8},{2,10},{4,12},{6,14},{8,16},{10,18},{12,20},{14,22},{16,24},... | collective-permute-start | bytes 688136 | tf_op jit(solution)/shard_map/ppermute | solution.py:141
  85.0 6.1 %collective-permute-start.34 = (bf16[64,1792]{1,0:T(8,128)(2,1)S(1)}, bf16[64,1792]{1,0:T(8,128)(2,1)S(1)}, u32[]{:S(2)}, u32[]{:S(2)}) collective-permute-start(bf16[64,1792]{1,0:T(8,128)(2,1)S(1)} %bitcast.41), channel_id=1, source_target_pairs={{0,4},{1,3},{2,6},{3,1},{4,0},{5,7},{6,2},{7,5},{8,12},{9,11},{10,... | collective-permute-start | bytes 688136 | tf_op jit(solution)/shard_map/ppermute | solution.py:138
  88.1 7.9 %collective-permute-start.33 = (bf16[64,1792]{1,0:T(8,128)(2,1)S(1)}, bf16[64,1792]{1,0:T(8,128)(2,1)S(1)}, u32[]{:S(2)}, u32[]{:S(2)}) collective-permute-start(bf16[64,1792]{1,0:T(8,128)(2,1)S(1)} %fusion.2), channel_id=1, source_target_pairs={{0,8},{2,10},{4,12},{6,14},{8,16},{10,18},{12,20},{14,22},{16,24},... | collective-permute-start | bytes 688136 | tf_op jit(solution)/shard_map/ppermute | solution.py:141
  96.1 0.7 copy-start.1

commit v5 on v4

--- a/solution.py
+++ b/solution.py
@@ -218,7 +218,7 @@
         ties += [came[p + 1]] if 1 <= p < planes - 1 else []
         ties += [held[p - 2][0]] if p >= 2 else []
         pairs[p] = join(after(came[p], *ties), near[p])
-        fars[p] = second_link(pairs[p])
+        fars[p] = shift(fars[2], 1) if p == 3 else second_link(pairs[p])
         if p == 0:
             came[1] = after(came[1], pairs[0])
         if p + 1 < planes:
@@ -238,7 +238,7 @@
     add_up(0, passes[planes - 1])
     carried = None
     for p in range(1, planes):
-        total = parts[p][0] + after(parts[p][1], passes[(p + 1) % planes]).astype(F32)
+        total = parts[p][0] + after(parts[p][1], *([passes[p + 1]] if p + 1 < planes else [])).astype(F32)
         passing = (total if carried is None else carried.astype(F32) + total).astype(BF16)
         carried = shift(passing, 1)
     total = carried.astype(F32) + parts[0][0] + parts[0][1].astype(F32)

time: 97 us -> 96.6 us (level)
  starting transfers between devices: 27.1 us -> 24.8 us
  waiting for transfers between devices: 48.3 us -> 50.2 us
    ppermute x6 -> x7, waiting for transfers between devices: 21.6 us -> 25.1 us  [shift(): lax.ppermute(a, 'ep', [(e, (e + QUAD * steps) % ep) for e in range(ep)])]
    ppermute x8 -> x7, waiting for transfers between devices: 12.7 us -> 11.1 us  [second_link(): return lax.ppermute(a, ('ep', 'tp'), pairs)]
    ppermute x8, waiting for transfers between devices: 12.5 us -> 11.1 us  [first_link(): return lax.ppermute(a, ('ep', 'tp'), pairs)]
    ppermute x13, waiting for transfers between devices: 1.65 us -> 2.92 us  [other_core(): return lax.ppermute(a, 'tp', [(0, 1), (1, 0)])]
    ppermute x8 -> x7, starting transfers between devices: 9.28 us -> 8.05 us  [second_link(): return lax.ppermute(a, ('ep', 'tp'), pairs)]
    ppermute x6 -> x7, starting transfers between devices: 3.58 us -> 3.5 us  [shift(): lax.ppermute(a, 'ep', [(e, (e + QUAD * steps) % ep) for e in range(ep)])]
  transfers between devices with their start and end apart: 35 -> 35, of which waited for: 17 -> 16; matrix products, arithmetic and copies ran while one was open for 1% -> 1% of each run, Pallas kernels for 18% -> 18%
where the time goes in v5:
time: 96.6 us; the launch traced here: 96.4 us
  waiting for transfers between devices  50.2 us (52%)
  starting transfers between devices  24.8 us (26%)
  Pallas kernels  19.4 us (20%)
  local copies, waits for them, and re-layouts  1.09 us (1%)
    ppermute x7, waiting for transfers between devices, shift(): lax.ppermute(a, 'ep', [(e, (e + QUAD * steps) % ep) for e in range(ep)])  25.1 us
    pallas_call x10, Pallas kernels, call(): pl.pallas_call(kernel, out_shape=outs, in_specs=[pl.BlockSpec(memory_spac...  19.4 us
    ppermute x8, starting transfers between devices, first_link(): return lax.ppermute(a, ('ep', 'tp'), pairs)  11.2 us
    ppermute x7, waiting for transfers between devices, second_link(): return lax.ppermute(a, ('ep', 'tp'), pairs)  11.1 us
    ppermute x8, waiting for transfers between devices, first_link(): return lax.ppermute(a, ('ep', 'tp'), pairs)  11.1 us
    ppermute x7, starting transfers between devices, second_link(): return lax.ppermute(a, ('ep', 'tp'), pairs)  8.05 us
    ppermute x7, starting transfers between devices, shift(): lax.ppermute(a, 'ep', [(e, (e + QUAD * steps) % ep) for e in range(ep)])  3.5 us
    ppermute x13, waiting for transfers between devices, other_core(): return lax.ppermute(a, 'tp', [(0, 1), (1, 0)])  2.92 us
  transfers between devices with their start and end apart: 35, of which 16 were waited for; matrix products, arithmetic and copies ran while one was open for 1% of the time, Pallas kernels for 18%

profile of v5, /device:TPU:0, one launch (start us, length us, event | category | flops | bytes accessed | tf_op | source)
XLA Modules:
  0.0 96.4 jit_solution(17069233443387670754)
XLA Ops:
  0.0 2.4 %shard_map.73 = bf16[32,3712]{1,0:T(8,128)(2,1)} custom-call(bf16[64,3584]{1,0:T(8,128)(2,1)} %tokens_ref.1, s32[16]{0:T(128)} %copied_ref.1, f32[8,64]{1,0:T(8,128)} %bitcast.42, s32[8,64]{1,0:T(8,128)} %bitcast.43), custom_call_target="tpu_custom_call" | custom-call | bytes 462912 | tf_op jit(solution)/shard_map/pallas_call | solution.py:104
  2.4 3.0 %collective-permute-start.1 = (bf16[32,3712]{1,0:T(8,128)(2,1)}, bf16[32,3712]{1,0:T(8,128)(2,1)S(1)}, u32[]{:S(2)}, u32[]{:S(2)}) collective-permute-start(bf16[32,3712]{1,0:T(8,128)(2,1)} %shard_map.73), channel_id=1, source_target_pairs={{0,2},{1,5},{2,0},{3,7},{4,6},{5,1},{6,4},{7,3},{8,10},{9,13},{10,... | collective-permute-start | bytes 712712 | tf_op jit(solution)/shard_map/ppermute | solution.py:134
  5.4 1.6 %collective-permute-start = (bf16[32,3712]{1,0:T(8,128)(2,1)}, bf16[32,3712]{1,0:T(8,128)(2,1)S(1)}, u32[]{:S(2)}, u32[]{:S(2)}) collective-permute-start(bf16[32,3712]{1,0:T(8,128)(2,1)} %shard_map.73), channel_id=1, source_target_pairs={{0,8},{2,10},{4,12},{6,14},{8,16},{10,18},{12,20},{14,22},{16,24},... | collective-permute-start | bytes 712712 | tf_op jit(solution)/shard_map/ppermute | solution.py:141
  7.0 4.2 %shard_map.74 = (bf16[3584,512]{1,0:T(8,128)(2,1)S(1)}, bf16[3584,512]{1,0:T(8,128)(2,1)S(1)}, bf16[512,1792]{1,0:T(8,128)(2,1)S(1)}, bf16[512,1792]{1,0:T(8,128)(2,1)S(1)}) custom-call(bf16[1,3584,512]{2,1,0:T(8,128)(2,1)} %gate_hbm, bf16[1,3584,512]{2,1,0:T(8,128)(2,1)} %up_hbm, bf16[1,512,3584]{2,1,0:T(8,128)(2,1)} %down_hbm), custom_call_target="tpu_custom_call" | custom-call | bytes 11010048 | tf_op jit(solution)/shard_map/pallas_call | solution.py:104
  11.3 1.6 %collective-permute-start.2 = (bf16[64,3712]{1,0:T(8,128)(2,1)S(1)}, bf16[64,3712]{1,0:T(8,128)(2,1)S(1)}, u32[]{:S(2)}, u32[]{:S(2)}) collective-permute-start(bf16[64,3712]{1,0:T(8,128)(2,1)S(1)} %constant_dynamic-update-slice_fusion.refs_0_), channel_id=1, source_target_pairs={{0,4},{1,3},{2,6},{3,1},{4,0},{5,7},{6,2},{7,5},{8,12},{9,11},{10,... | collective-permute-start | bytes 1425416 | tf_op jit(solution)/shard_map/ppermute | solution.py:138
  12.8 1.9 %collective-permute-done = bf16[32,3712]{1,0:T(8,128)(2,1)S(1)} collective-permute-done((bf16[32,3712]{1,0:T(8,128)(2,1)}, bf16[32,3712]{1,0:T(8,128)(2,1)S(1)}, u32[]{:S(2)}, u32[]{:S(2)}) %collective-permute-start) | collective-permute-done | bytes 237600 | tf_op jit(solution)/shard_map/ppermute | solution.py:141
  14.8 1.5 %collective-permute-start.4 = (bf16[32,3712]{1,0:T(8,128)(2,1)S(1)}, bf16[32,3712]{1,0:T(8,128)(2,1)S(1)}, u32[]{:S(2)}, u32[]{:S(2)}) collective-permute-start(bf16[32,3712]{1,0:T(8,128)(2,1)S(1)} %collective-permute-done), channel_id=1, source_target_pairs={{0,2},{1,5},{2,0},{3,7},{4,6},{5,1},{6,4},{7,3},{8,10},{9,13},{10,... | collective-permute-start | bytes 712712 | tf_op jit(solution)/shard_map/ppermute | solution.py:134
  16.3 6.8 %collective-permute-done.3 = bf16[32,3712]{1,0:T(8,128)(2,1)S(1)} collective-permute-done((bf16[32,3712]{1,0:T(8,128)(2,1)S(1)}, bf16[32,3712]{1,0:T(8,128)(2,1)S(1)}, u32[]{:S(2)}, u32[]{:S(2)}) %collective-permute-start.3) | collective-permute-done | bytes 237600 | tf_op jit(solution)/shard_map/ppermute | solution.py:141
  23.1 0.1 collective-permute-start.8
  23.2 1.1 %collective-permute-start.5 = (bf16[64,3712]{1,0:T(8,128)(2,1)S(1)}, bf16[64,3712]{1,0:T(8,128)(2,1)S(1)}, u32[]{:S(2)}, u32[]{:S(2)}) collective-permute-start(bf16[64,3712]{1,0:T(8,128)(2,1)S(1)} %constant_dynamic-update-slice_fusion.2.refs_0_), channel_id=1, source_target_pairs={{0,4},{1,3},{2,6},{3,1},{4,0},{5,7},{6,2},{7,5},{8,12},{9,11},{10,... | collective-permute-start | bytes 1425416 | tf_op jit(solution)/shard_map/ppermute | solution.py:138
  24.3 1.4 %collective-permute-start.6 = (bf16[32,3712]{1,0:T(8,128)(2,1)S(1)}, bf16[32,3712]{1,0:T(8,128)(2,1)S(1)}, u32[]{:S(2)}, u32[]{:S(2)}) collective-permute-start(bf16[32,3712]{1,0:T(8,128)(2,1)S(1)} %collective-permute-done.3), channel_id=1, source_target_pairs={{0,8},{2,10},{4,12},{6,14},{8,16},{10,18},{12,20},{14,22},{16,24},... | collective-permute-start | bytes 712712 | tf_op jit(solution)/shard_map/ppermute | solution.py:141
  25.7 0.7 collective-permute-start.9
  26.4 2.1 %shard_map.75 = (bf16[256,512]{1,0:T(8,128)(2,1)S(1)}, f32[256,128]{1,0:T(8,128)S(1)}) custom-call(bf16[64,3712]{1,0:T(8,128)(2,1)S(1)} %constant_dynamic-update-slice_fusion.refs_0_, bf16[64,3712]{1,0:T(8,128)(2,1)S(1)} %collective-permute-done.2.refs_1_, bf16[64,3712]{1,0:T(8,128)(2,1)S(1)} %collective-permute-done.7.refs_2_, ...), custom_call_target="tpu_custom_call" | custom-call | flops 1879048192 | bytes 9240576 | tf_op jit(solution)/shard_map/pallas_call | solution.py:104
  28.5 5.4 %collective-permute-done.6 = bf16[32,3712]{1,0:T(8,128)(2,1)S(1)} collective-permute-done((bf16[32,3712]{1,0:T(8,128)(2,1)S(1)}, bf16[32,3712]{1,0:T(8,128)(2,1)S(1)}, u32[]{:S(2)}, u32[]{:S(2)}) %collective-permute-start.6) | collective-permute-done | bytes 237600 | tf_op jit(solution)/shard_map/ppermute | solution.py:141
  33.9 0.5 collective-permute-done.5.refs_1_
  34.5 0.3 collective-permute-start.11
  34.8 0.3 collective-permute-start.15
  35.1 1.0 %collective-permute-start.12 = (bf16[64,3712]{1,0:T(8,128)(2,1)S(1)}, bf16[64,3712]{1,0:T(8,128)(2,1)S(1)}, u32[]{:S(2)}, u32[]{:S(2)}) collective-permute-start(bf16[64,3712]{1,0:T(8,128)(2,1)S(1)} %constant_dynamic-update-slice_fusion.4.refs_0_), channel_id=1, source_target_pairs={{0,4},{1,3},{2,6},{3,1},{4,0},{5,7},{6,2},{7,5},{8,12},{9,11},{10,... | collective-permute-start | bytes 1425416 | tf_op jit(solution)/shard_map/ppermute | solution.py:138
  36.1 1.7 %collective-permute-start.13 = (bf16[32,3712]{1,0:T(8,128)(2,1)S(1)}, bf16[32,3712]{1,0:T(8,128)(2,1)S(1)}, u32[]{:S(2)}, u32[]{:S(2)}) collective-permute-start(bf16[32,3712]{1,0:T(8,128)(2,1)S(1)} %collective-permute-done.6), channel_id=1, source_target_pairs={{0,2},{1,5},{2,0},{3,7},{4,6},{5,1},{6,4},{7,3},{8,10},{9,13},{10,... | collective-permute-start | bytes 712712 | tf_op jit(solution)/shard_map/ppermute | solution.py:134
  37.8 2.1 %shard_map.76 = (bf16[256,512]{1,0:T(8,128)(2,1)S(1)}, f32[256,128]{1,0:T(8,128)S(1)}) custom-call(bf16[64,3712]{1,0:T(8,128)(2,1)S(1)} %constant_dynamic-update-slice_fusion.2.refs_0_, bf16[64,3712]{1,0:T(8,128)(2,1)S(1)} %collective-permute-done.5.refs_1_, bf16[64,3712]{1,0:T(8,128)(2,1)S(1)} %collective-permute-done.10.refs_2_, ...), custom_call_target="tpu_custom_call" | custom-call | flops 1879048192 | bytes 9240576 | tf_op jit(solution)/shard_map/pallas_call | solution.py:104
  39.8 6.4 %collective-permute-done.12.refs_1_ = bf16[64,3712]{1,0:T(8,128)(2,1)S(1)} collective-permute-done((bf16[64,3712]{1,0:T(8,128)(2,1)S(1)}, bf16[64,3712]{1,0:T(8,128)(2,1)S(1)}, u32[]{:S(2)}, u32[]{:S(2)}) %collective-permute-start.12) | collective-permute-done | bytes 475168 | tf_op jit(solution)/shard_map/ppermute | solution.py:138
  46.3 0.1 collective-permute-start.19
  46.4 0.5 collective-permute-start.14
  46.9 0.3 collective-permute-start.24
  47.2 1.4 %collective-permute-done.14.other_ref = bf16[256,512]{1,0:T(8,128)(2,1)S(1)} collective-permute-done((bf16[256,512]{1,0:T(8,128)(2,1)S(1)}, bf16[256,512]{1,0:T(8,128)(2,1)S(1)}, u32[]{:S(2)}, u32[]{:S(2)}) %collective-permute-start.14) | collective-permute-done | bytes 262176 | tf_op jit(solution)/shard_map/ppermute | solution.py:144
  48.6 1.1 %shard_map.77 = (f32[128,1792]{1,0:T(8,128)S(1)}, bf16[128,1792]{1,0:T(8,128)(2,1)S(1)}) custom-call(bf16[256,512]{1,0:T(8,128)(2,1)S(1)} %get-tuple-element.59.hidden_ref, bf16[256,512]{1,0:T(8,128)(2,1)S(1)} %collective-permute-done.14.other_ref, f32[256,128]{1,0:T(8,128)S(1)} %get-tuple-element.60.scale_ref, ...), custom_call_target="tpu_custom_call" | custom-call | flops 939524096 | bytes 4325376 | tf_op jit(solution)/shard_map/pallas_call | solution.py:104
  49.7 1.3 %collective-permute-start.16 = (bf16[128,1792]{1,0:T(8,128)(2,1)S(1)}, bf16[128,1792]{1,0:T(8,128)(2,1)S(1)}, u32[]{:S(2)}, u32[]{:S(2)}) collective-permute-start(bf16[128,1792]{1,0:T(8,128)(2,1)S(1)} %get-tuple-element.63), channel_id=1, source_target_pairs={{0,2},{1,5},{2,0},{3,7},{4,6},{5,1},{6,4},{7,3},{8,10},{9,13},{10,... | collective-permute-start | bytes 1376264 | tf_op jit(solution)/shard_map/ppermute | solution.py:134
  51.1 2.1 %shard_map.78 = (bf16[256,512]{1,0:T(8,128)(2,1)S(1)}, f32[256,128]{1,0:T(8,128)S(1)}) custom-call(bf16[64,3712]{1,0:T(8,128)(2,1)S(1)} %constant_dynamic-update-slice_fusion.4.refs_0_, bf16[64,3712]{1,0:T(8,128)(2,1)S(1)} %collective-permute-done.12.refs_1_, bf16[64,3712]{1,0:T(8,128)(2,1)S(1)} %collective-permute-done.18.refs_2_, ...), custom_call_target="tpu_custom_call" | custom-call | flops 1879048192 | bytes 9240576 | tf_op jit(solution)/shard_map/pallas_call | solution.py:104
  53.2 0.1 collective-permute-start.20
  53.2 0.5 collective-permute-start.28
  53.7 0.1 collective-permute-start.25
  53.8 0.9 collective-permute-done.20.other_ref
  54.8 1.1 %shard_map.79 = (f32[128,1792]{1,0:T(8,128)S(1)}, bf16[128,1792]{1,0:T(8,128)(2,1)S(1)}) custom-call(bf16[256,512]{1,0:T(8,128)(2,1)S(1)} %get-tuple-element.66.hidden_ref, bf16[256,512]{1,0:T(8,128)(2,1)S(1)} %collective-permute-done.20.other_ref, f32[256,128]{1,0:T(8,128)S(1)} %get-tuple-element.67.scale_ref, ...), custom_call_target="tpu_custom_call" | custom-call | flops 939524096 | bytes 4325376 | tf_op jit(solution)/shard_map/pallas_call | solution.py:104
  55.9 0.8 collective-permute-start.21
  56.7 4.8 %collective-permute-done.24.refs_1_ = bf16[64,3712]{1,0:T(8,128)(2,1)S(1)} collective-permute-done((bf16[64,3712]{1,0:T(8,128)(2,1)S(1)}, bf16[64,3712]{1,0:T(8,128)(2,1)S(1)}, u32[]{:S(2)}, u32[]{:S(2)}) %collective-permute-start.24) | collective-permute-done | bytes 475168 | tf_op jit(solution)/shard_map/ppermute | solution.py:141
  61.6 0.1 convert_add_fusion.3
  61.7 1.1 %collective-permute-start.17 = (bf16[64,1792]{1,0:T(8,128)(2,1)S(1)}, bf16[64,1792]{1,0:T(8,128)(2,1)S(1)}, u32[]{:S(2)}, u32[]{:S(2)}) collective-permute-start(bf16[64,1792]{1,0:T(8,128)(2,1)S(1)} %bitcast.39), channel_id=1, source_target_pairs={{0,4},{1,3},{2,6},{3,1},{4,0},{5,7},{6,2},{7,5},{8,12},{9,11},{10,... | collective-permute-start | bytes 688136 | tf_op jit(solution)/shard_map/ppermute | solution.py:138
  62.8 0.6 collective-permute-done.26.refs_3_
  63.4 2.1 %shard_map.80 = (bf16[256,512]{1,0:T(8,128)(2,1)S(1)}, f32[256,128]{1,0:T(8,128)S(1)}) custom-call(bf16[64,3712]{1,0:T(8,128)(2,1)S(1)} %constant_dynamic-update-slice_fusion.6.refs_0_, bf16[64,3712]{1,0:T(8,128)(2,1)S(1)} %collective-permute-done.24.refs_1_, bf16[64,3712]{1,0:T(8,128)(2,1)S(1)} %collective-permute-done.25.refs_2_, ...), custom_call_target="tpu_custom_call" | custom-call | flops 1879048192 | bytes 9240576 | tf_op jit(solution)/shard_map/pallas_call | solution.py:104
  65.5 0.2 collective-permute-start.27
  65.7 0.1 convert_add_fusion.2
  65.8 1.1 %collective-permute-start.23 = (bf16[64,1792]{1,0:T(8,128)(2,1)S(1)}, bf16[64,1792]{1,0:T(8,128)(2,1)S(1)}, u32[]{:S(2)}, u32[]{:S(2)}) collective-permute-start(bf16[64,1792]{1,0:T(8,128)(2,1)S(1)} %bitcast.38), channel_id=1, source_target_pairs={{0,4},{1,3},{2,6},{3,1},{4,0},{5,7},{6,2},{7,5},{8,12},{9,11},{10,... | collective-permute-start | bytes 688136 | tf_op jit(solution)/shard_map/ppermute | solution.py:138
  66.9 0.9 collective-permute-done.17
  67.8 1.1 %shard_map.81 = (f32[128,1792]{1,0:T(8,128)S(1)}, bf16[128,1792]{1,0:T(8,128)(2,1)S(1)}) custom-call(bf16[256,512]{1,0:T(8,128)(2,1)S(1)} %get-tuple-element.72.hidden_ref, bf16[256,512]{1,0:T(8,128)(2,1)S(1)} %collective-permute-done.27.other_ref, f32[256,128]{1,0:T(8,128)S(1)} %get-tuple-element.73.scale_ref, ...), custom_call_target="tpu_custom_call" | custom-call | flops 939524096 | bytes 4325376 | tf_op jit(solution)/shard_map/pallas_call | solution.py:104
  68.9 1.4 %collective-permute-start.29 = (bf16[128,1792]{1,0:T(8,128)(2,1)S(1)}, bf16[128,1792]{1,0:T(8,128)(2,1)S(1)}, u32[]{:S(2)}, u32[]{:S(2)}) collective-permute-start(bf16[128,1792]{1,0:T(8,128)(2,1)S(1)} %get-tuple-element.75), channel_id=1, source_target_pairs={{0,2},{1,5},{2,0},{3,7},{4,6},{5,1},{6,4},{7,3},{8,10},{9,13},{10,... | collective-permute-start | bytes 1376264 | tf_op jit(solution)/shard_map/ppermute | solution.py:134
  70.4 0.1 collective-permute-start.22
  70.4 1.1 %shard_map.82 = (f32[128,1792]{1,0:T(8,128)S(1)}, bf16[128,1792]{1,0:T(8,128)(2,1)S(1)}) custom-call(bf16[256,512]{1,0:T(8,128)(2,1)S(1)} %get-tuple-element.76.hidden_ref, bf16[256,512]{1,0:T(8,128)(2,1)S(1)} %collective-permute-done.28.other_ref, f32[256,128]{1,0:T(8,128)S(1)} %get-tuple-element.77.scale_ref, ...), custom_call_target="tpu_custom_call" | custom-call | flops 939524096 | bytes 4325376 | tf_op jit(solution)/shard_map/pallas_call | solution.py:104
  71.6 0.8 collective-permute-start.33
  72.3 5.1 %collective-permute-done.29 = bf16[128,1792]{1,0:T(8,128)(2,1)S(1)} collective-permute-done((bf16[128,1792]{1,0:T(8,128)(2,1)S(1)}, bf16[128,1792]{1,0:T(8,128)(2,1)S(1)}, u32[]{:S(2)}, u32[]{:S(2)}) %collective-permute-start.29) | collective-permute-done | bytes 458784 | tf_op jit(solution)/shard_map/ppermute | solution.py:134
  77.5 0.1 convert_add_fusion.1
  77.6 1.1 %collective-permute-start.31 = (bf16[64,1792]{1,0:T(8,128)(2,1)S(1)}, bf16[64,1792]{1,0:T(8,128)(2,1)S(1)}, u32[]{:S(2)}, u32[]{:S(2)}) collective-permute-start(bf16[64,1792]{1,0:T(8,128)(2,1)S(1)} %bitcast.40), channel_id=1, source_target_pairs={{0,4},{1,3},{2,6},{3,1},{4,0},{5,7},{6,2},{7,5},{8,12},{9,11},{10,... | collective-permute-start | bytes 688136 | tf_op jit(solution)/shard_map/ppermute | solution.py:138
  78.7 0.1 collective-permute-done.22
  78.8 0.1 fusion.4
  78.9 0.1 collective-permute-start.30
  78.9 5.9 %collective-permute-done.33 = bf16[128,1792]{1,0:T(8,128)(2,1)S(1)} collective-permute-done((bf16[128,1792]{1,0:T(8,128)(2,1)S(1)}, bf16[128,1792]{1,0:T(8,128)(2,1)S(1)}, u32[]{:S(2)}, u32[]{:S(2)}) %collective-permute-start.33) | collective-permute-done | bytes 458784 | tf_op jit(solution)/shard_map/ppermute | solution.py:134
  84.8 0.1 convert_add_fusion
  85.0 1.1 %collective-permute-start.34 = (bf16[64,1792]{1,0:T(8,128)(2,1)S(1)}, bf16[64,1792]{1,0:T(8,128)(2,1)S(1)}, u32[]{:S(2)}, u32[]{:S(2)}) collective-permute-start(bf16[64,1792]{1,0:T(8,128)(2,1)S(1)} %bitcast.41), channel_id=1, source_target_pairs={{0,4},{1,3},{2,6},{3,1},{4,0},{5,7},{6,2},{7,5},{8,12},{9,11},{10,... | collective-permute-start | bytes 688136 | tf_op jit(solution)/shard_map/ppermute | solution.py:138
  86.1 1.5 %collective-permute-done.30 = bf16[64,1792]{1,0:T(8,128)(2,1)S(1)} collective-permute-done((bf16[64,1792]{1,0:T(8,128)(2,1)S(1)}, bf16[64,1792]{1,0:T(8,128)(2,1)S(1)}, u32[]{:S(2)}, u32[]{:S(2)}) %collective-permute-start.30) | collective-permute-done | bytes 229408 | tf_op jit(solution)/shard_map/ppermute | solution.py:141
  87.6 0.1 fusion.2
  87.7 0.1 collective-permute-start.32
  87.8 3.3 %collective-permute-done.34 = bf16[64,1792]{1,0:T(8,128)(2,1)S(1)} collective-permute-done((bf16[64,1792]{1,0:T(8,128)(2,1)S(1)}, bf16[64,1792]{1,0:T(8,128)(2,1)S(1)}, u32[]{:S(2)}, u32[]{:S(2)}) %collective-permute-start.34) | collective-permute-done | bytes 229408 | tf_op jit(solution)/shard_map/ppermute | solution.py:138
  91.1 4.5 %collective-permute-done.32 = bf16[64,1792]{1,0:T(8,128)(2,1)S(1)} collective-permute-done((bf16[64,1792]{1,0:T(8,128)(2,1)S(1)}, bf16[64,1792]{1,0:T(8,128)(2,1)S(1)}, u32[]{:S(2)}, u32[]{:S(2)}) %collective-permute-start.32) | collective-permute-done | bytes 229408 | tf_op jit(solution)/shard_map/ppermute | solution.py:141
  95.6 0.1 fusion
  95.7 0.7 copy-done.1
  (46 shorter events, 0.6 us)
Async XLA Ops:
  2.4 8.8 %copy-start = (bf16[32,3712]{1,0:T(8,128)(2,1)S(1)}, bf16[32,3712]{1,0:T(8,128)(2,1)}, u32[]{:S(2)}) copy-start(bf16[32,3712]{1,0:T(8,128)(2,1)} %shard_map.73) | copy-start | bytes 712708
  2.4 8.8 %collective-permute-start.1 = (bf16[32,3712]{1,0:T(8,128)(2,1)}, bf16[32,3712]{1,0:T(8,128)(2,1)S(1)}, u32[]{:S(2)}, u32[]{:S(2)}) collective-permute-start(bf16[32,3712]{1,0:T(8,128)(2,1)} %shard_map.73), channel_id=1, source_target_pairs={{0,2},{1,5},{2,0},{3,7},{4,6},{5,1},{6,4},{7,3},{8,10},{9,13},{10,... | collective-permute-start | bytes 712712 | tf_op jit(solution)/shard_map/ppermute | solution.py:134
  5.4 9.4 %collective-permute-start = (bf16[32,3712]{1,0:T(8,128)(2,1)}, bf16[32,3712]{1,0:T(8,128)(2,1)S(1)}, u32[]{:S(2)}, u32[]{:S(2)}) collective-permute-start(bf16[32,3712]{1,0:T(8,128)(2,1)} %shard_map.73), channel_id=1, source_target_pairs={{0,8},{2,10},{4,12},{6,14},{8,16},{10,18},{12,20},{14,22},{16,24},... | collective-permute-start | bytes 712712 | tf_op jit(solution)/shard_map/ppermute | solution.py:141
  11.3 11.8 %collective-permute-start.2 = (bf16[64,3712]{1,0:T(8,128)(2,1)S(1)}, bf16[64,3712]{1,0:T(8,128)(2,1)S(1)}, u32[]{:S(2)}, u32[]{:S(2)}) collective-permute-start(bf16[64,3712]{1,0:T(8,128)(2,1)S(1)} %constant_dynamic-update-slice_fusion.refs_0_), channel_id=1, source_target_pairs={{0,4},{1,3},{2,6},{3,1},{4,0},{5,7},{6,2},{7,5},{8,12},{9,11},{10,... | collective-permute-start | bytes 1425416 | tf_op jit(solution)/shard_map/ppermute | solution.py:138
  14.8 8.3 %collective-permute-start.3 = (bf16[32,3712]{1,0:T(8,128)(2,1)S(1)}, bf16[32,3712]{1,0:T(8,128)(2,1)S(1)}, u32[]{:S(2)}, u32[]{:S(2)}) collective-permute-start(bf16[32,3712]{1,0:T(8,128)(2,1)S(1)} %collective-permute-done), channel_id=1, source_target_pairs={{0,8},{2,10},{4,12},{6,14},{8,16},{10,18},{12,20},{14,22},{16,24},... | collective-permute-start | bytes 712712 | tf_op jit(solution)/shard_map/ppermute | solution.py:141
  14.8 8.3 %collective-permute-start.4 = (bf16[32,3712]{1,0:T(8,128)(2,1)S(1)}, bf16[32,3712]{1,0:T(8,128)(2,1)S(1)}, u32[]{:S(2)}, u32[]{:S(2)}) collective-permute-start(bf16[32,3712]{1,0:T(8,128)(2,1)S(1)} %collective-permute-done), channel_id=1, source_target_pairs={{0,2},{1,5},{2,0},{3,7},{4,6},{5,1},{6,4},{7,3},{8,10},{9,13},{10,... | collective-permute-start | bytes 712712 | tf_op jit(solution)/shard_map/ppermute | solution.py:134
  16.3 10.1 %collective-permute-start.7 = (bf16[64,3712]{1,0:T(8,128)(2,1)S(1)}, bf16[64,3712]{1,0:T(8,128)(2,1)S(1)}, u32[]{:S(2)}, u32[]{:S(2)}) collective-permute-start(bf16[64,3712]{1,0:T(8,128)(2,1)S(1)} %constant_dynamic-update-slice_fusion.refs_0_), channel_id=1, source_target_pairs={{0,1},{1,0},{2,3},{3,2},{4,5},{5,4},{6,7},{7,6},{8,9},{9,8},{10,11... | collective-permute-start | bytes 1425416 | tf_op jit(solution)/shard_map/ppermute | solution.py:144
  23.1 3.3 %collective-permute-start.8 = (bf16[64,3712]{1,0:T(8,128)(2,1)S(1)}, bf16[64,3712]{1,0:T(8,128)(2,1)S(1)}, u32[]{:S(2)}, u32[]{:S(2)}) collective-permute-start(bf16[64,3712]{1,0:T(8,128)(2,1)S(1)} %collective-permute-done.2.refs_1_), channel_id=1, source_target_pairs={{0,1},{1,0},{2,3},{3,2},{4,5},{5,4},{6,7},{7,6},{8,9},{9,8},{10,11... | collective-permute-start | bytes 1425416 | tf_op jit(solution)/shard_map/ppermute | solution.py:144
  23.2 11.3 %collective-permute-start.5 = (bf16[64,3712]{1,0:T(8,128)(2,1)S(1)}, bf16[64,3712]{1,0:T(8,128)(2,1)S(1)}, u32[]{:S(2)}, u32[]{:S(2)}) collective-permute-start(bf16[64,3712]{1,0:T(8,128)(2,1)S(1)} %constant_dynamic-update-slice_fusion.2.refs_0_), channel_id=1, source_target_pairs={{0,4},{1,3},{2,6},{3,1},{4,0},{5,7},{6,2},{7,5},{8,12},{9,11},{10,... | collective-permute-start | bytes 1425416 | tf_op jit(solution)/shard_map/ppermute | solution.py:138
  24.3 9.6 %collective-permute-start.6 = (bf16[32,3712]{1,0:T(8,128)(2,1)S(1)}, bf16[32,3712]{1,0:T(8,128)(2,1)S(1)}, u32[]{:S(2)}, u32[]{:S(2)}) collective-permute-start(bf16[32,3712]{1,0:T(8,128)(2,1)S(1)} %collective-permute-done.3), channel_id=1, source_target_pairs={{0,8},{2,10},{4,12},{6,14},{8,16},{10,18},{12,20},{14,22},{16,24},... | collective-permute-start | bytes 712712 | tf_op jit(solution)/shard_map/ppermute | solution.py:141
  25.7 8.8 %collective-permute-start.9 = (bf16[32,3712]{1,0:T(8,128)(2,1)S(1)}, bf16[32,3712]{1,0:T(8,128)(2,1)S(1)}, u32[]{:S(2)}, u32[]{:S(2)}) collective-permute-start(bf16[32,3712]{1,0:T(8,128)(2,1)S(1)} %collective-permute-done.3), channel_id=1, source_target_pairs={{0,2},{1,5},{2,0},{3,7},{4,6},{5,1},{6,4},{7,3},{8,10},{9,13},{10,... | collective-permute-start | bytes 712712 | tf_op jit(solution)/shard_map/ppermute | solution.py:134
  26.4 11.4 %collective-permute-start.10 = (bf16[64,3712]{1,0:T(8,128)(2,1)S(1)}, bf16[64,3712]{1,0:T(8,128)(2,1)S(1)}, u32[]{:S(2)}, u32[]{:S(2)}) collective-permute-start(bf16[64,3712]{1,0:T(8,128)(2,1)S(1)} %constant_dynamic-update-slice_fusion.2.refs_0_), channel_id=1, source_target_pairs={{0,1},{1,0},{2,3},{3,2},{4,5},{5,4},{6,7},{7,6},{8,9},{9,8},{10,11... | collective-permute-start | bytes 1425416 | tf_op jit(solution)/shard_map/ppermute | solution.py:144
  34.5 3.3 %collective-permute-start.11 = (bf16[64,3712]{1,0:T(8,128)(2,1)S(1)}, bf16[64,3712]{1,0:T(8,128)(2,1)S(1)}, u32[]{:S(2)}, u32[]{:S(2)}) collective-permute-start(bf16[64,3712]{1,0:T(8,128)(2,1)S(1)} %collective-permute-done.5.refs_1_), channel_id=1, source_target_pairs={{0,1},{1,0},{2,3},{3,2},{4,5},{5,4},{6,7},{7,6},{8,9},{9,8},{10,11... | collective-permute-start | bytes 1425416 | tf_op jit(solution)/shard_map/ppermute | solution.py:144
  34.8 12.5 %collective-permute-start.15 = (bf16[512,1792]{1,0:T(8,128)(2,1)S(1)}, bf16[512,1792]{1,0:T(8,128)(2,1)S(1)}, u32[]{:S(2)}, u32[]{:S(2)}) collective-permute-start(bf16[512,1792]{1,0:T(8,128)(2,1)S(1)} %get-tuple-element.61), channel_id=1, source_target_pairs={{0,1},{1,0},{2,3},{3,2},{4,5},{5,4},{6,7},{7,6},{8,9},{9,8},{10,11... | collective-permute-start | bytes 5505032 | tf_op jit(solution)/shard_map/ppermute | solution.py:144
  35.1 11.2 %collective-permute-start.12 = (bf16[64,3712]{1,0:T(8,128)(2,1)S(1)}, bf16[64,3712]{1,0:T(8,128)(2,1)S(1)}, u32[]{:S(2)}, u32[]{:S(2)}) collective-permute-start(bf16[64,3712]{1,0:T(8,128)(2,1)S(1)} %constant_dynamic-update-slice_fusion.4.refs_0_), channel_id=1, source_target_pairs={{0,4},{1,3},{2,6},{3,1},{4,0},{5,7},{6,2},{7,5},{8,12},{9,11},{10,... | collective-permute-start | bytes 1425416 | tf_op jit(solution)/shard_map/ppermute | solution.py:138
  36.1 10.2 %collective-permute-start.13 = (bf16[32,3712]{1,0:T(8,128)(2,1)S(1)}, bf16[32,3712]{1,0:T(8,128)(2,1)S(1)}, u32[]{:S(2)}, u32[]{:S(2)}) collective-permute-start(bf16[32,3712]{1,0:T(8,128)(2,1)S(1)} %collective-permute-done.6), channel_id=1, source_target_pairs={{0,2},{1,5},{2,0},{3,7},{4,6},{5,1},{6,4},{7,3},{8,10},{9,13},{10,... | collective-permute-start | bytes 712712 | tf_op jit(solution)/shard_map/ppermute | solution.py:134
  37.7 13.3 %collective-permute-start.18 = (bf16[64,3712]{1,0:T(8,128)(2,1)S(1)}, bf16[64,3712]{1,0:T(8,128)(2,1)S(1)}, u32[]{:S(2)}, u32[]{:S(2)}) collective-permute-start(bf16[64,3712]{1,0:T(8,128)(2,1)S(1)} %constant_dynamic-update-slice_fusion.4.refs_0_), channel_id=1, source_target_pairs={{0,1},{1,0},{2,3},{3,2},{4,5},{5,4},{6,7},{7,6},{8,9},{9,8},{10,11... | collective-permute-start | bytes 1425416 | tf_op jit(solution)/shard_map/ppermute | solution.py:144
  46.3 4.8 %collective-permute-start.19 = (bf16[64,3712]{1,0:T(8,128)(2,1)S(1)}, bf16[64,3712]{1,0:T(8,128)(2,1)S(1)}, u32[]{:S(2)}, u32[]{:S(2)}) collective-permute-start(bf16[64,3712]{1,0:T(8,128)(2,1)S(1)} %collective-permute-done.12.refs_1_), channel_id=1, source_target_pairs={{0,1},{1,0},{2,3},{3,2},{4,5},{5,4},{6,7},{7,6},{8,9},{9,8},{10,11... | collective-permute-start | bytes 1425416 | tf_op jit(solution)/shard_map/ppermute | solution.py:144
  46.4 2.2 %collective-permute-start.14 = (bf16[256,512]{1,0:T(8,128)(2,1)S(1)}, bf16[256,512]{1,0:T(8,128)(2,1)S(1)}, u32[]{:S(2)}, u32[]{:S(2)}) collective-permute-start(bf16[256,512]{1,0:T(8,128)(2,1)S(1)} %get-tuple-element.59.hidden_ref), channel_id=1, source_target_pairs={{0,1},{1,0},{2,3},{3,2},{4,5},{5,4},{6,7},{7,6},{8,9},{9,8},{10,11... | collective-permute-start | bytes 786440 | tf_op jit(solution)/shard_map/ppermute | solution.py:144
  46.9 14.7 %collective-permute-start.24 = (bf16[64,3712]{1,0:T(8,128)(2,1)S(1)}, bf16[64,3712]{1,0:T(8,128)(2,1)S(1)}, u32[]{:S(2)}, u32[]{:S(2)}) collective-permute-start(bf16[64,3712]{1,0:T(8,128)(2,1)S(1)} %collective-permute-done.12.refs_1_), channel_id=1, source_target_pairs={{0,8},{2,10},{4,12},{6,14},{8,16},{10,18},{12,20},{14,22},{16,24},... | collective-permute-start | bytes 1425416 | tf_op jit(solution)/shard_map/ppermute | solution.py:141
  49.7 11.8 %collective-permute-start.16 = (bf16[128,1792]{1,0:T(8,128)(2,1)S(1)}, bf16[128,1792]{1,0:T(8,128)(2,1)S(1)}, u32[]{:S(2)}, u32[]{:S(2)}) collective-permute-start(bf16[128,1792]{1,0:T(8,128)(2,1)S(1)} %get-tuple-element.63), channel_id=1, source_target_pairs={{0,2},{1,5},{2,0},{3,7},{4,6},{5,1},{6,4},{7,3},{8,10},{9,13},{10,... | collective-permute-start | bytes 1376264 | tf_op jit(solution)/shard_map/ppermute | solution.py:134
  53.2 1.6 %collective-permute-start.20 = (bf16[256,512]{1,0:T(8,128)(2,1)S(1)}, bf16[256,512]{1,0:T(8,128)(2,1)S(1)}, u32[]{:S(2)}, u32[]{:S(2)}) collective-permute-start(bf16[256,512]{1,0:T(8,128)(2,1)S(1)} %get-tuple-element.66.hidden_ref), channel_id=1, source_target_pairs={{0,1},{1,0},{2,3},{3,2},{4,5},{5,4},{6,7},{7,6},{8,9},{9,8},{10,11... | collective-permute-start | bytes 786440 | tf_op jit(solution)/shard_map/ppermute | solution.py:144
  53.2 17.2 %collective-permute-start.28 = (bf16[256,512]{1,0:T(8,128)(2,1)S(1)}, bf16[256,512]{1,0:T(8,128)(2,1)S(1)}, u32[]{:S(2)}, u32[]{:S(2)}) collective-permute-start(bf16[256,512]{1,0:T(8,128)(2,1)S(1)} %get-tuple-element.76.hidden_ref), channel_id=1, source_target_pairs={{0,1},{1,0},{2,3},{3,2},{4,5},{5,4},{6,7},{7,6},{8,9},{9,8},{10,11... | collective-permute-start | bytes 786440 | tf_op jit(solution)/shard_map/ppermute | solution.py:144
  53.7 9.1 %collective-permute-start.25 = (bf16[64,3712]{1,0:T(8,128)(2,1)S(1)}, bf16[64,3712]{1,0:T(8,128)(2,1)S(1)}, u32[]{:S(2)}, u32[]{:S(2)}) collective-permute-start(bf16[64,3712]{1,0:T(8,128)(2,1)S(1)} %constant_dynamic-update-slice_fusion.6.refs_0_), channel_id=1, source_target_pairs={{0,1},{1,0},{2,3},{3,2},{4,5},{5,4},{6,7},{7,6},{8,9},{9,8},{10,11... | collective-permute-start | bytes 1425416 | tf_op jit(solution)/shard_map/ppermute | solution.py:144
  55.9 9.8 %collective-permute-start.21 = (bf16[128,1792]{1,0:T(8,128)(2,1)S(1)}, bf16[128,1792]{1,0:T(8,128)(2,1)S(1)}, u32[]{:S(2)}, u32[]{:S(2)}) collective-permute-start(bf16[128,1792]{1,0:T(8,128)(2,1)S(1)} %get-tuple-element.69), channel_id=1, source_target_pairs={{0,2},{1,5},{2,0},{3,7},{4,6},{5,1},{6,4},{7,3},{8,10},{9,13},{10,... | collective-permute-start | bytes 1376264 | tf_op jit(solution)/shard_map/ppermute | solution.py:134
  61.6 1.8 %collective-permute-start.26 = (bf16[64,3712]{1,0:T(8,128)(2,1)S(1)}, bf16[64,3712]{1,0:T(8,128)(2,1)S(1)}, u32[]{:S(2)}, u32[]{:S(2)}) collective-permute-start(bf16[64,3712]{1,0:T(8,128)(2,1)S(1)} %collective-permute-done.24.refs_1_), channel_id=1, source_target_pairs={{0,1},{1,0},{2,3},{3,2},{4,5},{5,4},{6,7},{7,6},{8,9},{9,8},{10,11... | collective-permute-start | bytes 1425416 | tf_op jit(solution)/shard_map/ppermute | solution.py:144
  61.7 6.1 %collective-permute-start.17 = (bf16[64,1792]{1,0:T(8,128)(2,1)S(1)}, bf16[64,1792]{1,0:T(8,128)(2,1)S(1)}, u32[]{:S(2)}, u32[]{:S(2)}) collective-permute-start(bf16[64,1792]{1,0:T(8,128)(2,1)S(1)} %bitcast.39), channel_id=1, source_target_pairs={{0,4},{1,3},{2,6},{3,1},{4,0},{5,7},{6,2},{7,5},{8,12},{9,11},{10,... | collective-permute-start | bytes 688136 | tf_op jit(solution)/shard_map/ppermute | solution.py:138
  65.5 2.3 %collective-permute-start.27 = (bf16[256,512]{1,0:T(8,128)(2,1)S(1)}, bf16[256,512]{1,0:T(8,128)(2,1)S(1)}, u32[]{:S(2)}, u32[]{:S(2)}) collective-permute-start(bf16[256,512]{1,0:T(8,128)(2,1)S(1)} %get-tuple-element.72.hidden_ref), channel_id=1, source_target_pairs={{0,1},{1,0},{2,3},{3,2},{4,5},{5,4},{6,7},{7,6},{8,9},{9,8},{10,11... | collective-permute-start | bytes 786440 | tf_op jit(solution)/shard_map/ppermute | solution.py:144
  65.8 12.8 %collective-permute-start.23 = (bf16[64,1792]{1,0:T(8,128)(2,1)S(1)}, bf16[64,1792]{1,0:T(8,128)(2,1)S(1)}, u32[]{:S(2)}, u32[]{:S(2)}) collective-permute-start(bf16[64,1792]{1,0:T(8,128)(2,1)S(1)} %bitcast.38), channel_id=1, source_target_pairs={{0,4},{1,3},{2,6},{3,1},{4,0},{5,7},{6,2},{7,5},{8,12},{9,11},{10,... | collective-permute-start | bytes 688136 | tf_op jit(solution)/shard_map/ppermute | solution.py:138
  68.9 8.5 %collective-permute-start.29 = (bf16[128,1792]{1,0:T(8,128)(2,1)S(1)}, bf16[128,1792]{1,0:T(8,128)(2,1)S(1)}, u32[]{:S(2)}, u32[]{:S(2)}) collective-permute-start(bf16[128,1792]{1,0:T(8,128)(2,1)S(1)} %get-tuple-element.75), channel_id=1, source_target_pairs={{0,2},{1,5},{2,0},{3,7},{4,6},{5,1},{6,4},{7,3},{8,10},{9,13},{10,... | collective-permute-start | bytes 1376264 | tf_op jit(solution)/shard_map/ppermute | solution.py:134
  70.4 8.4 %collective-permute-start.22 = (bf16[64,1792]{1,0:T(8,128)(2,1)S(1)}, bf16[64,1792]{1,0:T(8,128)(2,1)S(1)}, u32[]{:S(2)}, u32[]{:S(2)}) collective-permute-start(bf16[64,1792]{1,0:T(8,128)(2,1)S(1)} %fusion.5), channel_id=1, source_target_pairs={{0,8},{2,10},{4,12},{6,14},{8,16},{10,18},{12,20},{14,22},{16,24},... | collective-permute-start | bytes 688136 | tf_op jit(solution)/shard_map/ppermute | solution.py:141
  71.6 13.3 %collective-permute-start.33 = (bf16[128,1792]{1,0:T(8,128)(2,1)S(1)}, bf16[128,1792]{1,0:T(8,128)(2,1)S(1)}, u32[]{:S(2)}, u32[]{:S(2)}) collective-permute-start(bf16[128,1792]{1,0:T(8,128)(2,1)S(1)} %get-tuple-element.78), channel_id=1, source_target_pairs={{0,2},{1,5},{2,0},{3,7},{4,6},{5,1},{6,4},{7,3},{8,10},{9,13},{10,... | collective-permute-start | bytes 1376264 | tf_op jit(solution)/shard_map/ppermute | solution.py:134
  77.6 8.5 %collective-permute-start.31 = (bf16[64,1792]{1,0:T(8,128)(2,1)S(1)}, bf16[64,1792]{1,0:T(8,128)(2,1)S(1)}, u32[]{:S(2)}, u32[]{:S(2)}) collective-permute-start(bf16[64,1792]{1,0:T(8,128)(2,1)S(1)} %bitcast.40), channel_id=1, source_target_pairs={{0,4},{1,3},{2,6},{3,1},{4,0},{5,7},{6,2},{7,5},{8,12},{9,11},{10,... | collective-permute-start | bytes 688136 | tf_op jit(solution)/shard_map/ppermute | solution.py:138
  78.9 8.7 %collective-permute-start.30 = (bf16[64,1792]{1,0:T(8,128)(2,1)S(1)}, bf16[64,1792]{1,0:T(8,128)(2,1)S(1)}, u32[]{:S(2)}, u32[]{:S(2)}) collective-permute-start(bf16[64,1792]{1,0:T(8,128)(2,1)S(1)} %fusion.4), channel_id=1, source_target_pairs={{0,8},{2,10},{4,12},{6,14},{8,16},{10,18},{12,20},{14,22},{16,24},... | collective-permute-start | bytes 688136 | tf_op jit(solution)/shard_map/ppermute | solution.py:141
  85.0 6.1 %collective-permute-start.34 = (bf16[64,1792]{1,0:T(8,128)(2,1)S(1)}, bf16[64,1792]{1,0:T(8,128)(2,1)S(1)}, u32[]{:S(2)}, u32[]{:S(2)}) collective-permute-start(bf16[64,1792]{1,0:T(8,128)(2,1)S(1)} %bitcast.41), channel_id=1, source_target_pairs={{0,4},{1,3},{2,6},{3,1},{4,0},{5,7},{6,2},{7,5},{8,12},{9,11},{10,... | collective-permute-start | bytes 688136 | tf_op jit(solution)/shard_map/ppermute | solution.py:138
  87.7 7.9 %collective-permute-start.32 = (bf16[64,1792]{1,0:T(8,128)(2,1)S(1)}, bf16[64,1792]{1,0:T(8,128)(2,1)S(1)}, u32[]{:S(2)}, u32[]{:S(2)}) collective-permute-start(bf16[64,1792]{1,0:T(8,128)(2,1)S(1)} %fusion.2), channel_id=1, source_target_pairs={{0,8},{2,10},{4,12},{6,14},{8,16},{10,18},{12,20},{14,22},{16,24},... | collective-permute-start | bytes 688136 | tf_op jit(solution)/shard_map/ppermute | solution.py:141
  95.7 0.7 copy-start.1
